TPU v7x, 32 devices: a whole 2x2x4 slice. The times are simulated.
32 devices in a mesh: grp: 2 (over core), tx: 4 (over y, x), ty: 4 (over z).
Axes of the slice: x: 2, y: 2, z: 4, core: 2. Of those that a mesh axis runs over, the one named last changes fastest.
Arguments:
- endpoints: float32 [2, 5, 16, 32, 512], P('grp', None, None, 'tx', 'ty'), may hold values from -4 to 5, as said below
Outputs:
- adjoints: float32 [2, 5, 16, 32, 512], P('grp', None, None, 'tx', 'ty')
- forward_states: float32 [2, 5, 16, 32, 512], P('grp', None, None, 'tx', 'ty')
Inputs may be any that keep to these rules, and one draw needn't show every extreme that they name: `endpoints`: in entry 0 the density lies in 1 to 2, each velocity component (momentum over density) in -0.5 to 0.5 and the pressure 0.4 (E - |m|^2 / (2 density)) in 0.5 to 1.5; entry 1 is a cotangent within -4 to 4.
All inputs are finite; a program needn't handle non-finite values.
Results may differ from a plain program's by a relative error of at most 0.00002.
Values sent between devices are 32-bit elements; how exact they have to be, the bound alone decides.
No kernel may reach another device: no remote copies, remote signals or barrier semaphores. Data moves between devices by JAX's collectives and lax.ppermute only.
A program may use at most 64 MiB of HBM per device.

v0:
```python
import jax
import jax.numpy as jnp
from jax import lax
from jax.sharding import PartitionSpec as P

gas_gamma = 1.4
time_step = 0.05
viscosity = 0.1
directions = ((1, 2), (2, 3), (3, 1))


def padded_2(shard, sides, width):
    for axis, dim in sides:
        count, length = (lax.axis_size(axis), shard.shape[dim])
        up = [(i, (i + 1) % count) for i in range(count)]
        down = [(j, i) for i, j in up]
        last = lax.slice_in_dim(shard, length - width, length, axis=dim)
        leading = lax.slice_in_dim(shard, 0, width, axis=dim)
        before = lax.ppermute(last, axis, up)
        after = lax.ppermute(leading, axis, down)
        shard = jnp.concatenate([before, shard, after], axis=dim)
    return shard


def shifted(value, axis, steps):
    count = lax.axis_size(axis)
    leading, last = (max(0, -steps), min(count, count - steps))
    return lax.ppermute(value, axis, [(source, source + steps) for source in range(leading, last)])


def euler_flux(fields, component):
    density = fields[0]
    inverse = 1.0 / density
    kinetic = (
        0.5 * inverse * (fields[1] * fields[1] + fields[2] * fields[2] + fields[3] * fields[3])
    )
    pressure = (gas_gamma - 1.0) * (fields[4] - kinetic)
    velocity = fields[component] * inverse
    components = [
        fields[component],
        fields[1] * velocity,
        fields[2] * velocity,
        fields[3] * velocity,
        (fields[4] + pressure) * velocity,
    ]
    components[component] = components[component] + pressure
    return jnp.stack(components)


def window(padded, spatial, offset):
    selector = [slice(None), slice(1, -1), slice(1, -1), slice(1, -1)]
    extent = padded.shape[spatial]
    selector[spatial] = slice(1 + offset, extent - 1 + offset)
    return padded[tuple(selector)]


def interior(padded):
    return padded[:, 1:-1, 1:-1, 1:-1]


def shrink_rate(padded):
    centre = interior(padded)
    tendency = jnp.zeros_like(centre)
    for component, spatial in directions:
        fluxes = euler_flux(padded, component)
        tendency = tendency - 0.5 * (window(fluxes, spatial, 1) - window(fluxes, spatial, -1))
        tendency = tendency + viscosity * (
            window(padded, spatial, 1) + window(padded, spatial, -1) - 2.0 * centre
        )
    return tendency


def shrink_adjoint(fields, padded):
    centre = interior(padded)
    diffusion = jnp.zeros_like(centre)
    weights = []
    for component, spatial in directions:
        weights.append(0.5 * (window(padded, spatial, 1) - window(padded, spatial, -1)))
        diffusion = diffusion + (
            window(padded, spatial, 1) + window(padded, spatial, -1) - 2.0 * centre
        )

    def all_fluxes(values):
        return tuple((euler_flux(values, component) for component, spatial in directions))

    outputs, pullback = jax.vjp(all_fluxes, fields)
    (pulled,) = pullback(tuple(weights))
    return pulled + viscosity * diffusion


def extend(values, margin):
    planar = padded_2(values, (("tx", 2), ("ty", 3)), margin)
    return jnp.concatenate([planar[:, -margin:], planar, planar[:, :margin]], axis=1)


def heun_step(fields):
    padded = extend(fields, 2)
    first_rate = shrink_rate(padded)
    section_state = interior(padded) + time_step * first_rate
    advanced = fields + 0.5 * time_step * (interior(first_rate) + shrink_rate(section_state))
    return (advanced, section_state)


def heun_adjoint(fields, section_state, cotangent):
    padded = extend(cotangent, 2)
    section_cot = 0.5 * time_step * shrink_adjoint(section_state, padded)
    weighted = 0.5 * time_step * interior(padded) + time_step * section_cot
    return cotangent + interior(section_cot) + shrink_adjoint(fields, weighted)


def shards(endpoints):
    leading = lax.axis_index("grp") == 0
    holding = endpoints[0]
    resting = jnp.array([1.0, 0.0, 0.0, 0.0, 2.5], jnp.float32)[
        :, None, None, None
    ] * jnp.ones_like(holding)
    initial = jnp.where(leading, holding, resting)
    midway, first_section = heun_step(initial)
    arrived = shifted(midway, "grp", 1)
    entering = jnp.where(leading, midway, arrived)
    ending, second_section = heun_step(entering)
    middle_cot = heun_adjoint(entering, second_section, holding)
    returned = shifted(middle_cot, "grp", -1)
    start_cot = heun_adjoint(initial, first_section, returned)
    adjoints = jnp.where(leading, start_cot, middle_cot)[None]
    states = jnp.where(leading, midway, ending)[None]
    return (adjoints, states)


def solution(mesh):
    placed = (P("grp", None, None, "tx", "ty"),)
    return jax.shard_map(
        shards,
        mesh=mesh,
        in_specs=placed,
        out_specs=(P("grp", None, None, "tx", "ty"), P("grp", None, None, "tx", "ty")),
        check_vma=False,
    )
```

profile of v0, /device:TPU:0, one launch (start us, length us, event | category | flops | bytes accessed | tf_op | source)
XLA Modules:
  0.0 137.3 jit_solution(10213494367665371617)
XLA Ops:
  1.7 3.0 %collective-permute-start.4 = (f32[5,16,2,128]{3,1,2,0:T(8,128)S(1)}, f32[5,16,2,128]{3,1,2,0:T(8,128)S(1)}, u32[]{:S(2)}, u32[]{:S(2)}) collective-permute-start(f32[5,16,2,128]{3,1,2,0:T(8,128)S(1)} %get-tuple-element.356), channel_id=1, source_target_pairs={{0,4},{4,8},{8,12},{12,0},{1,5},{5,9},{9,13},{13,1},{2,6},{6,10},{... | collective-permute-start | bytes 245768 | tf_op jit(solution)/shard_map/ppermute | solution.py:19
  7.9 1.9 %collective-permute-start.1 = (f32[5,16,2,128]{3,1,2,0:T(8,128)S(1)}, f32[5,16,2,128]{3,1,2,0:T(8,128)S(1)}, u32[]{:S(2)}, u32[]{:S(2)}) collective-permute-start(f32[5,16,2,128]{3,1,2,0:T(8,128)S(1)} %get-tuple-element.359), channel_id=1, source_target_pairs={{4,0},{8,4},{12,8},{0,12},{5,1},{9,5},{13,9},{1,13},{6,2},{10,6},{... | collective-permute-start | bytes 245768 | tf_op jit(solution)/shard_map/ppermute | solution.py:20
  11.2 3.7 %collective-permute-start.7 = (f32[5,16,12,2]{1,3,2,0:T(2,128)S(1)}, f32[5,16,12,2]{1,3,2,0:T(2,128)S(1)}, u32[]{:S(2)}, u32[]{:S(2)}) collective-permute-start(f32[5,16,12,2]{1,3,2,0:T(2,128)S(1)} %copy.86), channel_id=1, source_target_pairs={{1,0},{2,1},{3,2},{0,3},{5,4},{6,5},{7,6},{4,7},{9,8},{10,9},{11,1... | collective-permute-start | bytes 23048 | tf_op jit(solution)/shard_map/ppermute | solution.py:20
  15.8 5.2 %collective-permute-done.6 = f32[5,16,12,2]{1,3,2,0:T(2,128)S(1)} collective-permute-done((f32[5,16,12,2]{1,3,2,0:T(2,128)S(1)}, f32[5,16,12,2]{1,3,2,0:T(2,128)S(1)}, u32[]{:S(2)}, u32[]{:S(2)}) %collective-permute-start.6) | collective-permute-done | bytes 7712 | tf_op jit(solution)/shard_map/ppermute | solution.py:19
  23.6 5.7 %multiply_add_fusion.3 = (f32[5,18,10,130]{3,1,2,0:T(8,128)S(1)}, f32[5,18,10,130]{3,1,2,0:T(8,128)S(1)}) fusion(f32[5,20,12,132]{3,1,2,0:T(8,128)S(1)} %pad_maximum_fusion, f32[5,16,12,2]{3,1,2,0:T(8,128)S(1)} %copy.65, f32[5,16,2,128]{3,1,2,0:T(8,128)S(1)} %collective-permute-done.5, f32[5,16,8,128]{3,1,2,0:T(8,128)S(1)} %broadcast_select_fusion, ...), kind=kLoop, calls=%fused_computation.140 | loop fusion | flops 3978000 | bytes 6717600 | tf_op jit(solution)/shard_map/add | solution.py:99
  33.4 2.2 %collective-permute-start.8 = (f32[5,16,8,128]{3,2,1,0:T(8,128)S(1)}, f32[5,16,8,128]{3,2,1,0:T(8,128)}, u32[]{:S(2)}, u32[]{:S(2)}) collective-permute-start(f32[5,16,8,128]{3,2,1,0:T(8,128)S(1)} %copy.66), channel_id=1, source_target_pairs={{0,16},{1,17},{2,18},{3,19},{4,20},{5,21},{6,22},{7,23},{8,24},{9,... | collective-permute-start | bytes 983048 | tf_op jit(solution)/shard_map/ppermute | solution.py:28
  36.7 3.9 %collective-permute-start.3 = (f32[5,16,12,2]{1,3,2,0:T(2,128)S(1)}, f32[5,16,12,2]{1,3,2,0:T(2,128)S(1)}, u32[]{:S(2)}, u32[]{:S(2)}) collective-permute-start(f32[5,16,12,2]{1,3,2,0:T(2,128)S(1)} %copy.84), channel_id=1, source_target_pairs={{1,0},{2,1},{3,2},{0,3},{5,4},{6,5},{7,6},{4,7},{9,8},{10,9},{11,1... | collective-permute-start | bytes 23048 | tf_op jit(solution)/shard_map/ppermute | solution.py:20
  40.6 1.7 %collective-permute-done.2 = f32[5,16,12,2]{1,3,2,0:T(2,128)S(1)} collective-permute-done((f32[5,16,12,2]{1,3,2,0:T(2,128)S(1)}, f32[5,16,12,2]{1,3,2,0:T(2,128)S(1)}, u32[]{:S(2)}, u32[]{:S(2)}) %collective-permute-start.2) | collective-permute-done | bytes 7712 | tf_op jit(solution)/shard_map/ppermute | solution.py:19
  45.9 2.6 %collective-permute-start.9 = (f32[5,16,2,128]{3,1,2,0:T(8,128)S(1)}, f32[5,16,2,128]{3,1,2,0:T(8,128)S(1)}, u32[]{:S(2)}, u32[]{:S(2)}) collective-permute-start(f32[5,16,2,128]{3,1,2,0:T(8,128)S(1)} %get-tuple-element.354), channel_id=1, source_target_pairs={{0,4},{4,8},{8,12},{12,0},{1,5},{5,9},{9,13},{13,1},{2,6},{6,10},{... | collective-permute-start | bytes 245768 | tf_op jit(solution)/shard_map/ppermute | solution.py:19
  48.9 2.5 %subtract_multiply_fusion.4 = (f32[5,18,10,130]{3,1,2,0:T(8,128)}, f32[5,18,10,130]{3,1,2,0:T(8,128)}) fusion(f32[5,20,12,132]{3,1,2,0:T(8,128)S(1)} %pad_maximum_fusion.2), kind=kLoop, calls=%fused_computation.138 | loop fusion | flops 468000 | bytes 2808000 | tf_op jit(solution)/shard_map/mul | solution.py:78
  54.1 2.1 %copy.87 = f32[5,16,12,2]{1,3,2,0:T(2,128)} copy(f32[5,16,12,2]{3,1,2,0:T(8,128)} %get-tuple-element.280) | data formatting | bytes 15360
  56.1 2.1 %copy.88 = f32[5,16,12,2]{1,3,2,0:T(2,128)} copy(f32[5,16,12,2]{3,1,2,0:T(8,128)} %get-tuple-element.281) | data formatting | bytes 15360
  58.2 3.9 %collective-permute-start.12 = (f32[5,16,12,2]{1,3,2,0:T(2,128)}, f32[5,16,12,2]{1,3,2,0:T(2,128)}, u32[]{:S(2)}, u32[]{:S(2)}) collective-permute-start(f32[5,16,12,2]{1,3,2,0:T(2,128)} %copy.88), channel_id=1, source_target_pairs={{1,0},{2,1},{3,2},{0,3},{5,4},{6,5},{7,6},{4,7},{9,8},{10,9},{11,1... | collective-permute-start | bytes 23048 | tf_op jit(solution)/shard_map/ppermute | solution.py:20
  62.1 3.4 %subtract_multiply_fusion.5 = f32[5,18,10,130]{3,1,2,0:T(8,128)} fusion(f32[5,2,12,132]{3,1,2,0:T(2,128)} %copy-done.36, f32[5,16,12,2]{3,1,2,0:T(8,128)S(1)} %copy.61, f32[5,16,2,128]{3,1,2,0:T(8,128)S(1)} %copy-done.32, f32[5,16,8,128]{3,1,2,0:T(8,128)S(1)} %bitcast.17, f32[5,16,2,128]{3,1,2,0:T(8,128)S(1)} %collective-permute-done, ...), kind=kLoop, calls=%fused_computation.141 | loop fusion | flops 1404000 | bytes 1101600 | tf_op jit(solution)/shard_map/mul | solution.py:78
  65.5 1.7 %unstack.297 = f32[1,18,10,130]{3,1,2,0:T(8,128)} slice(f32[5,18,10,130]{3,1,2,0:T(8,128)} %get-tuple-element.200), slice={[0:1], [0:18], [0:10], [0:130]} | slice | bytes 187200 | tf_op jit(solution)/shard_map/transpose(jvp())/unstack | solution.py:47
  73.9 6.5 %multiply_add_fusion.2 = (f32[5,18,10,130]{3,1,2,0:T(8,128)S(1)}, f32[5,18,10,130]{3,1,2,0:T(8,128)}) fusion(f32[5,20,12,132]{3,1,2,0:T(8,128)S(1)} %pad_maximum_fusion.1, f32[5,16,12,2]{3,1,2,0:T(8,128)S(1)} %copy-done.11, f32[5,16,2,128]{3,1,2,0:T(8,128)S(1)} %copy-done.43, f32[5,16,8,128]{3,1,2,0:T(8,128)S(1)} %copy_select_fusion, ...), kind=kLoop, calls=%fused_computation.139 | loop fusion | flops 3978000 | bytes 6717600 | tf_op jit(solution)/shard_map/add | solution.py:99
  89.2 4.6 %multiply_add_fusion.1 = (f32[5,18,10,130]{3,1,2,0:T(8,128)S(1)}, f32[5,18,10,130]{3,1,2,0:T(8,128)S(1)}) fusion(f32[5,20,12,132]{3,1,2,0:T(8,128)S(1)} %copy-done.1, f32[5,16,12,2]{3,1,2,0:T(8,128)S(1)} %copy-done.7, f32[5,16,2,128]{3,1,2,0:T(8,128)S(1)} %copy-done.33, f32[5,16,8,128]{3,1,2,0:T(8,128)S(1)} %bitcast.18, ...), kind=kLoop, calls=%fused_computation.136 | loop fusion | flops 7605000 | bytes 6998400 | tf_op jit(solution)/shard_map/add | solution.py:107
  97.6 2.2 %collective-permute-done.13 = f32[5,16,8,128]{3,2,1,0:T(8,128)S(1)} collective-permute-done((f32[5,16,8,128]{3,2,1,0:T(8,128)S(1)}, f32[5,16,8,128]{3,2,1,0:T(8,128)S(1)}, u32[]{:S(2)}, u32[]{:S(2)}) %collective-permute-start.13) | collective-permute-done | bytes 327712 | tf_op jit(solution)/shard_map/ppermute | solution.py:28
  102.9 3.3 %collective-permute-done.14 = f32[5,16,2,128]{3,1,2,0:T(8,128)S(1)} collective-permute-done((f32[5,16,2,128]{3,1,2,0:T(8,128)S(1)}, f32[5,16,2,128]{3,1,2,0:T(8,128)S(1)}, u32[]{:S(2)}, u32[]{:S(2)}) %collective-permute-start.14) | collective-permute-done | bytes 81952 | tf_op jit(solution)/shard_map/ppermute | solution.py:19
  108.2 2.1 %copy.76 = f32[5,16,12,2]{1,3,2,0:T(2,128)} copy(f32[5,16,12,2]{3,1,2,0:T(8,128)} %get-tuple-element.278) | data formatting | bytes 15360 | tf_op jit(solution)/shard_map/slice | solution.py:17
  110.2 2.1 %copy.77 = f32[5,16,12,2]{1,3,2,0:T(2,128)} copy(f32[5,16,12,2]{3,1,2,0:T(8,128)} %get-tuple-element.279) | data formatting | bytes 15360 | tf_op jit(solution)/shard_map/slice | solution.py:18
  112.3 2.6 %collective-permute-start.17 = (f32[5,16,12,2]{1,3,2,0:T(2,128)}, f32[5,16,12,2]{1,3,2,0:T(2,128)}, u32[]{:S(2)}, u32[]{:S(2)}) collective-permute-start(f32[5,16,12,2]{1,3,2,0:T(2,128)} %copy.77), channel_id=1, source_target_pairs={{1,0},{2,1},{3,2},{0,3},{5,4},{6,5},{7,6},{4,7},{9,8},{10,9},{11,1... | collective-permute-start | bytes 23048 | tf_op jit(solution)/shard_map/ppermute | solution.py:20
  114.9 4.0 %fusion.107 = f32[1,5,16,8,128]{4,2,3,1,0:T(8,128)S(1)} fusion(f32[5,16,8,128]{3,1,2,0:T(8,128)S(1)} %copy-done.22, f32[5,18,10,130]{3,1,2,0:T(8,128)S(1)} %get-tuple-element.96, f32[5,18,10,130]{3,1,2,0:T(8,128)} %copy-done.47, f32[5,18,10,130]{3,1,2,0:T(8,128)} %copy-done.48, f32[5,18,10,130]{3,1,2,0:T(8,128)} %copy-done.46, ...), kind=kLoop, calls=%fused_computation.207 | loop fusion | flops 2211840 | bytes 5570561 | tf_op jit(solution)/shard_map/broadcast_in_dim | solution.py:126
  130.3 3.8 %multiply_add_fusion = (f32[5,18,10,130]{3,1,2,0:T(8,128)S(1)}, f32[5,18,10,130]{3,1,2,0:T(8,128)S(1)}) fusion(f32[5,20,12,132]{3,1,2,0:T(8,128)S(1)} %pad_maximum_fusion.3, f32[5,16,12,2]{3,1,2,0:T(8,128)S(1)} %copy.79, f32[5,16,12,128]{3,1,2,0:T(8,128)S(1)} %copy-done.3, f32[5,16,12,2]{3,1,2,0:T(8,128)S(1)} %copy.78, ...), kind=kLoop, calls=%fused_computation.132 | loop fusion | flops 7137000 | bytes 6998400 | tf_op jit(solution)/shard_map/add | solution.py:107
  (225 shorter events, 59.4 us)
Async XLA Ops:
  1.7 8.0 %collective-permute-start.4 = (f32[5,16,2,128]{3,1,2,0:T(8,128)S(1)}, f32[5,16,2,128]{3,1,2,0:T(8,128)S(1)}, u32[]{:S(2)}, u32[]{:S(2)}) collective-permute-start(f32[5,16,2,128]{3,1,2,0:T(8,128)S(1)} %get-tuple-element.356), channel_id=1, source_target_pairs={{0,4},{4,8},{8,12},{12,0},{1,5},{5,9},{9,13},{13,1},{2,6},{6,10},{... | collective-permute-start | bytes 245768 | tf_op jit(solution)/shard_map/ppermute | solution.py:19
  4.7 5.4 %collective-permute-start.5 = (f32[5,16,2,128]{3,1,2,0:T(8,128)S(1)}, f32[5,16,2,128]{3,1,2,0:T(8,128)S(1)}, u32[]{:S(2)}, u32[]{:S(2)}) collective-permute-start(f32[5,16,2,128]{3,1,2,0:T(8,128)S(1)} %get-tuple-element.357), channel_id=1, source_target_pairs={{4,0},{8,4},{12,8},{0,12},{5,1},{9,5},{13,9},{1,13},{6,2},{10,6},{... | collective-permute-start | bytes 245768 | tf_op jit(solution)/shard_map/ppermute | solution.py:20
  6.8 8.1 %collective-permute-start = (f32[5,16,2,128]{3,1,2,0:T(8,128)S(1)}, f32[5,16,2,128]{3,1,2,0:T(8,128)S(1)}, u32[]{:S(2)}, u32[]{:S(2)}) collective-permute-start(f32[5,16,2,128]{3,1,2,0:T(8,128)S(1)} %get-tuple-element.358), channel_id=1, source_target_pairs={{0,4},{4,8},{8,12},{12,0},{1,5},{5,9},{9,13},{13,1},{2,6},{6,10},{... | collective-permute-start | bytes 245768 | tf_op jit(solution)/shard_map/ppermute | solution.py:19
  7.9 7.1 %collective-permute-start.1 = (f32[5,16,2,128]{3,1,2,0:T(8,128)S(1)}, f32[5,16,2,128]{3,1,2,0:T(8,128)S(1)}, u32[]{:S(2)}, u32[]{:S(2)}) collective-permute-start(f32[5,16,2,128]{3,1,2,0:T(8,128)S(1)} %get-tuple-element.359), channel_id=1, source_target_pairs={{4,0},{8,4},{12,8},{0,12},{5,1},{9,5},{13,9},{1,13},{6,2},{10,6},{... | collective-permute-start | bytes 245768 | tf_op jit(solution)/shard_map/ppermute | solution.py:20
  11.2 10.2 %collective-permute-start.7 = (f32[5,16,12,2]{1,3,2,0:T(2,128)S(1)}, f32[5,16,12,2]{1,3,2,0:T(2,128)S(1)}, u32[]{:S(2)}, u32[]{:S(2)}) collective-permute-start(f32[5,16,12,2]{1,3,2,0:T(2,128)S(1)} %copy.86), channel_id=1, source_target_pairs={{1,0},{2,1},{3,2},{0,3},{5,4},{6,5},{7,6},{4,7},{9,8},{10,9},{11,1... | collective-permute-start | bytes 23048 | tf_op jit(solution)/shard_map/ppermute | solution.py:20
  15.0 6.0 %collective-permute-start.6 = (f32[5,16,12,2]{1,3,2,0:T(2,128)S(1)}, f32[5,16,12,2]{1,3,2,0:T(2,128)S(1)}, u32[]{:S(2)}, u32[]{:S(2)}) collective-permute-start(f32[5,16,12,2]{1,3,2,0:T(2,128)S(1)} %copy.85), channel_id=1, source_target_pairs={{0,1},{1,2},{2,3},{3,0},{4,5},{5,6},{6,7},{7,4},{8,9},{9,10},{10,1... | collective-permute-start | bytes 23048 | tf_op jit(solution)/shard_map/ppermute | solution.py:19
  15.0 28.7 %copy-start.31 = (f32[5,16,2,128]{3,1,2,0:T(8,128)}, f32[5,16,2,128]{3,1,2,0:T(8,128)S(1)}, u32[]{:S(2)}) copy-start(f32[5,16,2,128]{3,1,2,0:T(8,128)S(1)} %collective-permute-done.1) | copy-start | bytes 245764
  33.4 10.9 %collective-permute-start.8 = (f32[5,16,8,128]{3,2,1,0:T(8,128)S(1)}, f32[5,16,8,128]{3,2,1,0:T(8,128)}, u32[]{:S(2)}, u32[]{:S(2)}) collective-permute-start(f32[5,16,8,128]{3,2,1,0:T(8,128)S(1)} %copy.66), channel_id=1, source_target_pairs={{0,16},{1,17},{2,18},{3,19},{4,20},{5,21},{6,22},{7,23},{8,24},{9,... | collective-permute-start | bytes 983048 | tf_op jit(solution)/shard_map/ppermute | solution.py:28
  36.2 6.1 %collective-permute-start.2 = (f32[5,16,12,2]{1,3,2,0:T(2,128)S(1)}, f32[5,16,12,2]{1,3,2,0:T(2,128)S(1)}, u32[]{:S(2)}, u32[]{:S(2)}) collective-permute-start(f32[5,16,12,2]{1,3,2,0:T(2,128)S(1)} %copy.83), channel_id=1, source_target_pairs={{0,1},{1,2},{2,3},{3,0},{4,5},{5,6},{6,7},{7,4},{8,9},{9,10},{10,1... | collective-permute-start | bytes 23048 | tf_op jit(solution)/shard_map/ppermute | solution.py:19
  36.7 6.0 %collective-permute-start.3 = (f32[5,16,12,2]{1,3,2,0:T(2,128)S(1)}, f32[5,16,12,2]{1,3,2,0:T(2,128)S(1)}, u32[]{:S(2)}, u32[]{:S(2)}) collective-permute-start(f32[5,16,12,2]{1,3,2,0:T(2,128)S(1)} %copy.84), channel_id=1, source_target_pairs={{1,0},{2,1},{3,2},{0,3},{5,4},{6,5},{7,6},{4,7},{9,8},{10,9},{11,1... | collective-permute-start | bytes 23048 | tf_op jit(solution)/shard_map/ppermute | solution.py:20
  42.7 19.4 %copy-start.4 = (f32[5,16,12,2]{3,1,2,0:T(8,128)}, f32[5,16,12,2]{3,1,2,0:T(8,128)S(1)}, u32[]{:S(2)}) copy-start(f32[5,16,12,2]{3,1,2,0:T(8,128)S(1)} %copy.60) | copy-start | bytes 23044
  43.2 18.9 %copy-start.6 = (f32[5,16,12,2]{3,1,2,0:T(8,128)}, f32[5,16,12,2]{3,1,2,0:T(8,128)S(1)}, u32[]{:S(2)}) copy-start(f32[5,16,12,2]{3,1,2,0:T(8,128)S(1)} %copy.61) | copy-start | bytes 23044
  43.6 18.5 %copy-start.34 = (f32[5,2,12,132]{3,1,2,0:T(2,128)}, f32[5,2,12,132]{3,1,2,0:T(2,128)S(1)}, u32[]{:S(2)}) copy-start(f32[5,2,12,132]{3,1,2,0:T(2,128)S(1)} %get-tuple-element.234) | copy-start | bytes 190084
  45.9 5.5 %collective-permute-start.9 = (f32[5,16,2,128]{3,1,2,0:T(8,128)S(1)}, f32[5,16,2,128]{3,1,2,0:T(8,128)S(1)}, u32[]{:S(2)}, u32[]{:S(2)}) collective-permute-start(f32[5,16,2,128]{3,1,2,0:T(8,128)S(1)} %get-tuple-element.354), channel_id=1, source_target_pairs={{0,4},{4,8},{8,12},{12,0},{1,5},{5,9},{9,13},{13,1},{2,6},{6,10},{... | collective-permute-start | bytes 245768 | tf_op jit(solution)/shard_map/ppermute | solution.py:19
  48.5 4.4 %collective-permute-start.10 = (f32[5,16,2,128]{3,1,2,0:T(8,128)S(1)}, f32[5,16,2,128]{3,1,2,0:T(8,128)S(1)}, u32[]{:S(2)}, u32[]{:S(2)}) collective-permute-start(f32[5,16,2,128]{3,1,2,0:T(8,128)S(1)} %get-tuple-element.355), channel_id=1, source_target_pairs={{4,0},{8,4},{12,8},{0,12},{5,1},{9,5},{13,9},{1,13},{6,2},{10,6},{... | collective-permute-start | bytes 245768 | tf_op jit(solution)/shard_map/ppermute | solution.py:20
  53.0 9.1 %copy-start.32 = (f32[5,16,2,128]{3,1,2,0:T(8,128)S(1)}, f32[5,16,2,128]{3,1,2,0:T(8,128)}, u32[]{:S(2)}) copy-start(f32[5,16,2,128]{3,1,2,0:T(8,128)} %copy-done.31) | copy-start | bytes 245764
  58.2 11.4 %collective-permute-start.12 = (f32[5,16,12,2]{1,3,2,0:T(2,128)}, f32[5,16,12,2]{1,3,2,0:T(2,128)}, u32[]{:S(2)}, u32[]{:S(2)}) collective-permute-start(f32[5,16,12,2]{1,3,2,0:T(2,128)} %copy.88), channel_id=1, source_target_pairs={{1,0},{2,1},{3,2},{0,3},{5,4},{6,5},{7,6},{4,7},{9,8},{10,9},{11,1... | collective-permute-start | bytes 23048 | tf_op jit(solution)/shard_map/ppermute | solution.py:20
  62.1 6.3 %collective-permute-start.11 = (f32[5,16,12,2]{1,3,2,0:T(2,128)}, f32[5,16,12,2]{1,3,2,0:T(2,128)}, u32[]{:S(2)}, u32[]{:S(2)}) collective-permute-start(f32[5,16,12,2]{1,3,2,0:T(2,128)} %copy.87), channel_id=1, source_target_pairs={{0,1},{1,2},{2,3},{3,0},{4,5},{5,6},{6,7},{7,4},{8,9},{9,10},{10,1... | collective-permute-start | bytes 23048 | tf_op jit(solution)/shard_map/ppermute | solution.py:19
  96.3 3.5 %collective-permute-start.13 = (f32[5,16,8,128]{3,2,1,0:T(8,128)S(1)}, f32[5,16,8,128]{3,2,1,0:T(8,128)S(1)}, u32[]{:S(2)}, u32[]{:S(2)}) collective-permute-start(f32[5,16,8,128]{3,2,1,0:T(8,128)S(1)} %copy.72), channel_id=1, source_target_pairs={{16,0},{17,1},{18,2},{19,3},{20,4},{21,5},{22,6},{23,7},{24,8},{25... | collective-permute-start | bytes 983048 | tf_op jit(solution)/shard_map/ppermute | solution.py:28
  99.9 6.2 %collective-permute-start.14 = (f32[5,16,2,128]{3,1,2,0:T(8,128)S(1)}, f32[5,16,2,128]{3,1,2,0:T(8,128)S(1)}, u32[]{:S(2)}, u32[]{:S(2)}) collective-permute-start(f32[5,16,2,128]{3,1,2,0:T(8,128)S(1)} %copy.73), channel_id=1, source_target_pairs={{0,4},{4,8},{8,12},{12,0},{1,5},{5,9},{9,13},{13,1},{2,6},{6,10},{... | collective-permute-start | bytes 245768 | tf_op jit(solution)/shard_map/ppermute | solution.py:19
  101.4 4.9 %collective-permute-start.15 = (f32[5,16,2,128]{3,1,2,0:T(8,128)S(1)}, f32[5,16,2,128]{3,1,2,0:T(8,128)S(1)}, u32[]{:S(2)}, u32[]{:S(2)}) collective-permute-start(f32[5,16,2,128]{3,1,2,0:T(8,128)S(1)} %copy.74), channel_id=1, source_target_pairs={{4,0},{8,4},{12,8},{0,12},{5,1},{9,5},{13,9},{1,13},{6,2},{10,6},{... | collective-permute-start | bytes 245768 | tf_op jit(solution)/shard_map/ppermute | solution.py:20
  107.1 7.8 %copy-start.22 = (f32[5,16,8,128]{3,1,2,0:T(8,128)S(1)}, f32[5,16,8,128]{3,1,2,0:T(8,128)}, u32[]{:S(2)}) copy-start(f32[5,16,8,128]{3,1,2,0:T(8,128)} %copy-done.20) | copy-start | bytes 983044
  112.3 10.2 %collective-permute-start.17 = (f32[5,16,12,2]{1,3,2,0:T(2,128)}, f32[5,16,12,2]{1,3,2,0:T(2,128)}, u32[]{:S(2)}, u32[]{:S(2)}) collective-permute-start(f32[5,16,12,2]{1,3,2,0:T(2,128)} %copy.77), channel_id=1, source_target_pairs={{1,0},{2,1},{3,2},{0,3},{5,4},{6,5},{7,6},{4,7},{9,8},{10,9},{11,1... | collective-permute-start | bytes 23048 | tf_op jit(solution)/shard_map/ppermute | solution.py:20
  114.9 6.3 %collective-permute-start.16 = (f32[5,16,12,2]{1,3,2,0:T(2,128)}, f32[5,16,12,2]{1,3,2,0:T(2,128)}, u32[]{:S(2)}, u32[]{:S(2)}) collective-permute-start(f32[5,16,12,2]{1,3,2,0:T(2,128)} %copy.76), channel_id=1, source_target_pairs={{0,1},{1,2},{2,3},{3,0},{4,5},{5,6},{6,7},{7,4},{8,9},{9,10},{10,1... | collective-permute-start | bytes 23048 | tf_op jit(solution)/shard_map/ppermute | solution.py:19
  (44 other events, 79.6 us)
where the time goes:
time: 138 us; the launch traced here: 137 us
  other arithmetic  49.6 us (36%)
  local copies, waits for them, and re-layouts  38.6 us (28%)
  starting transfers between devices  30.5 us (22%)
  waiting for transfers between devices  17.1 us (12%)
  between operations  1.52 us (1%)
    unnamed x115, local copies, waits for them, and re-layouts  23.2 us
    ppermute x8, starting transfers between devices, padded_2(): after = lax.ppermute(leading, axis, down)  18.9 us
    ppermute x8, waiting for transfers between devices, padded_2(): before = lax.ppermute(last, axis, up)  12.9 us
    add x2, other arithmetic, heun_step(): section_state = interior(padded) + time_step * first_rate  12.2 us
    mul x6, other arithmetic, shrink_adjoint(): 0.5 * (window(padded, spatial, 1) - window(padded, spatial, -1))  9.23 us
    add x2, other arithmetic, heun_adjoint(): weighted = 0.5 * time_step * interior(padded) + time_step * section_cot  8.36 us
    ppermute x8, starting transfers between devices, padded_2(): before = lax.ppermute(last, axis, up)  8.09 us
    slice x9, local copies, waits for them, and re-layouts, padded_2(): last = lax.slice_in_dim(shard, length - width, length, axis=dim)  4.68 us
  transfers between devices with their start and end apart: 18, of which 8 were waited for; matrix products, arithmetic and copies ran while one was open for 16% of the time, Pallas kernels for 0%

commit v1 on v0

v1 whole, which is shorter than its diff:
```python
import jax
import jax.numpy as jnp
from jax import lax
from jax.experimental import pallas as pl
from jax.experimental.pallas import tpu as pltpu
from jax.sharding import PartitionSpec as P


NF = 5
WS = 6
WC = 4
ROWS = 8
HALF = 64
LANES = 128
TOTAL = ROWS + 2 * WS
FK = [(f, k) for f in range(NF) for k in range(2)]
VMEM_LIMIT = 32 * 2**20
UNROLL = 2


def lanes():
    lane = lax.broadcasted_iota(jnp.int32, (8, LANES), 1)
    core = lax.axis_index("grp")
    return lane, core, (lane + HALF * core) & (LANES - 1)


def turn(x, shift):
    return pltpu.roll(x, shift % LANES, 1)


def pack_kernel(own_ref, got_ref, t0, t1, up0, down0, up1, down1, side):
    lane, core, q = lanes()
    mine = q < HALF
    first = core == 0
    for f, k in FK:
        state, cot = [], []
        for r in range(ROWS):
            rows = pl.ds(f * 16 * ROWS + k * ROWS + r, 8, stride=2 * ROWS)
            a, b = own_ref[rows, :], got_ref[rows, :]
            state.append(jnp.where(first, a, b))
            cot.append(jnp.where(first, b, a))
            t0[r, f, k] = state[r]
            t1[r, f, k] = cot[r]
        for src, width, up, down in ((state, WS, up0, down0), (cot, WC, up1, down1)):
            n = width // 2
            for j in range(n):
                up[j, f, k] = jnp.where(
                    mine, src[ROWS - width + j], turn(src[ROWS - n + j], HALF)
                )
                down[j, f, k] = jnp.where(mine, src[j], turn(src[n + j], HALF))
        acc = jnp.zeros((8, LANES), jnp.float32)
        for src, width, base in ((state, WS, 0), (cot, WC, ROWS * WS)):
            for r in range(ROWS):
                at = base + width * r
                moved = pltpu.roll(src[r], at + width * core, 1)
                acc = jnp.where((lane >= at) & (lane < at + width), moved, acc)
        side[f, k] = acc


def beside(side, f, k, r, width, base, lane, core, tile):
    shift = LANES - width - base - width * r + width * core
    shift = jnp.where(shift >= LANES, shift - LANES, shift)
    moved = pltpu.roll(side[f, k], shift, 1)
    outer = ((lane + width * (1 - core)) & (LANES - 1)) < width
    return jnp.where(outer, moved, tile)


def corner_kernel(t0, t1, side, up, down):
    lane, core, q = lanes()
    for f, k in FK:
        tight = []
        for src, width, base in ((t0, WS, 0), (t1, WC, ROWS * WS)):
            rows = []
            for r in range(ROWS):
                full = beside(side, f, k, r, width, base, lane, core, src[r, f, k])
                gap = LANES - HALF - 2 * width
                rows.append(jnp.where(q >= HALF + width, turn(full, -gap), full))
            tight.append(rows)
        for out, lift in ((up, True), (down, False)):
            acc = jnp.zeros((8, LANES), jnp.float32)
            for rows, width, base in ((tight[0], WS, 0), (tight[1], WC, 2 * WS * WS)):
                for j in range(width):
                    at = base + 2 * width * j
                    moved = turn(rows[ROWS - width + j if lift else j], at - HALF)
                    acc = jnp.where((q >= at) & (q < at + 2 * width), moved, acc)
            out[f, k] = acc


def halo_row(packed, corner, f, k, j, width, base, q):
    n = width // 2
    row = packed[j % n, f, k]
    if j >= n:
        row = turn(row, HALF)
    at = base + 2 * width * j
    c = corner[f, k]
    row = jnp.where((q >= HALF) & (q < HALF + width), turn(c, HALF - at), row)
    return jnp.where(q >= LANES - width, turn(c, LANES - 2 * width - at), row)


def assemble(dst, offset, tile, side, low, high, clow, chigh, width, sbase, cbase):
    lane, core, q = lanes()
    for f, k in FK:
        for r in range(ROWS):
            dst[offset + width + r, f, k] = beside(
                side, f, k, r, width, sbase, lane, core, tile[r, f, k]
            )
        for j in range(width):
            dst[offset + j, f, k] = halo_row(low, clow, f, k, j, width, cbase, q)
            dst[offset + width + ROWS + j, f, k] = halo_row(
                high, chigh, f, k, j, width, cbase, q
            )


def load(ref, r):
    return [[ref[r, f, k] for f in range(NF)] for k in range(2)]


def invert(x):
    r = pl.reciprocal(x, approx=True)
    r = r * (2.0 - x * r)
    return r * (2.0 - x * r)


def fluxes(v):
    rho, m1, m2, m3, en = v
    inv = invert(rho)
    v1, v2, v3 = m1 * inv, m2 * inv, m3 * inv
    a, b, c = m1 * v1, m2 * v2, m3 * v3
    p = 0.4 * (en - 0.5 * (a + b + c))
    h = en + p
    m12, m13, m23 = m1 * v2, m1 * v3, m2 * v3
    return (
        (m1, a + p, m12, m13, h * v1),
        (m2, m12, b + p, m23, h * v2),
        (m3, m13, m23, c + p, h * v3),
    )


def pieces(v, want):
    prev = [[None] * 2 for _ in range(NF)]
    after = [[None] * 2 for _ in range(NF)]
    here = [[None] * 2 for _ in range(NF)]
    fl = [fluxes(v[k]) for k in range(2)]
    for f in range(NF):
        s = [0.2 * v[k][f] for k in range(2)]
        if "prev" in want:
            prev[f] = [s[k] - fl[k][0][f] for k in range(2)]
        if "after" in want:
            after[f] = [s[k] + fl[k][0][f] for k in range(2)]
        if "here" in want:
            ym = [s[k] - fl[k][1][f] for k in range(2)]
            yp = [s[k] + fl[k][1][f] for k in range(2)]
            zm = [s[k] - fl[k][2][f] for k in range(2)]
            zp = [s[k] + fl[k][2][f] for k in range(2)]
            zc = [
                zm[1] + pltpu.roll(zp[1], 1, 0),
                pltpu.roll(zm[0], 7, 0) + zp[0],
            ]
            here[f] = [
                (turn(ym[k], -1) + turn(yp[k], 1)) + (zc[k] - 1.2 * v[k][f])
                for k in range(2)
            ]
    return prev, after, here


def flat(x):
    return tuple(x[f][k] for f, k in FK)


def rate_pass(src, lo, hi, emit):
    _, after, _ = pieces(load(src, lo), ("after",))
    prev_after = flat(after)
    _, after, here = pieces(load(src, lo + 1), ("after", "here"))
    pend = tuple(a + b for a, b in zip(flat(here), prev_after))

    def body(r, carry):
        pend, prev_after = carry
        prev, after, here = pieces(load(src, r), ("prev", "after", "here"))
        emit(r - 1, [a + b for a, b in zip(pend, flat(prev))])
        return tuple(a + b for a, b in zip(flat(here), prev_after)), flat(after)

    pend, _ = lax.fori_loop(lo + 2, hi - 1, body, (pend, flat(after)), unroll=UNROLL)
    prev, _, _ = pieces(load(src, hi - 1), ("prev",))
    emit(hi - 2, [a + b for a, b in zip(pend, flat(prev))])


def forward_kernel(tile, side, low, high, clow, chigh, s0, u1, s1, u2, u0):
    assemble(u0, 0, tile, side, low, high, clow, chigh, WS, 0, 0)

    def section(base, dst):
        def emit(r, rate):
            for (f, k), x in zip(FK, rate):
                dst[r, f, k] = base[r, f, k] + 0.025 * x

        return emit

    def advance(base, sec, dst, shift):
        def emit(r, rate):
            for (f, k), x in zip(FK, rate):
                mean = 0.5 * (base[r, f, k] + sec[r, f, k])
                dst[r - shift, f, k] = mean + 0.0125 * x

        return emit

    rate_pass(u0, 0, TOTAL, section(u0, s0))
    rate_pass(s0, 1, TOTAL - 1, advance(u0, s0, u1, 0))
    rate_pass(u1, 2, TOTAL - 2, section(u1, s1))
    rate_pass(s1, WS - 1, WS + ROWS + 1, advance(u1, s1, u2, WS))


def pulled(state, w, r, emit, sr=None):
    v = load(state, r if sr is None else sr)
    wm, wc, wp = load(w, r - 1), load(w, r), load(w, r + 1)
    for k in range(2):
        rho, m1, m2, m3, en = v[k]
        inv = invert(rho)
        v1, v2, v3 = m1 * inv, m2 * inv, m3 * inv
        kin = 0.5 * (v1 * v1 + v2 * v2 + v3 * v3)
        p = 0.4 * (en - rho * kin)
        h = (en + p) * inv
        d1, d2, d3, around = [], [], [], []
        for f in range(NF):
            left, right = turn(wc[k][f], 1), turn(wc[k][f], -1)
            if k == 0:
                below, above = pltpu.roll(wc[1][f], 1, 0), wc[1][f]
            else:
                below, above = wc[0][f], pltpu.roll(wc[0][f], 7, 0)
            d1.append(wp[k][f] - wm[k][f])
            d2.append(right - left)
            d3.append(above - below)
            around.append(
                ((wp[k][f] + wm[k][f]) + (right + left)) + (above + below)
            )
        a = [(m1 * d1[f] + m2 * d2[f] + m3 * d3[f]) * (1.0 if f == 0 else inv) for f in range(NF)]
        b1, b2, b3 = [
            d[0] + v1 * d[1] + v2 * d[2] + v3 * d[3] + h * d[4] for d in (d1, d2, d3)
        ]
        pc = 0.4 * (d1[1] + d2[2] + d3[3] + a[4])
        out = [
            pc * kin - (a[1] * v1 + a[2] * v2 + a[3] * v3 + a[4] * h),
            b1 + a[1] - pc * v1,
            b2 + a[2] - pc * v2,
            b3 + a[3] - pc * v3,
            a[4] + pc,
        ]
        for f in range(NF):
            emit(f, k, out[f] + (0.2 * around[f] - 1.2 * wc[k][f]), wc[k][f])


def adjoint_kernel(
    tile0, tile1, side, low, high, clow, chigh, s0, u1, s1, u2,
    keep_a, keep_s, send, lam, cot, wgt, lam1,
):
    assemble(lam, WS - WC, tile1, side, low, high, clow, chigh, WC, ROWS * WS, 2 * WS * WS)
    lane, core, q = lanes()
    first = core == 0
    mine = q < HALF

    def section(state, lam, lo, hi):
        def body(r, _):
            def emit(f, k, x, w):
                c = 0.0125 * x
                cot[r, f, k] = c
                wgt[r, f, k] = 0.0125 * w + 0.025 * c

            pulled(state, lam, r, emit)
            return 0

        lax.fori_loop(lo, hi, body, 0, unroll=UNROLL)

    section(s1, lam, 3, TOTAL - 3)

    def first_body(r, _):
        def emit(f, k, x, w):
            lam1[r, f, k] = lam[r, f, k] + cot[r, f, k] + x

        pulled(u1, wgt, r, emit)
        return 0

    lax.fori_loop(4, TOTAL - 4, first_body, 0, unroll=UNROLL)
    section(s0, lam1, 5, TOTAL - 5)

    def last_body(r, _):
        i = r - WS

        def emit(f, k, x, w):
            before = lam1[r, f, k]
            start = before + cot[r, f, k] + x
            mid, end = u1[r, f, k], u2[i, f, k]
            keep_a[i, f, k] = jnp.where(first, start, before)
            keep_s[i, f, k] = jnp.where(first, mid, end)
            away_a = jnp.where(first, before, start)
            away_s = jnp.where(first, end, mid)
            send[i, f, k] = jnp.where(mine, away_a, turn(away_s, HALF))

        pulled(tile0, wgt, r, emit, sr=i)
        return 0

    lax.fori_loop(WS, WS + ROWS, last_body, 0, unroll=UNROLL)


def merge_kernel(keep_a, keep_s, got, out_a, out_s):
    lane, core, q = lanes()
    mine = q < HALF
    for f, k in FK:
        for r in range(ROWS):
            rows = pl.ds(f * 16 * ROWS + k * ROWS + r, 8, stride=2 * ROWS)
            other = got[r, f, k]
            out_a[rows, :] = jnp.where(mine, keep_a[r, f, k], other)
            out_s[rows, :] = jnp.where(mine, keep_s[r, f, k], turn(other, HALF))


def call(kernel, outs, scratch, *args, flops=0):
    shapes = [jax.ShapeDtypeStruct(s, jnp.float32) for s in outs]
    size = 4 * sum(a.size for a in args)
    return pl.pallas_call(
        kernel,
        out_shape=shapes,
        scratch_shapes=[pltpu.VMEM(s, jnp.float32) for s in scratch],
        compiler_params=pltpu.CompilerParams(vmem_limit_bytes=VMEM_LIMIT),
        cost_estimate=pl.CostEstimate(flops=flops, bytes_accessed=size, transcendentals=0),
    )(*args)


def rows_of(n):
    return (n, NF, 2, 8, LANES)


def ring(count, step):
    return [(i, (i + step) % count) for i in range(count)]


def shards(endpoints):
    shape = endpoints.shape
    tx, ty = lax.axis_size("tx"), lax.axis_size("ty")
    own = endpoints.reshape(-1, LANES)
    swap = [(0, 1), (1, 0)]
    got = lax.ppermute(own, "grp", swap)
    block = (NF, 2, 8, LANES)
    t0, t1, up0, down0, up1, down1, side = call(
        pack_kernel,
        [rows_of(ROWS), rows_of(ROWS), rows_of(WS // 2), rows_of(WS // 2),
         rows_of(WC // 2), rows_of(WC // 2), block],
        [],
        own, got,
    )
    pairs = [(i, ty + (i - 1) % ty) for i in range(ty)]
    pairs += [(b, a) for a, b in pairs]
    side = lax.ppermute(side, ("grp", "ty"), pairs)
    low0 = lax.ppermute(up0, "tx", ring(tx, 1))
    high0 = lax.ppermute(down0, "tx", ring(tx, -1))
    cup, cdown = call(corner_kernel, [block, block], [], t0, t1, side)
    clow = lax.ppermute(cup, "tx", ring(tx, 1))
    chigh = lax.ppermute(cdown, "tx", ring(tx, -1))
    low1 = lax.ppermute(up1, "tx", ring(tx, 1))
    high1 = lax.ppermute(down1, "tx", ring(tx, -1))
    full = rows_of(TOTAL)
    s0, u1, s1, u2 = call(
        forward_kernel, [full, full, full, rows_of(ROWS)], [full],
        t0, side, low0, high0, clow, chigh, flops=10**7,
    )
    keep_a, keep_s, send = call(
        adjoint_kernel, [rows_of(ROWS)] * 3, [full] * 4,
        t0, t1, side, low1, high1, clow, chigh, s0, u1, s1, u2, flops=10**7,
    )
    other = lax.ppermute(send, "grp", swap)
    adjoints, states = call(
        merge_kernel, [own.shape, own.shape], [], keep_a, keep_s, other
    )
    return adjoints.reshape(shape), states.reshape(shape)


def solution(mesh):
    placed = P("grp", None, None, "tx", "ty")
    return jax.shard_map(
        shards, mesh=mesh, in_specs=(placed,), out_specs=(placed, placed), check_vma=False
    )
```

time: 138 us -> 32.8 us (0.24)
  other arithmetic: 49.6 us -> 0 us
  local copies, waits for them, and re-layouts: 38.6 us -> 0.97 us
  starting transfers between devices: 30.5 us -> 13.6 us
  Pallas kernels: 0 us -> 10.3 us
  waiting for transfers between devices: 17.1 us -> 7.17 us
    add x6 -> x0, other arithmetic: 22.4 us -> none  [the longest x2 12.2 us: heun_step(): section_state = interior(padded) + time_step * first_rate]
    unnamed x115 -> x2, local copies, waits for them, and re-layouts: 23.2 us -> 0.97 us
    ppermute x18 -> x9, starting transfers between devices: 30.5 us -> 13.6 us  [the longest x1 4.78 us: shards(): side = lax.ppermute(side, ('grp', 'ty'), pairs)]
    mul x30 -> x0, other arithmetic: 12.2 us -> none  [the longest x6 9.23 us: shrink_adjoint(): 0.5 * (window(padded, spatial, 1) - window(padded, spatial, -1))]
    pallas_call x0 -> x5, Pallas kernels: none -> 10.3 us  [call(): pl.pallas_call(kernel, out_shape=shapes, scratch_shapes=[pltpu.VMEM(s, jn...]
    ppermute x18 -> x9, waiting for transfers between devices: 17.1 us -> 7.17 us  [the longest x1 2.28 us: shards(): chigh = lax.ppermute(cdown, 'tx', ring(tx, -1))]
    slice x12 -> x0, local copies, waits for them, and re-layouts: 6.8 us -> none  [the longest x9 4.68 us: padded_2(): last = lax.slice_in_dim(shard, length - width, length, axis=dim)]
    ppermute x8 -> x0, local copies, waits for them, and re-layouts: 6.73 us -> none  [the longest x4 3.39 us: padded_2(): after = lax.ppermute(leading, axis, down)]
  transfers between devices with their start and end apart: 18 -> 9, of which waited for: 8 -> 4; matrix products, arithmetic and copies ran while one was open for 16% -> 0% of each run, Pallas kernels for 0% -> 17%
where the time goes in v1:
time: 32.8 us; the launch traced here: 32.7 us
  starting transfers between devices  13.6 us (41%)
  Pallas kernels  10.3 us (31%)
  waiting for transfers between devices  7.17 us (22%)
  local copies, waits for them, and re-layouts  0.97 us (3%)
  between operations  0.68 us (2%)
    pallas_call x5, Pallas kernels, call(): pl.pallas_call(kernel, out_shape=shapes, scratch_shapes=[pltpu.VMEM(s, jn...  10.3 us
    ppermute x1, starting transfers between devices, shards(): side = lax.ppermute(side, ('grp', 'ty'), pairs)  4.78 us
    ppermute x1, starting transfers between devices, shards(): low1 = lax.ppermute(up1, 'tx', ring(tx, 1))  2.39 us
    ppermute x1, waiting for transfers between devices, shards(): chigh = lax.ppermute(cdown, 'tx', ring(tx, -1))  2.28 us
    ppermute x1, waiting for transfers between devices, shards(): clow = lax.ppermute(cup, 'tx', ring(tx, 1))  1.79 us
    ppermute x1, starting transfers between devices, shards(): chigh = lax.ppermute(cdown, 'tx', ring(tx, -1))  1.72 us
    ppermute x1, waiting for transfers between devices, shards(): other = lax.ppermute(send, 'grp', swap)  1.62 us
    ppermute x1, starting transfers between devices, shards(): low0 = lax.ppermute(up0, 'tx', ring(tx, 1))  1.49 us
  transfers between devices with their start and end apart: 9, of which 4 were waited for; matrix products, arithmetic and copies ran while one was open for 0% of the time, Pallas kernels for 17%

profile of v1, /device:TPU:0, one launch (start us, length us, event | category | flops | bytes accessed | tf_op | source)
XLA Modules:
  0.0 32.7 jit_solution(3889554856189092287)
XLA Ops:
  0.6 0.5 %collective-permute-start = (f32[640,128]{1,0:T(8,128)}, f32[640,128]{1,0:T(8,128)S(1)}, u32[]{:S(2)}, u32[]{:S(2)}) collective-permute-start(f32[640,128]{1,0:T(8,128)} %bitcast.3), channel_id=1, source_target_pairs={{0,16},{16,0},{1,17},{17,1},{2,18},{18,2},{3,19},{19,3},{4,20},{20... | collective-permute-start | bytes 983048 | tf_op jit(solution)/shard_map/ppermute | solution.py:338
  1.1 1.5 %collective-permute-done.got_ref = f32[640,128]{1,0:T(8,128)S(1)} collective-permute-done((f32[640,128]{1,0:T(8,128)}, f32[640,128]{1,0:T(8,128)S(1)}, u32[]{:S(2)}, u32[]{:S(2)}) %collective-permute-start) | collective-permute-done | bytes 327712 | tf_op jit(solution)/shard_map/ppermute | solution.py:338
  2.6 1.0 %copy-done = f32[1,5,16,8,128]{4,3,2,1,0:T(8,128)S(1)} copy-done((f32[1,5,16,8,128]{4,3,2,1,0:T(8,128)S(1)}, f32[1,5,16,8,128]{4,3,2,1,0:T(8,128)}, u32[]{:S(2)}) %copy-start) | copy-done | bytes 327704
  3.6 0.4 %shard_map.30 = (f32[8,5,2,8,128]{4,3,2,1,0:T(8,128)S(1)}, f32[8,5,2,8,128]{4,3,2,1,0:T(8,128)S(1)}, f32[3,5,2,8,128]{4,3,2,1,0:T(8,128)S(1)}, f32[3,5,2,8,128]{...) custom-call(f32[640,128]{1,0:T(8,128)S(1)} %bitcast.4, ...), custom_call_target="tpu_custom_call" | custom-call | bytes 655360 | tf_op jit(solution)/shard_map/pallas_call | solution.py:316
  4.0 4.8 %collective-permute-start.1 = (f32[5,2,8,128]{3,2,1,0:T(8,128)S(1)}, f32[5,2,8,128]{3,2,1,0:T(8,128)S(1)}, u32[]{:S(2)}, u32[]{:S(2)}) collective-permute-start(f32[5,2,8,128]{3,2,1,0:T(8,128)S(1)} %get-tuple-element.22), channel_id=1, source_target_pairs={{0,19},{1,16},{2,17},{3,18},{19,0},{16,1},{17,2},{18,3},{4,23},{5,... | collective-permute-start | bytes 122888 | tf_op jit(solution)/shard_map/ppermute | solution.py:349
  8.7 1.5 %collective-permute-start.6 = (f32[3,5,2,8,128]{4,3,2,1,0:T(8,128)S(1)}, f32[3,5,2,8,128]{4,3,2,1,0:T(8,128)S(1)}, u32[]{:S(2)}, u32[]{:S(2)}) collective-permute-start(f32[3,5,2,8,128]{4,3,2,1,0:T(8,128)S(1)} %get-tuple-element.27), channel_id=1, source_target_pairs={{0,4},{4,8},{8,12},{12,0},{1,5},{5,9},{9,13},{13,1},{2,6},{6,10},{... | collective-permute-start | bytes 368648 | tf_op jit(solution)/shard_map/ppermute | solution.py:350
  10.2 1.4 %collective-permute-start.7 = (f32[3,5,2,8,128]{4,3,2,1,0:T(8,128)S(1)}, f32[3,5,2,8,128]{4,3,2,1,0:T(8,128)S(1)}, u32[]{:S(2)}, u32[]{:S(2)}) collective-permute-start(f32[3,5,2,8,128]{4,3,2,1,0:T(8,128)S(1)} %get-tuple-element.28), channel_id=1, source_target_pairs={{0,12},{4,0},{8,4},{12,8},{1,13},{5,1},{9,5},{13,9},{2,14},{6,2},{... | collective-permute-start | bytes 368648 | tf_op jit(solution)/shard_map/ppermute | solution.py:351
  11.7 0.0 collective-permute-done.1.side
  11.7 1.4 %shard_map.31 = (f32[5,2,8,128]{3,2,1,0:T(8,128)S(1)}, f32[5,2,8,128]{3,2,1,0:T(8,128)S(1)}) custom-call(f32[8,5,2,8,128]{4,3,2,1,0:T(8,128)S(1)} %get-tuple-element.20.t0.tile.tile0, f32[8,5,2,8,128]{4,3,2,1,0:T(8,128)S(1)} %get-tuple-element.21.t1.tile1, f32[5,2,8,128]{3,2,1,0:T(8,128)S(1)} %collective-permute-done.1.side), custom_call_target="tpu_custom_call" | custom-call | bytes 696320 | tf_op jit(solution)/shard_map/pallas_call | solution.py:316
  13.1 0.6 %collective-permute-start.4 = (f32[5,2,8,128]{3,2,1,0:T(8,128)S(1)}, f32[5,2,8,128]{3,2,1,0:T(8,128)S(1)}, u32[]{:S(2)}, u32[]{:S(2)}) collective-permute-start(f32[5,2,8,128]{3,2,1,0:T(8,128)S(1)} %get-tuple-element.25), channel_id=1, source_target_pairs={{0,4},{4,8},{8,12},{12,0},{1,5},{5,9},{9,13},{13,1},{2,6},{6,10},{... | collective-permute-start | bytes 122888 | tf_op jit(solution)/shard_map/ppermute | solution.py:353
  13.8 2.4 %collective-permute-start.2 = (f32[2,5,2,8,128]{4,3,2,1,0:T(8,128)S(1)}, f32[2,5,2,8,128]{4,3,2,1,0:T(8,128)S(1)}, u32[]{:S(2)}, u32[]{:S(2)}) collective-permute-start(f32[2,5,2,8,128]{4,3,2,1,0:T(8,128)S(1)} %get-tuple-element.23), channel_id=1, source_target_pairs={{0,4},{4,8},{8,12},{12,0},{1,5},{5,9},{9,13},{13,1},{2,6},{6,10},{... | collective-permute-start | bytes 245768 | tf_op jit(solution)/shard_map/ppermute | solution.py:355
  16.2 0.5 %collective-permute-start.3 = (f32[2,5,2,8,128]{4,3,2,1,0:T(8,128)S(1)}, f32[2,5,2,8,128]{4,3,2,1,0:T(8,128)S(1)}, u32[]{:S(2)}, u32[]{:S(2)}) collective-permute-start(f32[2,5,2,8,128]{4,3,2,1,0:T(8,128)S(1)} %get-tuple-element.24), channel_id=1, source_target_pairs={{0,12},{4,0},{8,4},{12,8},{1,13},{5,1},{9,5},{13,9},{2,14},{6,2},{... | collective-permute-start | bytes 245768 | tf_op jit(solution)/shard_map/ppermute | solution.py:356
  16.7 1.8 %collective-permute-done.4.clow = f32[5,2,8,128]{3,2,1,0:T(8,128)S(1)} collective-permute-done((f32[5,2,8,128]{3,2,1,0:T(8,128)S(1)}, f32[5,2,8,128]{3,2,1,0:T(8,128)S(1)}, u32[]{:S(2)}, u32[]{:S(2)}) %collective-permute-start.4) | collective-permute-done | bytes 40992 | tf_op jit(solution)/shard_map/ppermute | solution.py:353
  18.5 1.7 %collective-permute-start.5 = (f32[5,2,8,128]{3,2,1,0:T(8,128)S(1)}, f32[5,2,8,128]{3,2,1,0:T(8,128)S(1)}, u32[]{:S(2)}, u32[]{:S(2)}) collective-permute-start(f32[5,2,8,128]{3,2,1,0:T(8,128)S(1)} %get-tuple-element.26), channel_id=1, source_target_pairs={{0,12},{4,0},{8,4},{12,8},{1,13},{5,1},{9,5},{13,9},{2,14},{6,2},{... | collective-permute-start | bytes 122888 | tf_op jit(solution)/shard_map/ppermute | solution.py:354
  20.2 2.3 %collective-permute-done.5.chigh = f32[5,2,8,128]{3,2,1,0:T(8,128)S(1)} collective-permute-done((f32[5,2,8,128]{3,2,1,0:T(8,128)S(1)}, f32[5,2,8,128]{3,2,1,0:T(8,128)S(1)}, u32[]{:S(2)}, u32[]{:S(2)}) %collective-permute-start.5) | collective-permute-done | bytes 40992 | tf_op jit(solution)/shard_map/ppermute | solution.py:354
  22.5 0.0 collective-permute-done.6.low
  22.5 0.0 collective-permute-done.7.high
  22.5 4.1 %shard_map.32 = (f32[20,5,2,8,128]{4,3,2,1,0:T(8,128)S(1)}, f32[20,5,2,8,128]{4,3,2,1,0:T(8,128)S(1)}, f32[20,5,2,8,128]{4,3,2,1,0:T(8,128)S(1)}, f32[8,5,2,8,128]{4,3,2,1,0:T(8,128)S(1)}) custom-call(f32[8,5,2,8,128]{4,3,2,1,0:T(8,128)S(1)} %get-tuple-element.20.t0.tile.tile0, f32[5,2,8,128]{3,2,1,0:T(8,128)S(1)} %collective-permute-done.1.side, ...), custom_call_target="tpu_custom_call" | custom-call | flops 10000000 | bytes 696320 | tf_op jit(solution)/shard_map/pallas_call | solution.py:316
  26.6 0.0 collective-permute-done.2.low
  26.6 0.0 collective-permute-done.3.high
  26.6 3.4 %shard_map.33 = (f32[8,5,2,8,128]{4,3,2,1,0:T(8,128)S(1)}, f32[8,5,2,8,128]{4,3,2,1,0:T(8,128)S(1)}, f32[8,5,2,8,128]{4,3,2,1,0:T(8,128)S(1)}) custom-call(f32[8,5,2,8,128]{4,3,2,1,0:T(8,128)S(1)} %get-tuple-element.20.t0.tile.tile0, f32[8,5,2,8,128]{4,3,2,1,0:T(8,128)S(1)} %get-tuple-element.21.t1.tile1, f32[5,2,8,128]{3,2,1,0:T(8,128)S(1)} %collective-permute-done.1.side, ...), custom_call_target="tpu_custom_call" | custom-call | flops 10000000 | bytes 3727360 | tf_op jit(solution)/shard_map/pallas_call | solution.py:316
  30.0 0.1 collective-permute-start.8
  30.1 1.6 %collective-permute-done.8.got = f32[8,5,2,8,128]{4,3,2,1,0:T(8,128)S(1)} collective-permute-done((f32[8,5,2,8,128]{4,3,2,1,0:T(8,128)S(1)}, f32[8,5,2,8,128]{4,3,2,1,0:T(8,128)S(1)}, u32[]{:S(2)}, u32[]{:S(2)}) %collective-permute-start.8) | collective-permute-done | bytes 327712 | tf_op jit(solution)/shard_map/ppermute | solution.py:366
  31.7 1.0 %shard_map.34 = (f32[640,128]{1,0:T(8,128)}, f32[640,128]{1,0:T(8,128)}) custom-call(f32[8,5,2,8,128]{4,3,2,1,0:T(8,128)S(1)} %get-tuple-element.33.keep_a, f32[8,5,2,8,128]{4,3,2,1,0:T(8,128)S(1)} %get-tuple-element.34.keep_s, f32[8,5,2,8,128]{4,3,2,1,0:T(8,128)S(1)} %collective-permute-done.8.got), custom_call_target="tpu_custom_call" | custom-call | bytes 983040 | tf_op jit(solution)/shard_map/pallas_call | solution.py:316
  (1 shorter events, 0.0 us)
Async XLA Ops:
  0.6 2.0 %collective-permute-start = (f32[640,128]{1,0:T(8,128)}, f32[640,128]{1,0:T(8,128)S(1)}, u32[]{:S(2)}, u32[]{:S(2)}) collective-permute-start(f32[640,128]{1,0:T(8,128)} %bitcast.3), channel_id=1, source_target_pairs={{0,16},{16,0},{1,17},{17,1},{2,18},{18,2},{3,19},{19,3},{4,20},{20... | collective-permute-start | bytes 983048 | tf_op jit(solution)/shard_map/ppermute | solution.py:338
  2.6 1.0 %copy-start = (f32[1,5,16,8,128]{4,3,2,1,0:T(8,128)S(1)}, f32[1,5,16,8,128]{4,3,2,1,0:T(8,128)}, u32[]{:S(2)}) copy-start(f32[1,5,16,8,128]{4,3,2,1,0:T(8,128)} %param.1) | copy-start | bytes 983044
  4.0 7.7 %collective-permute-start.1 = (f32[5,2,8,128]{3,2,1,0:T(8,128)S(1)}, f32[5,2,8,128]{3,2,1,0:T(8,128)S(1)}, u32[]{:S(2)}, u32[]{:S(2)}) collective-permute-start(f32[5,2,8,128]{3,2,1,0:T(8,128)S(1)} %get-tuple-element.22), channel_id=1, source_target_pairs={{0,19},{1,16},{2,17},{3,18},{19,0},{16,1},{17,2},{18,3},{4,23},{5,... | collective-permute-start | bytes 122888 | tf_op jit(solution)/shard_map/ppermute | solution.py:349
  8.7 13.7 %collective-permute-start.6 = (f32[3,5,2,8,128]{4,3,2,1,0:T(8,128)S(1)}, f32[3,5,2,8,128]{4,3,2,1,0:T(8,128)S(1)}, u32[]{:S(2)}, u32[]{:S(2)}) collective-permute-start(f32[3,5,2,8,128]{4,3,2,1,0:T(8,128)S(1)} %get-tuple-element.27), channel_id=1, source_target_pairs={{0,4},{4,8},{8,12},{12,0},{1,5},{5,9},{9,13},{13,1},{2,6},{6,10},{... | collective-permute-start | bytes 368648 | tf_op jit(solution)/shard_map/ppermute | solution.py:350
  10.2 12.3 %collective-permute-start.7 = (f32[3,5,2,8,128]{4,3,2,1,0:T(8,128)S(1)}, f32[3,5,2,8,128]{4,3,2,1,0:T(8,128)S(1)}, u32[]{:S(2)}, u32[]{:S(2)}) collective-permute-start(f32[3,5,2,8,128]{4,3,2,1,0:T(8,128)S(1)} %get-tuple-element.28), channel_id=1, source_target_pairs={{0,12},{4,0},{8,4},{12,8},{1,13},{5,1},{9,5},{13,9},{2,14},{6,2},{... | collective-permute-start | bytes 368648 | tf_op jit(solution)/shard_map/ppermute | solution.py:351
  13.1 5.4 %collective-permute-start.4 = (f32[5,2,8,128]{3,2,1,0:T(8,128)S(1)}, f32[5,2,8,128]{3,2,1,0:T(8,128)S(1)}, u32[]{:S(2)}, u32[]{:S(2)}) collective-permute-start(f32[5,2,8,128]{3,2,1,0:T(8,128)S(1)} %get-tuple-element.25), channel_id=1, source_target_pairs={{0,4},{4,8},{8,12},{12,0},{1,5},{5,9},{9,13},{13,1},{2,6},{6,10},{... | collective-permute-start | bytes 122888 | tf_op jit(solution)/shard_map/ppermute | solution.py:353
  13.8 12.8 %collective-permute-start.2 = (f32[2,5,2,8,128]{4,3,2,1,0:T(8,128)S(1)}, f32[2,5,2,8,128]{4,3,2,1,0:T(8,128)S(1)}, u32[]{:S(2)}, u32[]{:S(2)}) collective-permute-start(f32[2,5,2,8,128]{4,3,2,1,0:T(8,128)S(1)} %get-tuple-element.23), channel_id=1, source_target_pairs={{0,4},{4,8},{8,12},{12,0},{1,5},{5,9},{9,13},{13,1},{2,6},{6,10},{... | collective-permute-start | bytes 245768 | tf_op jit(solution)/shard_map/ppermute | solution.py:355
  16.2 10.4 %collective-permute-start.3 = (f32[2,5,2,8,128]{4,3,2,1,0:T(8,128)S(1)}, f32[2,5,2,8,128]{4,3,2,1,0:T(8,128)S(1)}, u32[]{:S(2)}, u32[]{:S(2)}) collective-permute-start(f32[2,5,2,8,128]{4,3,2,1,0:T(8,128)S(1)} %get-tuple-element.24), channel_id=1, source_target_pairs={{0,12},{4,0},{8,4},{12,8},{1,13},{5,1},{9,5},{13,9},{2,14},{6,2},{... | collective-permute-start | bytes 245768 | tf_op jit(solution)/shard_map/ppermute | solution.py:356
  18.5 4.0 %collective-permute-start.5 = (f32[5,2,8,128]{3,2,1,0:T(8,128)S(1)}, f32[5,2,8,128]{3,2,1,0:T(8,128)S(1)}, u32[]{:S(2)}, u32[]{:S(2)}) collective-permute-start(f32[5,2,8,128]{3,2,1,0:T(8,128)S(1)} %get-tuple-element.26), channel_id=1, source_target_pairs={{0,12},{4,0},{8,4},{12,8},{1,13},{5,1},{9,5},{13,9},{2,14},{6,2},{... | collective-permute-start | bytes 122888 | tf_op jit(solution)/shard_map/ppermute | solution.py:354
  30.0 1.7 %collective-permute-start.8 = (f32[8,5,2,8,128]{4,3,2,1,0:T(8,128)S(1)}, f32[8,5,2,8,128]{4,3,2,1,0:T(8,128)S(1)}, u32[]{:S(2)}, u32[]{:S(2)}) collective-permute-start(f32[8,5,2,8,128]{4,3,2,1,0:T(8,128)S(1)} %get-tuple-element.35), channel_id=1, source_target_pairs={{0,16},{16,0},{1,17},{17,1},{2,18},{18,2},{3,19},{19,3},{4,20},{20... | collective-permute-start | bytes 983048 | tf_op jit(solution)/shard_map/ppermute | solution.py:366

commit v2 on v1

v2 whole, which is shorter than its diff:
```python
import jax
import jax.numpy as jnp
from jax import lax
from jax.experimental import pallas as pl
from jax.experimental.pallas import tpu as pltpu
from jax.sharding import PartitionSpec as P


NF = 5
WS = 6
WC = 4
ROWS = 8
HALF = 64
LANES = 128
TOTAL = ROWS + 2 * WS
FK = [(f, k) for f in range(NF) for k in range(2)]
VMEM_LIMIT = 32 * 2**20
UNROLL = 4
CORNER = WS * (WS - 1) // 2 + WC * (WC - 1) // 2


def lanes():
    lane = lax.broadcasted_iota(jnp.int32, (8, LANES), 1)
    core = lax.axis_index("grp")
    return lane, core


def owned(lane, core):
    return ((lane + HALF * core) & (LANES - 1)) < HALF


def turn(x, shift):
    if isinstance(shift, int):
        shift %= LANES
    else:
        shift &= LANES - 1
    return pltpu.roll(x, shift, 1)


def triangle(width, base):
    return [(w, base + w * (w - 1) // 2) for w in reversed(range(width))]


def corner(which):
    return triangle(WS, 0) if which == 0 else triangle(WC, WS * (WS - 1) // 2)


def tile_lane(which, r):
    if which == 0:
        return CORNER + WS * r if r < 5 else HALF + CORNER + WS * (r - 5)
    if r < 3:
        return CORNER + 5 * WS + WC * r
    return HALF + CORNER + 3 * WS + WC * (r - 3)


def own_kernel(own, rows_out):
    for f, k in FK:
        for r in range(ROWS):
            rows = pl.ds(f * 16 * ROWS + k * ROWS + r, 8, stride=2 * ROWS)
            rows_out[r, f, k] = own[rows, :]


def pack_rows(tile, outs, width, lane, core):
    mine = owned(lane, core)
    n = width // 2
    for out, start in zip(outs, (ROWS - width, 0)):
        for j in range(n):
            dst, i = out(j)
            for f, k in FK:
                pair = turn(tile[start + n + j, f, k], HALF)
                dst[i + 2 * f + k] = jnp.where(mine, tile[start + j, f, k], pair)


def pack_kernel(own, got, t0, t1, first_up, first_down, rest_up, rest_down, side):
    lane, core = lanes()
    first = core == 0
    zero = jnp.zeros((8, LANES), jnp.float32)
    sides = [zero for _ in FK]
    edges = [[zero] * NF for _ in range(2)]
    for r in range(ROWS):
        rows = [[], []]
        for f, k in FK:
            at = pl.ds(f * 16 * ROWS + k * ROWS + r, 8, stride=2 * ROWS)
            a, b = own[r, f, k], got[at, :]
            rows[0].append(jnp.where(first, a, b))
            rows[1].append(jnp.where(first, b, a))
            t0[r, f, k] = rows[0][-1]
            t1[r, f, k] = rows[1][-1]
        for which, width in ((0, WS), (1, WC)):
            at = tile_lane(which, r)
            for k in range(2):
                place = (lane - 32 * k) & (LANES - 1)
                mask = (place >= at) & (place < at + width)
                for f in range(NF):
                    i = 2 * f + k
                    moved = turn(rows[which][i], at + 32 * k + width * core)
                    sides[i] = jnp.where(mask, moved, sides[i])
            for d, away in ((0, ROWS - 1 - r), (1, r)):
                if away >= width:
                    continue
                w, at2 = corner(which)[away]
                if w == 0:
                    continue
                for k in range(2):
                    place = (lane - 32 * k) & (HALF - 1)
                    mask = (place >= at2) & (place < at2 + w)
                    for f in range(NF):
                        shift = at2 + 32 * k + HALF * d + w * core
                        moved = turn(rows[which][2 * f + k], shift)
                        edges[d][f] = jnp.where(mask, moved, edges[d][f])
    for i, (f, k) in enumerate(FK):
        side[f, k] = sides[i]
    for f in range(NF):
        first_up[f] = edges[0][f]
        first_down[f] = edges[1][f]

    def out(head, rest):
        return lambda j: (head, NF) if j == 0 else (rest, 2 * NF * (j - 1))

    pack_rows(t0, (out(first_up, rest_up), out(first_down, rest_down)), WS, lane, core)


def side_kernel(side, low, high, t1, y, up1, down1):
    lane, core = lanes()
    for k in range(2):
        place = (lane - 32 * k) & (LANES - 1)
        for f in range(NF):
            with_high = jnp.where(
                (place >= HALF) & (place < HALF + CORNER), high[f], side[f, k]
            )
            y[f, k] = jnp.where(place < CORNER, low[f], with_high)
    pack_rows(
        t1, (lambda j: (up1, 2 * NF * j), lambda j: (down1, 2 * NF * j)), WC, lane, core
    )


def assemble(dst, offset, which, tile, y, edges, packed):
    lane, core = lanes()
    width = WC if which else WS
    n = width // 2
    for r in range(ROWS):
        outer = ((lane + width * (1 - core)) & (LANES - 1)) < width
        for f, k in FK:
            shift = LANES - width + width * core - tile_lane(which, r) - 32 * k
            dst[offset + width + r, f, k] = jnp.where(
                outer, turn(y[f, k], shift), tile[r, f, k]
            )
    for d in range(2):
        for away in range(width):
            w, at = corner(which)[away]
            j = width - 1 - away if d == 0 else away
            row = offset + j if d == 0 else offset + width + ROWS + j
            src, base = packed[d](j % n)
            if w:
                outer = ((lane + w * (1 - core)) & (LANES - 1)) < w
                inner = ((lane - HALF + w * core) & (LANES - 1)) < w
            for f, k in FK:
                v = src[base + 2 * f + k]
                if j >= n:
                    v = turn(v, HALF)
                if w:
                    o = turn(y[f, k], LANES - w + w * core - HALF * d - at - 32 * k)
                    i = turn(edges[d][f], HALF * d - at - 32 * k - w * core)
                    v = jnp.where(inner, i, jnp.where(outer, o, v))
                dst[row, f, k] = v


def load(ref, r):
    return [[ref[r, f, k] for f in range(NF)] for k in range(2)]


def invert(x):
    r = pltpu.reciprocal(x, approx=True)
    r = r * (2.0 - x * r)
    return r * (2.0 - x * r)


STEP = 0.025


def fluxes(v):
    rho, m1, m2, m3, en = v
    inv = STEP * invert(rho)
    v1, v2, v3 = m1 * inv, m2 * inv, m3 * inv
    a, b, c = m1 * v1, m2 * v2, m3 * v3
    p = (0.4 * STEP) * en - 0.2 * (a + b + c)
    h = en + (1.0 / STEP) * p
    m12, m13, m23 = m1 * v2, m1 * v3, m2 * v3
    return (
        (STEP * m1, a + p, m12, m13, h * v1),
        (STEP * m2, m12, b + p, m23, h * v2),
        (STEP * m3, m13, m23, c + p, h * v3),
    )


def pieces(v, want):
    prev = [[None] * 2 for _ in range(NF)]
    after = [[None] * 2 for _ in range(NF)]
    here = [[None] * 2 for _ in range(NF)]
    fl = [fluxes(v[k]) for k in range(2)]
    for f in range(NF):
        s = [(0.2 * STEP) * v[k][f] for k in range(2)]
        if "prev" in want:
            prev[f] = [s[k] - fl[k][0][f] for k in range(2)]
        if "after" in want:
            after[f] = [s[k] + fl[k][0][f] for k in range(2)]
        if "here" in want:
            ym = [s[k] - fl[k][1][f] for k in range(2)]
            yp = [s[k] + fl[k][1][f] for k in range(2)]
            zm = [s[k] - fl[k][2][f] for k in range(2)]
            zp = [s[k] + fl[k][2][f] for k in range(2)]
            zc = [
                zm[1] + pltpu.roll(zp[1], 1, 0),
                pltpu.roll(zm[0], 7, 0) + zp[0],
            ]
            here[f] = [(turn(ym[k], -1) + turn(yp[k], 1)) + zc[k] for k in range(2)]
    return prev, after, here


def flat(x):
    return tuple(x[f][k] for f, k in FK)


KEEP = 1.0 - 1.2 * STEP


def rate_pass(src, lo, hi, emit):
    _, after, _ = pieces(load(src, lo), ("after",))
    prev_after = flat(after)
    _, after, here = pieces(load(src, lo + 1), ("after", "here"))
    pend = tuple(a + b for a, b in zip(flat(here), prev_after))

    def body(r, carry):
        pend, prev_after = carry
        prev, after, here = pieces(load(src, r), ("prev", "after", "here"))
        emit(r - 1, [a + b for a, b in zip(pend, flat(prev))])
        return tuple(a + b for a, b in zip(flat(here), prev_after)), flat(after)

    pend, _ = lax.fori_loop(lo + 2, hi - 1, body, (pend, flat(after)), unroll=UNROLL)
    prev, _, _ = pieces(load(src, hi - 1), ("prev",))
    emit(hi - 2, [a + b for a, b in zip(pend, flat(prev))])


def forward_kernel(
    tile, y, first_low, first_high, rest_low, rest_high, s0, u1, s1, u2, u0
):
    def packed(head, rest):
        return lambda j: (head, NF) if j == 0 else (rest, 2 * NF * (j - 1))

    assemble(
        u0, 0, 0, tile, y, (first_low, first_high),
        (packed(first_low, rest_low), packed(first_high, rest_high)),
    )

    def section(base, dst):
        def emit(r, rate):
            for (f, k), x in zip(FK, rate):
                dst[r, f, k] = KEEP * base[r, f, k] + x

        return emit

    def advance(base, sec, dst, shift):
        def emit(r, rate):
            for (f, k), x in zip(FK, rate):
                dst[r - shift, f, k] = 0.5 * (
                    base[r, f, k] + (KEEP * sec[r, f, k] + x)
                )

        return emit

    rate_pass(u0, 0, TOTAL, section(u0, s0))
    rate_pass(s0, 1, TOTAL - 1, advance(u0, s0, u1, 0))
    rate_pass(u1, 2, TOTAL - 2, section(u1, s1))
    rate_pass(s1, WS - 1, WS + ROWS + 1, advance(u1, s1, u2, WS))


def pulled(state, w, r, emit, sr=None):
    v = load(state, r if sr is None else sr)
    wm, wc, wp = load(w, r - 1), load(w, r), load(w, r + 1)
    for k in range(2):
        rho, m1, m2, m3, en = v[k]
        inv = invert(rho)
        v1, v2, v3 = m1 * inv, m2 * inv, m3 * inv
        kin = 0.5 * (v1 * v1 + v2 * v2 + v3 * v3)
        p = 0.4 * (en - rho * kin)
        h = (en + p) * inv
        d1, d2, d3, around = [], [], [], []
        for f in range(NF):
            left, right = turn(wc[k][f], 1), turn(wc[k][f], -1)
            if k == 0:
                below, above = pltpu.roll(wc[1][f], 1, 0), wc[1][f]
            else:
                below, above = wc[0][f], pltpu.roll(wc[0][f], 7, 0)
            d1.append(wp[k][f] - wm[k][f])
            d2.append(right - left)
            d3.append(above - below)
            around.append(((wp[k][f] + wm[k][f]) + (right + left)) + (above + below))
        a = [
            (m1 * d1[f] + m2 * d2[f] + m3 * d3[f]) * (1.0 if f == 0 else inv)
            for f in range(NF)
        ]
        b1, b2, b3 = [
            d[0] + v1 * d[1] + v2 * d[2] + v3 * d[3] + h * d[4] for d in (d1, d2, d3)
        ]
        pc = 0.4 * (d1[1] + d2[2] + d3[3] + a[4])
        out = [
            pc * kin - (a[1] * v1 + a[2] * v2 + a[3] * v3 + a[4] * h),
            b1 + a[1] - pc * v1,
            b2 + a[2] - pc * v2,
            b3 + a[3] - pc * v3,
            a[4] + pc,
        ]
        for f in range(NF):
            emit(f, k, out[f] + (0.2 * around[f] - 1.2 * wc[k][f]), wc[k][f])


def adjoint_kernel(
    tile0, tile1, y, first_low, first_high, low, high, s0, u1, s1, u2,
    keep_a, keep_s, send, lam, cot, wgt, lam1,
):
    assemble(
        lam, WS - WC, 1, tile1, y, (first_low, first_high),
        (lambda j: (low, 2 * NF * j), lambda j: (high, 2 * NF * j)),
    )
    lane, core = lanes()
    first = core == 0
    mine = owned(lane, core)

    def section(state, lam, lo, hi):
        def body(r, _):
            def emit(f, k, x, w):
                c = 0.0125 * x
                cot[r, f, k] = c
                wgt[r, f, k] = 0.0125 * w + 0.025 * c

            pulled(state, lam, r, emit)
            return 0

        lax.fori_loop(lo, hi, body, 0, unroll=UNROLL)

    section(s1, lam, 3, TOTAL - 3)

    def first_body(r, _):
        def emit(f, k, x, w):
            lam1[r, f, k] = lam[r, f, k] + cot[r, f, k] + x

        pulled(u1, wgt, r, emit)
        return 0

    lax.fori_loop(4, TOTAL - 4, first_body, 0, unroll=UNROLL)
    section(s0, lam1, 5, TOTAL - 5)

    def last_body(r, _):
        i = r - WS

        def emit(f, k, x, w):
            before = lam1[r, f, k]
            start = before + cot[r, f, k] + x
            mid, end = u1[r, f, k], u2[i, f, k]
            keep_a[i, f, k] = jnp.where(first, start, before)
            keep_s[i, f, k] = jnp.where(first, mid, end)
            away_a = jnp.where(first, before, start)
            away_s = jnp.where(first, end, mid)
            send[i, f, k] = jnp.where(mine, away_a, turn(away_s, HALF))

        pulled(tile0, wgt, r, emit, sr=i)
        return 0

    lax.fori_loop(WS, WS + ROWS, last_body, 0, unroll=UNROLL)


def merge_kernel(keep_a, keep_s, got, out_a, out_s):
    lane, core = lanes()
    mine = owned(lane, core)
    for f, k in FK:
        for r in range(ROWS):
            rows = pl.ds(f * 16 * ROWS + k * ROWS + r, 8, stride=2 * ROWS)
            other = got[r, f, k]
            out_a[rows, :] = jnp.where(mine, keep_a[r, f, k], other)
            out_s[rows, :] = jnp.where(mine, keep_s[r, f, k], turn(other, HALF))


def call(kernel, name, outs, scratch, *args, flops=0):
    shapes = [jax.ShapeDtypeStruct(s, jnp.float32) for s in outs]
    size = 4 * sum(a.size for a in args)
    return pl.pallas_call(
        kernel,
        out_shape=shapes,
        name=name,
        scratch_shapes=[pltpu.VMEM(s, jnp.float32) for s in scratch],
        compiler_params=pltpu.CompilerParams(vmem_limit_bytes=VMEM_LIMIT),
        cost_estimate=pl.CostEstimate(flops=flops, bytes_accessed=size, transcendentals=0),
    )(*args)


def rows_of(n):
    return (n, NF, 2, 8, LANES)


def ring(count, step):
    return [(i, (i + step) % count) for i in range(count)]


def shards(endpoints):
    shape = endpoints.shape
    tx, ty = lax.axis_size("tx"), lax.axis_size("ty")
    own = endpoints.reshape(-1, LANES)
    swap = [(0, 1), (1, 0)]
    up, down = ring(tx, 1), ring(tx, -1)
    got = lax.ppermute(own, "grp", swap)
    (mine,) = call(own_kernel, "own", [rows_of(ROWS)], [], own, flops=10**6)
    block = (NF, 2, 8, LANES)
    head, rest = (3 * NF, 8, LANES), (4 * NF, 8, LANES)
    t0, t1, first_up, first_down, rest_up, rest_down, side = call(
        pack_kernel, "pack",
        [rows_of(ROWS), rows_of(ROWS), head, head, rest, rest, block], [], mine, got,
    )
    first_low = lax.ppermute(first_up, "tx", up)
    first_high = lax.ppermute(first_down, "tx", down)
    rest_low = lax.ppermute(rest_up, "tx", up)
    rest_high = lax.ppermute(rest_down, "tx", down)
    y, up1, down1 = call(
        side_kernel, "side", [block, rest, rest], [],
        side, first_low, first_high, t1, flops=10**9,
    )
    pairs = [(i, ty + (i - 1) % ty) for i in range(ty)]
    pairs += [(b, a) for a, b in pairs]
    y = lax.ppermute(y, ("grp", "ty"), pairs)
    low1 = lax.ppermute(up1, "tx", up)
    high1 = lax.ppermute(down1, "tx", down)
    full = rows_of(TOTAL)
    s0, u1, s1, u2 = call(
        forward_kernel, "forward", [full, full, full, rows_of(ROWS)], [full],
        t0, y, first_low, first_high, rest_low, rest_high, flops=10**9,
    )
    keep_a, keep_s, send = call(
        adjoint_kernel, "adjoint", [rows_of(ROWS)] * 3, [full] * 4,
        t0, t1, y, first_low, first_high, low1, high1, s0, u1, s1, u2, flops=10**8,
    )
    other = lax.ppermute(send, "grp", swap)
    adjoints, states = call(
        merge_kernel, "merge", [own.shape, own.shape], [], keep_a, keep_s, other
    )
    return adjoints.reshape(shape), states.reshape(shape)


def solution(mesh):
    placed = P("grp", None, None, "tx", "ty")
    return jax.shard_map(
        shards, mesh=mesh, in_specs=(placed,), out_specs=(placed, placed), check_vma=False
    )
```

time: 32.8 us -> 25.8 us (0.79)
  waiting for transfers between devices: 7.17 us -> 3.35 us
  Pallas kernels: 10.3 us -> 8 us
  starting transfers between devices: 13.6 us -> 12.7 us
    ppermute x7, waiting for transfers between devices: 4.08 us -> 1.35 us  [the longest x1 1.07 us: shards(): first_high = lax.ppermute(first_down, 'tx', down)]
    pallas_call x5 -> x6, Pallas kernels: 10.3 us -> 8 us  [call(): pl.pallas_call(kernel, out_shape=shapes, name=name, scratch_shapes=[pltpu...]
    ppermute x1, waiting for transfers between devices: 1.47 us -> 0.38 us  [shards(): got = lax.ppermute(own, 'grp', swap)]
    ppermute x7, starting transfers between devices: 13 us -> 12.1 us  [the longest x1 2.91 us: shards(): first_low = lax.ppermute(first_up, 'tx', up)]
  transfers between devices with their start and end apart: 9 -> 9, of which waited for: 4 -> 4; matrix products, arithmetic and copies ran while one was open for 0% -> 0% of each run, Pallas kernels for 17% -> 14%
where the time goes in v2:
time: 25.8 us; the launch traced here: 25.7 us
  starting transfers between devices  12.7 us (49%)
  Pallas kernels  8 us (31%)
  waiting for transfers between devices  3.35 us (13%)
  local copies, waits for them, and re-layouts  0.97 us (4%)
  between operations  0.69 us (3%)
    pallas_call x6, Pallas kernels, call(): pl.pallas_call(kernel, out_shape=shapes, name=name, scratch_shapes=[pltpu...  8 us
    ppermute x1, starting transfers between devices, shards(): first_low = lax.ppermute(first_up, 'tx', up)  2.91 us
    ppermute x1, starting transfers between devices, shards(): y = lax.ppermute(y, ('grp', 'ty'), pairs)  2.29 us
    ppermute x1, starting transfers between devices, shards(): rest_high = lax.ppermute(rest_down, 'tx', down)  1.92 us
    ppermute x1, waiting for transfers between devices, shards(): other = lax.ppermute(send, 'grp', swap)  1.62 us
    ppermute x1, starting transfers between devices, shards(): low1 = lax.ppermute(up1, 'tx', up)  1.61 us
    ppermute x1, starting transfers between devices, shards(): high1 = lax.ppermute(down1, 'tx', down)  1.31 us
    ppermute x1, waiting for transfers between devices, shards(): first_high = lax.ppermute(first_down, 'tx', down)  1.07 us
  transfers between devices with their start and end apart: 9, of which 4 were waited for; matrix products, arithmetic and copies ran while one was open for 0% of the time, Pallas kernels for 14%

profile of v2, /device:TPU:0, one launch (start us, length us, event | category | flops | bytes accessed | tf_op | source)
XLA Modules:
  0.0 25.7 jit_solution(5078827347868518564)
XLA Ops:
  0.6 0.5 %collective-permute-start = (f32[640,128]{1,0:T(8,128)}, f32[640,128]{1,0:T(8,128)S(1)}, u32[]{:S(2)}, u32[]{:S(2)}) collective-permute-start(f32[640,128]{1,0:T(8,128)} %bitcast.3), channel_id=1, source_target_pairs={{0,16},{16,0},{1,17},{17,1},{2,18},{18,2},{3,19},{19,3},{4,20},{20... | collective-permute-start | bytes 983048 | tf_op jit(solution)/shard_map/ppermute | solution.py:410
  1.1 1.0 %copy-done = f32[1,5,16,8,128]{4,3,2,1,0:T(8,128)S(1)} copy-done((f32[1,5,16,8,128]{4,3,2,1,0:T(8,128)S(1)}, f32[1,5,16,8,128]{4,3,2,1,0:T(8,128)}, u32[]{:S(2)}) %copy-start) | copy-done | bytes 327704
  2.1 0.1 own.1
  2.2 0.4 %collective-permute-done.got = f32[640,128]{1,0:T(8,128)S(1)} collective-permute-done((f32[640,128]{1,0:T(8,128)}, f32[640,128]{1,0:T(8,128)S(1)}, u32[]{:S(2)}, u32[]{:S(2)}) %collective-permute-start) | collective-permute-done | bytes 327712 | tf_op jit(solution)/shard_map/ppermute | solution.py:410
  2.6 0.5 %pack.1 = (f32[8,5,2,8,128]{4,3,2,1,0:T(8,128)S(1)}, f32[8,5,2,8,128]{4,3,2,1,0:T(8,128)S(1)}, f32[15,8,128]{2,1,0:T(8,128)S(1)}, f32[15,8,128]{2,1,0:T(8,128)S(...) custom-call(f32[8,5,2,8,128]{4,3,2,1,0:T(8,128)S(1)} %own.1, ...), custom_call_target="tpu_custom_call" | custom-call | bytes 655360 | tf_op jit(solution)/shard_map/pack/pallas_call | solution.py:386
  3.1 2.9 %collective-permute-start.1 = (f32[15,8,128]{2,1,0:T(8,128)S(1)}, f32[15,8,128]{2,1,0:T(8,128)S(1)}, u32[]{:S(2)}, u32[]{:S(2)}) collective-permute-start(f32[15,8,128]{2,1,0:T(8,128)S(1)} %get-tuple-element.24), channel_id=1, source_target_pairs={{0,4},{4,8},{8,12},{12,0},{1,5},{5,9},{9,13},{13,1},{2,6},{6,10},{... | collective-permute-start | bytes 184328 | tf_op jit(solution)/shard_map/ppermute | solution.py:418
  6.0 1.0 %collective-permute-start.2 = (f32[15,8,128]{2,1,0:T(8,128)S(1)}, f32[15,8,128]{2,1,0:T(8,128)S(1)}, u32[]{:S(2)}, u32[]{:S(2)}) collective-permute-start(f32[15,8,128]{2,1,0:T(8,128)S(1)} %get-tuple-element.25), channel_id=1, source_target_pairs={{0,12},{4,0},{8,4},{12,8},{1,13},{5,1},{9,5},{13,9},{2,14},{6,2},{... | collective-permute-start | bytes 184328 | tf_op jit(solution)/shard_map/ppermute | solution.py:419
  7.0 1.0 %collective-permute-start.6 = (f32[20,8,128]{2,1,0:T(8,128)S(1)}, f32[20,8,128]{2,1,0:T(8,128)S(1)}, u32[]{:S(2)}, u32[]{:S(2)}) collective-permute-start(f32[20,8,128]{2,1,0:T(8,128)S(1)} %get-tuple-element.29), channel_id=1, source_target_pairs={{0,4},{4,8},{8,12},{12,0},{1,5},{5,9},{9,13},{13,1},{2,6},{6,10},{... | collective-permute-start | bytes 245768 | tf_op jit(solution)/shard_map/ppermute | solution.py:420
  8.1 1.9 %collective-permute-start.7 = (f32[20,8,128]{2,1,0:T(8,128)S(1)}, f32[20,8,128]{2,1,0:T(8,128)S(1)}, u32[]{:S(2)}, u32[]{:S(2)}) collective-permute-start(f32[20,8,128]{2,1,0:T(8,128)S(1)} %get-tuple-element.30), channel_id=1, source_target_pairs={{0,12},{4,0},{8,4},{12,8},{1,13},{5,1},{9,5},{13,9},{2,14},{6,2},{... | collective-permute-start | bytes 245768 | tf_op jit(solution)/shard_map/ppermute | solution.py:421
  10.0 0.0 collective-permute-done.1.low.first_low
  10.0 1.1 %collective-permute-done.2.high.first_high = f32[15,8,128]{2,1,0:T(8,128)S(1)} collective-permute-done((f32[15,8,128]{2,1,0:T(8,128)S(1)}, f32[15,8,128]{2,1,0:T(8,128)S(1)}, u32[]{:S(2)}, u32[]{:S(2)}) %collective-permute-start.2) | collective-permute-done | bytes 61472 | tf_op jit(solution)/shard_map/ppermute | solution.py:419
  11.0 0.1 side.1
  11.2 2.3 %collective-permute-start.3 = (f32[5,2,8,128]{3,2,1,0:T(8,128)S(1)}, f32[5,2,8,128]{3,2,1,0:T(8,128)S(1)}, u32[]{:S(2)}, u32[]{:S(2)}) collective-permute-start(f32[5,2,8,128]{3,2,1,0:T(8,128)S(1)} %get-tuple-element.26), channel_id=1, source_target_pairs={{0,19},{1,16},{2,17},{3,18},{19,0},{16,1},{17,2},{18,3},{4,23},{5,... | collective-permute-start | bytes 122888 | tf_op jit(solution)/shard_map/ppermute | solution.py:428
  13.5 1.6 %collective-permute-start.4 = (f32[20,8,128]{2,1,0:T(8,128)S(1)}, f32[20,8,128]{2,1,0:T(8,128)S(1)}, u32[]{:S(2)}, u32[]{:S(2)}) collective-permute-start(f32[20,8,128]{2,1,0:T(8,128)S(1)} %get-tuple-element.27), channel_id=1, source_target_pairs={{0,4},{4,8},{8,12},{12,0},{1,5},{5,9},{9,13},{13,1},{2,6},{6,10},{... | collective-permute-start | bytes 245768 | tf_op jit(solution)/shard_map/ppermute | solution.py:429
  15.1 1.3 %collective-permute-start.5 = (f32[20,8,128]{2,1,0:T(8,128)S(1)}, f32[20,8,128]{2,1,0:T(8,128)S(1)}, u32[]{:S(2)}, u32[]{:S(2)}) collective-permute-start(f32[20,8,128]{2,1,0:T(8,128)S(1)} %get-tuple-element.28), channel_id=1, source_target_pairs={{0,12},{4,0},{8,4},{12,8},{1,13},{5,1},{9,5},{13,9},{2,14},{6,2},{... | collective-permute-start | bytes 245768 | tf_op jit(solution)/shard_map/ppermute | solution.py:430
  16.4 0.0 collective-permute-done.6.rest_low
  16.4 0.0 collective-permute-done.7.rest_high
  16.4 0.2 collective-permute-done.3.y
  16.6 3.3 %forward.1 = (f32[20,5,2,8,128]{4,3,2,1,0:T(8,128)S(1)}, f32[20,5,2,8,128]{4,3,2,1,0:T(8,128)S(1)}, f32[20,5,2,8,128]{4,3,2,1,0:T(8,128)S(1)}, f32[8,5,2,8,128]{4,3,2,1,0:T(8,128)S(1)}) custom-call(f32[8,5,2,8,128]{4,3,2,1,0:T(8,128)S(1)} %get-tuple-element.21.tile.tile0, f32[5,2,8,128]{3,2,1,0:T(8,128)S(1)} %collective-permute-done.3.y, ...), custom_call_target="tpu_custom_call" | custom-call | flops 1000000000 | bytes 655360 | tf_op jit(solution)/shard_map/forward/pallas_call | solution.py:386
  20.0 0.0 collective-permute-done.5.high
  20.0 3.0 %adjoint.1 = (f32[8,5,2,8,128]{4,3,2,1,0:T(8,128)S(1)}, f32[8,5,2,8,128]{4,3,2,1,0:T(8,128)S(1)}, f32[8,5,2,8,128]{4,3,2,1,0:T(8,128)S(1)}) custom-call(f32[8,5,2,8,128]{4,3,2,1,0:T(8,128)S(1)} %get-tuple-element.21.tile.tile0, f32[8,5,2,8,128]{4,3,2,1,0:T(8,128)S(1)} %get-tuple-element.22.t1.tile1, f32[5,2,8,128]{3,2,1,0:T(8,128)S(1)} %collective-permute-done.3.y, ...), custom_call_target="tpu_custom_call" | custom-call | flops 100000000 | bytes 3768320 | tf_op jit(solution)/shard_map/adjoint/pallas_call | solution.py:386
  23.0 0.1 collective-permute-start.8
  23.1 1.6 %collective-permute-done.8.got = f32[8,5,2,8,128]{4,3,2,1,0:T(8,128)S(1)} collective-permute-done((f32[8,5,2,8,128]{4,3,2,1,0:T(8,128)S(1)}, f32[8,5,2,8,128]{4,3,2,1,0:T(8,128)S(1)}, u32[]{:S(2)}, u32[]{:S(2)}) %collective-permute-start.8) | collective-permute-done | bytes 327712 | tf_op jit(solution)/shard_map/ppermute | solution.py:440
  24.7 1.0 %merge.1 = (f32[640,128]{1,0:T(8,128)}, f32[640,128]{1,0:T(8,128)}) custom-call(f32[8,5,2,8,128]{4,3,2,1,0:T(8,128)S(1)} %get-tuple-element.35.keep_a, f32[8,5,2,8,128]{4,3,2,1,0:T(8,128)S(1)} %get-tuple-element.36.keep_s, f32[8,5,2,8,128]{4,3,2,1,0:T(8,128)S(1)} %collective-permute-done.8.got), custom_call_target="tpu_custom_call" | custom-call | bytes 983040 | tf_op jit(solution)/shard_map/merge/pallas_call | solution.py:386
  (2 shorter events, 0.0 us)
Async XLA Ops:
  0.6 2.0 %collective-permute-start = (f32[640,128]{1,0:T(8,128)}, f32[640,128]{1,0:T(8,128)S(1)}, u32[]{:S(2)}, u32[]{:S(2)}) collective-permute-start(f32[640,128]{1,0:T(8,128)} %bitcast.3), channel_id=1, source_target_pairs={{0,16},{16,0},{1,17},{17,1},{2,18},{18,2},{3,19},{19,3},{4,20},{20... | collective-permute-start | bytes 983048 | tf_op jit(solution)/shard_map/ppermute | solution.py:410
  1.1 1.0 %copy-start = (f32[1,5,16,8,128]{4,3,2,1,0:T(8,128)S(1)}, f32[1,5,16,8,128]{4,3,2,1,0:T(8,128)}, u32[]{:S(2)}) copy-start(f32[1,5,16,8,128]{4,3,2,1,0:T(8,128)} %param.1) | copy-start | bytes 983044
  3.1 6.9 %collective-permute-start.1 = (f32[15,8,128]{2,1,0:T(8,128)S(1)}, f32[15,8,128]{2,1,0:T(8,128)S(1)}, u32[]{:S(2)}, u32[]{:S(2)}) collective-permute-start(f32[15,8,128]{2,1,0:T(8,128)S(1)} %get-tuple-element.24), channel_id=1, source_target_pairs={{0,4},{4,8},{8,12},{12,0},{1,5},{5,9},{9,13},{13,1},{2,6},{6,10},{... | collective-permute-start | bytes 184328 | tf_op jit(solution)/shard_map/ppermute | solution.py:418
  6.0 5.0 %collective-permute-start.2 = (f32[15,8,128]{2,1,0:T(8,128)S(1)}, f32[15,8,128]{2,1,0:T(8,128)S(1)}, u32[]{:S(2)}, u32[]{:S(2)}) collective-permute-start(f32[15,8,128]{2,1,0:T(8,128)S(1)} %get-tuple-element.25), channel_id=1, source_target_pairs={{0,12},{4,0},{8,4},{12,8},{1,13},{5,1},{9,5},{13,9},{2,14},{6,2},{... | collective-permute-start | bytes 184328 | tf_op jit(solution)/shard_map/ppermute | solution.py:419
  7.0 9.3 %collective-permute-start.6 = (f32[20,8,128]{2,1,0:T(8,128)S(1)}, f32[20,8,128]{2,1,0:T(8,128)S(1)}, u32[]{:S(2)}, u32[]{:S(2)}) collective-permute-start(f32[20,8,128]{2,1,0:T(8,128)S(1)} %get-tuple-element.29), channel_id=1, source_target_pairs={{0,4},{4,8},{8,12},{12,0},{1,5},{5,9},{9,13},{13,1},{2,6},{6,10},{... | collective-permute-start | bytes 245768 | tf_op jit(solution)/shard_map/ppermute | solution.py:420
  8.1 8.3 %collective-permute-start.7 = (f32[20,8,128]{2,1,0:T(8,128)S(1)}, f32[20,8,128]{2,1,0:T(8,128)S(1)}, u32[]{:S(2)}, u32[]{:S(2)}) collective-permute-start(f32[20,8,128]{2,1,0:T(8,128)S(1)} %get-tuple-element.30), channel_id=1, source_target_pairs={{0,12},{4,0},{8,4},{12,8},{1,13},{5,1},{9,5},{13,9},{2,14},{6,2},{... | collective-permute-start | bytes 245768 | tf_op jit(solution)/shard_map/ppermute | solution.py:421
  11.2 5.5 %collective-permute-start.3 = (f32[5,2,8,128]{3,2,1,0:T(8,128)S(1)}, f32[5,2,8,128]{3,2,1,0:T(8,128)S(1)}, u32[]{:S(2)}, u32[]{:S(2)}) collective-permute-start(f32[5,2,8,128]{3,2,1,0:T(8,128)S(1)} %get-tuple-element.26), channel_id=1, source_target_pairs={{0,19},{1,16},{2,17},{3,18},{19,0},{16,1},{17,2},{18,3},{4,23},{5,... | collective-permute-start | bytes 122888 | tf_op jit(solution)/shard_map/ppermute | solution.py:428
  13.5 6.5 %collective-permute-start.4 = (f32[20,8,128]{2,1,0:T(8,128)S(1)}, f32[20,8,128]{2,1,0:T(8,128)S(1)}, u32[]{:S(2)}, u32[]{:S(2)}) collective-permute-start(f32[20,8,128]{2,1,0:T(8,128)S(1)} %get-tuple-element.27), channel_id=1, source_target_pairs={{0,4},{4,8},{8,12},{12,0},{1,5},{5,9},{9,13},{13,1},{2,6},{6,10},{... | collective-permute-start | bytes 245768 | tf_op jit(solution)/shard_map/ppermute | solution.py:429
  15.1 4.9 %collective-permute-start.5 = (f32[20,8,128]{2,1,0:T(8,128)S(1)}, f32[20,8,128]{2,1,0:T(8,128)S(1)}, u32[]{:S(2)}, u32[]{:S(2)}) collective-permute-start(f32[20,8,128]{2,1,0:T(8,128)S(1)} %get-tuple-element.28), channel_id=1, source_target_pairs={{0,12},{4,0},{8,4},{12,8},{1,13},{5,1},{9,5},{13,9},{2,14},{6,2},{... | collective-permute-start | bytes 245768 | tf_op jit(solution)/shard_map/ppermute | solution.py:430
  23.0 1.7 %collective-permute-start.8 = (f32[8,5,2,8,128]{4,3,2,1,0:T(8,128)S(1)}, f32[8,5,2,8,128]{4,3,2,1,0:T(8,128)S(1)}, u32[]{:S(2)}, u32[]{:S(2)}) collective-permute-start(f32[8,5,2,8,128]{4,3,2,1,0:T(8,128)S(1)} %get-tuple-element.37), channel_id=1, source_target_pairs={{0,16},{16,0},{1,17},{17,1},{2,18},{18,2},{3,19},{19,3},{4,20},{20... | collective-permute-start | bytes 983048 | tf_op jit(solution)/shard_map/ppermute | solution.py:440

commit v3 on v2

v3 whole, which is shorter than its diff:
```python
import jax
import jax.numpy as jnp
from jax import lax
from jax.experimental import pallas as pl
from jax.experimental.pallas import tpu as pltpu
from jax.sharding import PartitionSpec as P


NF = 5
WS = 6
WC = 4
ROWS = 8
HALF = 64
LANES = 128
TOTAL = ROWS + 2 * WS
FK = [(f, k) for f in range(NF) for k in range(2)]
VMEM_LIMIT = 32 * 2**20
UNROLL = 4
UP1 = WS * NF
CORNER = WS * (WS - 1) // 2 + WC * (WC - 1) // 2


def lanes():
    lane = lax.broadcasted_iota(jnp.int32, (8, LANES), 1)
    core = lax.axis_index("grp")
    return lane, core


def owned(lane, core):
    return ((lane + HALF * core) & (LANES - 1)) < HALF


def turn(x, shift):
    if isinstance(shift, int):
        shift %= LANES
    else:
        shift &= LANES - 1
    return pltpu.roll(x, shift, 1)


def triangle(width, base):
    return [(w, base + w * (w - 1) // 2) for w in reversed(range(width))]


def corner(which):
    return triangle(WS, 0) if which == 0 else triangle(WC, WS * (WS - 1) // 2)


def tile_lane(which, r):
    if which == 0:
        return CORNER + WS * r if r < 5 else HALF + CORNER + WS * (r - 5)
    if r < 3:
        return CORNER + 5 * WS + WC * r
    return HALF + CORNER + 3 * WS + WC * (r - 3)


def own_kernel(own, rows_out):
    for f, k in FK:
        for r in range(ROWS):
            rows = pl.ds(f * 16 * ROWS + k * ROWS + r, 8, stride=2 * ROWS)
            rows_out[r, f, k] = own[rows, :]


def pack_rows(tile, out, start, n, pairs, base, lane, core):
    mine = owned(lane, core)
    for i, j in enumerate(pairs):
        for f, k in FK:
            other = turn(tile[start + n + j, f, k], HALF)
            at = base + 2 * NF * i + 2 * f + k
            out[at] = jnp.where(mine, tile[start + j, f, k], other)


def first_kernel(own, got, t0, t1, first_up, first_down):
    lane, core = lanes()
    first = core == 0
    zero = jnp.zeros((8, LANES), jnp.float32)
    edges = [[zero] * NF for _ in range(2)]
    for r in range(ROWS):
        rows = [[], []]
        for f, k in FK:
            at = pl.ds(f * 16 * ROWS + k * ROWS + r, 8, stride=2 * ROWS)
            a, b = own[r, f, k], got[at, :]
            rows[0].append(jnp.where(first, a, b))
            rows[1].append(jnp.where(first, b, a))
            t0[r, f, k] = rows[0][-1]
            t1[r, f, k] = rows[1][-1]
        for which, width in ((0, WS), (1, WC)):
            for d, away in ((0, ROWS - 1 - r), (1, r)):
                if away >= width:
                    continue
                w, at = corner(which)[away]
                if w == 0:
                    continue
                for k in range(2):
                    place = (lane - 32 * k) & (HALF - 1)
                    mask = (place >= at) & (place < at + w)
                    for f in range(NF):
                        shift = at + 32 * k + HALF * d + w * core
                        moved = turn(rows[which][2 * f + k], shift)
                        edges[d][f] = jnp.where(mask, moved, edges[d][f])
    for f in range(NF):
        first_up[f] = edges[0][f]
        first_down[f] = edges[1][f]


def rest_kernel(t0, t1, side, rest_up, rest_down):
    lane, core = lanes()
    pack_rows(t0, rest_up, ROWS - WS, WS // 2, (0, 1, 2), 0, lane, core)
    pack_rows(t0, rest_down, 0, WS // 2, (0, 1, 2), 0, lane, core)
    sides = [jnp.zeros((8, LANES), jnp.float32) for _ in FK]
    for r in range(ROWS):
        for which, width, tile in ((0, WS, t0), (1, WC, t1)):
            at = tile_lane(which, r)
            for k in range(2):
                place = (lane - 32 * k) & (LANES - 1)
                mask = (place >= at) & (place < at + width)
                for f in range(NF):
                    i = 2 * f + k
                    moved = turn(tile[r, f, k], at + 32 * k + width * core)
                    sides[i] = jnp.where(mask, moved, sides[i])
    for i, (f, k) in enumerate(FK):
        side[f, k] = sides[i]


def side_kernel(side, low, high, t1, y, up1, down1):
    lane, core = lanes()
    for k in range(2):
        place = (lane - 32 * k) & (LANES - 1)
        for f in range(NF):
            with_high = jnp.where(
                (place >= HALF) & (place < HALF + CORNER), high[f], side[f, k]
            )
            y[f, k] = jnp.where(place < CORNER, low[f], with_high)
    pack_rows(t1, up1, ROWS - WC, WC // 2, (0, 1), 0, lane, core)
    pack_rows(t1, down1, 0, WC // 2, (0, 1), 0, lane, core)


def assemble_tile(dst, offset, which, tile, y):
    lane, core = lanes()
    width = WC if which else WS
    for r in range(ROWS):
        outer = ((lane + width * (1 - core)) & (LANES - 1)) < width
        for f, k in FK:
            shift = LANES - width + width * core - tile_lane(which, r) - 32 * k
            dst[offset + r, f, k] = jnp.where(outer, turn(y[f, k], shift), tile[r, f, k])


def assemble_halo(dst, offset, which, d, y, edges, packed):
    lane, core = lanes()
    mine = owned(lane, core)
    width = WC if which else WS
    n = width // 2
    for away in range(width):
        w, at = corner(which)[away]
        j = away if d else width - 1 - away
        src, base = packed(j % n)
        if w:
            outer = ((lane + w * (1 - core)) & (LANES - 1)) < w
            inner = ((lane - HALF + w * core) & (LANES - 1)) < w
        for f, k in FK:
            v = src[base + 2 * f + k]
            if j >= n:
                v = turn(v, HALF)
            if w:
                o = turn(y[f, k], LANES - w + w * core - HALF * d - at - 32 * k)
                i = turn(edges[f], HALF * d - at - 32 * k - w * core)
                v = jnp.where(inner, i, jnp.where(outer, o, v))
            dst[offset + j, f, k] = v


def halo_kernel(t0, t1, y, first_low, first_high, rest_low, rest_high, u0, lam):
    assemble_halo(u0, 0, 0, 0, y, first_low, lambda j: (rest_low, 2 * NF * j))
    assemble_tile(u0, WS, 0, t0, y)
    assemble_halo(u0, WS + ROWS, 0, 1, y, first_high, lambda j: (rest_high, 2 * NF * j))
    assemble_tile(lam, WS, 1, t1, y)


def load(ref, r):
    return [[ref[r, f, k] for f in range(NF)] for k in range(2)]


def invert(x):
    return pltpu.reciprocal(x, approx=True)


STEP = 0.025


def fluxes(v):
    rho, m1, m2, m3, en = v
    inv = STEP * invert(rho)
    v1, v2, v3 = m1 * inv, m2 * inv, m3 * inv
    a, b, c = m1 * v1, m2 * v2, m3 * v3
    p = (0.4 * STEP) * en - 0.2 * (a + b + c)
    h = en + (1.0 / STEP) * p
    m12, m13, m23 = m1 * v2, m1 * v3, m2 * v3
    return (
        (STEP * m1, a + p, m12, m13, h * v1),
        (STEP * m2, m12, b + p, m23, h * v2),
        (STEP * m3, m13, m23, c + p, h * v3),
    )


def pieces(v, along_y=True):
    before, after, here, left, right = [], [], [], [], []
    fl = [fluxes(v[k]) for k in range(2)]
    for f in range(NF):
        s = [(0.2 * STEP) * v[k][f] for k in range(2)]
        before += [s[k] - fl[k][0][f] for k in range(2)]
        after += [s[k] + fl[k][0][f] for k in range(2)]
        if along_y:
            zm = [s[k] - fl[k][2][f] for k in range(2)]
            zp = [s[k] + fl[k][2][f] for k in range(2)]
            here += [
                zm[1] + pltpu.roll(zp[1], 1, 0),
                pltpu.roll(zm[0], 7, 0) + zp[0],
            ]
            left += [s[k] - fl[k][1][f] for k in range(2)]
            right += [s[k] + fl[k][1][f] for k in range(2)]
    return before, after, here, left, right


KEEP = 1.0 - 1.2 * STEP


def rate_pass(src, lo, hi, emit):
    _, edge, _, _, _ = pieces(load(src, lo), False)
    _, after, here, left, right = pieces(load(src, lo + 1))
    here = [a + b for a, b in zip(here, edge)]

    def done(here, left, right, before):
        return [
            (turn(a, -1) + turn(b, 1)) + (c + d)
            for a, b, c, d in zip(left, right, here, before)
        ]

    def body(r, carry):
        here, after, left, right = carry
        before, after2, here2, left2, right2 = pieces(load(src, r))
        emit(r - 1, done(here, left, right, before))
        here2 = [a + b for a, b in zip(here2, after)]
        return here2, after2, left2, right2

    here, _, left, right = lax.fori_loop(
        lo + 2, hi - 1, body, (here, after, left, right), unroll=UNROLL
    )
    before, _, _, _, _ = pieces(load(src, hi - 1), False)
    emit(hi - 2, done(here, left, right, before))


def forward_kernel(u0, s0, u1, s1, u2):
    def section(base, dst):
        def emit(r, rate):
            for (f, k), x in zip(FK, rate):
                dst[r, f, k] = KEEP * base[r, f, k] + x

        return emit

    def advance(base, sec, dst, shift):
        def emit(r, rate):
            for (f, k), x in zip(FK, rate):
                dst[r - shift, f, k] = 0.5 * (
                    base[r, f, k] + (KEEP * sec[r, f, k] + x)
                )

        return emit

    rate_pass(u0, 0, TOTAL, section(u0, s0))
    rate_pass(s0, 1, TOTAL - 1, advance(u0, s0, u1, 0))
    rate_pass(u1, 2, TOTAL - 2, section(u1, s1))
    rate_pass(s1, WS - 1, WS + ROWS + 1, advance(u1, s1, u2, WS))


def beside_lanes(row):
    diff, total = [[], []], [[], []]
    for k in range(2):
        for x in row[k]:
            before, after = turn(x, 1), turn(x, -1)
            diff[k].append(after - before)
            total[k].append(after + before)
    return diff, total


def pulled(v, wm, wc, wp, diff, total, emit):
    for k in range(2):
        rho, m1, m2, m3, en = v[k]
        inv = invert(rho)
        v1, v2, v3 = m1 * inv, m2 * inv, m3 * inv
        kin = 0.5 * (v1 * v1 + v2 * v2 + v3 * v3)
        h = 1.4 * (en * inv) - 0.4 * kin
        d1, d2, d3, around = [], diff[k], [], []
        for f in range(NF):
            if k == 0:
                below, above = pltpu.roll(wc[1][f], 1, 0), wc[1][f]
            else:
                below, above = wc[0][f], pltpu.roll(wc[0][f], 7, 0)
            d1.append(wp[k][f] - wm[k][f])
            d3.append(above - below)
            around.append(((wp[k][f] + wm[k][f]) + total[k][f]) + (above + below))
        a = [v1 * d1[f] + v2 * d2[f] + v3 * d3[f] for f in range(1, NF)]
        b1, b2, b3 = [
            d[0] + v1 * d[1] + v2 * d[2] + v3 * d[3] + h * d[4] for d in (d1, d2, d3)
        ]
        pc = 0.4 * (d1[1] + d2[2] + d3[3] + a[3])
        out = [
            pc * kin - (a[0] * v1 + a[1] * v2 + a[2] * v3 + a[3] * h),
            b1 + a[0] - pc * v1,
            b2 + a[1] - pc * v2,
            b3 + a[2] - pc * v3,
            a[3] + pc,
        ]
        for f in range(NF):
            emit(f, k, out[f] + (0.2 * around[f] - 1.2 * wc[k][f]), wc[k][f])


def pull_pass(state, w, lo, hi, emit, shift=0):
    def body(r, carry):
        wp = load(w, r + 1)
        ahead = beside_lanes(wp)
        pulled(
            load(state, r - shift), load(w, r - 1), load(w, r), wp, *carry,
            lambda f, k, x, c: emit(r, f, k, x, c),
        )
        return ahead

    lax.fori_loop(lo, hi, body, beside_lanes(load(w, lo)), unroll=UNROLL)


def adjoint_kernel(
    low_lam, tile0, y, first_low, first_high, low, high, s0, u1, s1, u2,
    keep_a, keep_s, send, lam, cot, wgt, lam1,
):
    assemble_halo(lam, WS - WC, 1, 0, y, first_low, lambda j: (low, 2 * NF * j))
    assemble_halo(lam, WS + ROWS, 1, 1, y, first_high, lambda j: (high, 2 * NF * j))
    lane, core = lanes()
    first = core == 0
    mine = owned(lane, core)

    def section(r, f, k, x, w):
        c = 0.0125 * x
        cot[r, f, k] = c
        wgt[r, f, k] = 0.0125 * w + 0.025 * c

    def middle(r, f, k, x, w):
        lam1[r, f, k] = lam[r, f, k] + (cot[r, f, k] + x)

    def last(r, f, k, x, w):
        i = r - WS
        before = lam1[r, f, k]
        start = before + (cot[r, f, k] + x)
        mid, end = u1[r, f, k], u2[i, f, k]
        keep_a[i, f, k] = jnp.where(first, start, before)
        keep_s[i, f, k] = jnp.where(first, mid, end)
        away_a = jnp.where(first, before, start)
        away_s = jnp.where(first, end, mid)
        send[i, f, k] = jnp.where(mine, away_a, turn(away_s, HALF))

    pull_pass(s1, lam, 3, TOTAL - 3, section)
    pull_pass(u1, wgt, 4, TOTAL - 4, middle)
    pull_pass(s0, lam1, 5, TOTAL - 5, section)
    pull_pass(tile0, wgt, WS, WS + ROWS, last, shift=WS)


def merge_kernel(keep_a, keep_s, got, out_a, out_s):
    lane, core = lanes()
    mine = owned(lane, core)
    for f, k in FK:
        for r in range(ROWS):
            rows = pl.ds(f * 16 * ROWS + k * ROWS + r, 8, stride=2 * ROWS)
            other = got[r, f, k]
            out_a[rows, :] = jnp.where(mine, keep_a[r, f, k], other)
            out_s[rows, :] = jnp.where(mine, keep_s[r, f, k], turn(other, HALF))


def call(kernel, name, outs, scratch, *args, flops=0, aliases=None):
    shapes = [jax.ShapeDtypeStruct(s, jnp.float32) for s in outs]
    size = 4 * sum(a.size for a in args)
    return pl.pallas_call(
        kernel,
        out_shape=shapes,
        name=name,
        scratch_shapes=[pltpu.VMEM(s, jnp.float32) for s in scratch],
        input_output_aliases=aliases or {},
        compiler_params=pltpu.CompilerParams(vmem_limit_bytes=VMEM_LIMIT),
        cost_estimate=pl.CostEstimate(flops=flops, bytes_accessed=size, transcendentals=0),
    )(*args)


def rows_of(n):
    return (n, NF, 2, 8, LANES)


def ring(count, step):
    return [(i, (i + step) % count) for i in range(count)]


def shards(endpoints):
    shape = endpoints.shape
    tx, ty = lax.axis_size("tx"), lax.axis_size("ty")
    own = endpoints.reshape(-1, LANES)
    swap = [(0, 1), (1, 0)]
    up, down = ring(tx, 1), ring(tx, -1)
    tile, full = rows_of(ROWS), rows_of(TOTAL)
    block = (NF, 2, 8, LANES)

    def pack(rows):
        return (NF * rows, 8, LANES)

    edge = (NF, 8, LANES)
    got = lax.ppermute(own, "grp", swap)
    (mine,) = call(own_kernel, "own", [tile], [], own, flops=10**6)
    t0, t1, first_up, first_down = call(
        first_kernel, "first", [tile, tile, edge, edge], [], mine, got,
        flops=10**6,
    )
    first_low = lax.ppermute(first_up, "tx", up)
    first_high = lax.ppermute(first_down, "tx", down)
    side, rest_up, rest_down = call(
        rest_kernel, "rest", [block, pack(WS), pack(WS)], [], t0, t1, flops=10**6
    )
    rest_low = lax.ppermute(rest_up, "tx", up)
    rest_high = lax.ppermute(rest_down, "tx", down)
    y, up1, down1 = call(
        side_kernel, "side", [block, pack(WC), pack(WC)], [],
        side, first_low, first_high, t1, flops=10**10,
    )
    pairs = [(i, ty + (i - 1) % ty) for i in range(ty)]
    pairs += [(b, a) for a, b in pairs]
    y = lax.ppermute(y, ("grp", "ty"), pairs)
    low1 = lax.ppermute(up1, "tx", up)
    high1 = lax.ppermute(down1, "tx", down)
    u0, lam = call(
        halo_kernel, "halo", [full, full], [],
        t0, t1, y, first_low, first_high, rest_low, rest_high, flops=10**7,
    )
    s0, u1, s1, u2 = call(
        forward_kernel, "forward", [full, full, full, tile], [], u0, flops=10**9,
    )
    keep_a, keep_s, send, _ = call(
        adjoint_kernel, "adjoint", [tile, tile, tile, full], [full] * 3,
        lam, t0, y, first_low, first_high, low1, high1, s0, u1, s1, u2, flops=10**8, aliases={0: 3},
    )
    other = lax.ppermute(send, "grp", swap)
    adjoints, states = call(
        merge_kernel, "merge", [own.shape, own.shape], [], keep_a, keep_s, other
    )
    return adjoints.reshape(shape), states.reshape(shape)


def solution(mesh):
    placed = P("grp", None, None, "tx", "ty")
    return jax.shard_map(
        shards, mesh=mesh, in_specs=(placed,), out_specs=(placed, placed), check_vma=False
    )
```

time: 25.8 us -> 25.2 us (0.977)
  waiting for transfers between devices: 3.35 us -> 2.29 us
  starting transfers between devices: 12.7 us -> 13.1 us
    ppermute x1, waiting for transfers between devices: 1.07 us -> 0.01 us  [shards(): first_high = lax.ppermute(first_down, 'tx', down)]
    ppermute x1, starting transfers between devices: 1.61 us -> 1.14 us  [shards(): low1 = lax.ppermute(up1, 'tx', up)]
    ppermute x1, starting transfers between devices: 1.31 us -> 1.78 us  [shards(): high1 = lax.ppermute(down1, 'tx', down)]
    ppermute x1, starting transfers between devices: 2.29 us -> 2.7 us  [shards(): y = lax.ppermute(y, ('grp', 'ty'), pairs)]
    pallas_call x6 -> x8, Pallas kernels: 8 us -> 7.92 us  [call(): pl.pallas_call(kernel, out_shape=shapes, name=name, scratch_shapes=[pltpu...]
  transfers between devices with their start and end apart: 9 -> 9, of which waited for: 4 -> 4; matrix products, arithmetic and copies ran while one was open for 0% -> 0% of each run, Pallas kernels for 14% -> 15%
where the time goes in v3:
time: 25.2 us; the launch traced here: 25 us
  starting transfers between devices  13.1 us (52%)
  Pallas kernels  7.92 us (31%)
  waiting for transfers between devices  2.29 us (9%)
  local copies, waits for them, and re-layouts  0.97 us (4%)
  between operations  0.69 us (3%)
    pallas_call x8, Pallas kernels, call(): pl.pallas_call(kernel, out_shape=shapes, name=name, scratch_shapes=[pltpu...  7.92 us
    ppermute x1, starting transfers between devices, shards(): first_low = lax.ppermute(first_up, 'tx', up)  2.91 us
    ppermute x1, starting transfers between devices, shards(): y = lax.ppermute(y, ('grp', 'ty'), pairs)  2.7 us
    ppermute x1, starting transfers between devices, shards(): rest_high = lax.ppermute(rest_down, 'tx', down)  1.92 us
    ppermute x1, starting transfers between devices, shards(): high1 = lax.ppermute(down1, 'tx', down)  1.78 us
    ppermute x1, waiting for transfers between devices, shards(): other = lax.ppermute(send, 'grp', swap)  1.62 us
    ppermute x1, starting transfers between devices, shards(): low1 = lax.ppermute(up1, 'tx', up)  1.14 us
    ppermute x1, starting transfers between devices, shards(): rest_low = lax.ppermute(rest_up, 'tx', up)  1.06 us
  transfers between devices with their start and end apart: 9, of which 4 were waited for; matrix products, arithmetic and copies ran while one was open for 0% of the time, Pallas kernels for 15%

profile of v3, /device:TPU:0, one launch (start us, length us, event | category | flops | bytes accessed | tf_op | source)
XLA Modules:
  0.0 25.0 jit_solution(13649001645406341344)
XLA Ops:
  0.6 0.5 %collective-permute-start = (f32[640,128]{1,0:T(8,128)}, f32[640,128]{1,0:T(8,128)S(1)}, u32[]{:S(2)}, u32[]{:S(2)}) collective-permute-start(f32[640,128]{1,0:T(8,128)} %bitcast.3), channel_id=1, source_target_pairs={{0,16},{16,0},{1,17},{17,1},{2,18},{18,2},{3,19},{19,3},{4,20},{20... | collective-permute-start | bytes 983048 | tf_op jit(solution)/shard_map/ppermute | solution.py:410
  1.1 1.0 %copy-done = f32[1,5,16,8,128]{4,3,2,1,0:T(8,128)S(1)} copy-done((f32[1,5,16,8,128]{4,3,2,1,0:T(8,128)S(1)}, f32[1,5,16,8,128]{4,3,2,1,0:T(8,128)}, u32[]{:S(2)}) %copy-start) | copy-done | bytes 327704
  2.1 0.1 own.1
  2.2 0.4 %collective-permute-done.got = f32[640,128]{1,0:T(8,128)S(1)} collective-permute-done((f32[640,128]{1,0:T(8,128)}, f32[640,128]{1,0:T(8,128)S(1)}, u32[]{:S(2)}, u32[]{:S(2)}) %collective-permute-start) | collective-permute-done | bytes 327712 | tf_op jit(solution)/shard_map/ppermute | solution.py:410
  2.6 0.3 %first.1 = (f32[8,5,2,8,128]{4,3,2,1,0:T(8,128)S(1)}, f32[8,5,2,8,128]{4,3,2,1,0:T(8,128)S(1)}, f32[5,8,128]{2,1,0:T(8,128)S(1)}, f32[5,8,128]{2,1,0:T(8,128)S(1)}) custom-call(f32[8,5,2,8,128]{4,3,2,1,0:T(8,128)S(1)} %own.1, f32[640,128]{1,0:T(8,128)S(1)} %collective-permute-done.got), custom_call_target="tpu_custom_call" | custom-call | flops 1000000 | bytes 655360 | tf_op jit(solution)/shard_map/first/pallas_call | solution.py:378
  2.9 2.9 %collective-permute-start.1 = (f32[5,8,128]{2,1,0:T(8,128)S(1)}, f32[5,8,128]{2,1,0:T(8,128)S(1)}, u32[]{:S(2)}, u32[]{:S(2)}) collective-permute-start(f32[5,8,128]{2,1,0:T(8,128)S(1)} %get-tuple-element.26), channel_id=1, source_target_pairs={{0,4},{4,8},{8,12},{12,0},{1,5},{5,9},{9,13},{13,1},{2,6},{6,10},{... | collective-permute-start | bytes 61448 | tf_op jit(solution)/shard_map/ppermute | solution.py:416
  5.8 1.0 %collective-permute-start.2 = (f32[5,8,128]{2,1,0:T(8,128)S(1)}, f32[5,8,128]{2,1,0:T(8,128)S(1)}, u32[]{:S(2)}, u32[]{:S(2)}) collective-permute-start(f32[5,8,128]{2,1,0:T(8,128)S(1)} %get-tuple-element.27), channel_id=1, source_target_pairs={{0,12},{4,0},{8,4},{12,8},{1,13},{5,1},{9,5},{13,9},{2,14},{6,2},{... | collective-permute-start | bytes 61448 | tf_op jit(solution)/shard_map/ppermute | solution.py:417
  6.8 0.3 %rest.1 = (f32[5,2,8,128]{3,2,1,0:T(8,128)S(1)}, f32[30,8,128]{2,1,0:T(8,128)S(1)}, f32[30,8,128]{2,1,0:T(8,128)S(1)}) custom-call(f32[8,5,2,8,128]{4,3,2,1,0:T(8,128)S(1)} %get-tuple-element.23.t0.tile0, f32[8,5,2,8,128]{4,3,2,1,0:T(8,128)S(1)} %get-tuple-element.24.t1), custom_call_target="tpu_custom_call" | custom-call | flops 1000000 | bytes 655360 | tf_op jit(solution)/shard_map/rest/pallas_call | solution.py:378
  7.1 1.1 %collective-permute-start.4 = (f32[30,8,128]{2,1,0:T(8,128)S(1)}, f32[30,8,128]{2,1,0:T(8,128)S(1)}, u32[]{:S(2)}, u32[]{:S(2)}) collective-permute-start(f32[30,8,128]{2,1,0:T(8,128)S(1)} %get-tuple-element.29), channel_id=1, source_target_pairs={{0,4},{4,8},{8,12},{12,0},{1,5},{5,9},{9,13},{13,1},{2,6},{6,10},{... | collective-permute-start | bytes 368648 | tf_op jit(solution)/shard_map/ppermute | solution.py:421
  8.2 1.9 %collective-permute-start.5 = (f32[30,8,128]{2,1,0:T(8,128)S(1)}, f32[30,8,128]{2,1,0:T(8,128)S(1)}, u32[]{:S(2)}, u32[]{:S(2)}) collective-permute-start(f32[30,8,128]{2,1,0:T(8,128)S(1)} %get-tuple-element.30), channel_id=1, source_target_pairs={{0,12},{4,0},{8,4},{12,8},{1,13},{5,1},{9,5},{13,9},{2,14},{6,2},{... | collective-permute-start | bytes 368648 | tf_op jit(solution)/shard_map/ppermute | solution.py:422
  10.1 0.0 collective-permute-done.1.low.first_low
  10.1 0.1 side.1
  10.2 2.7 %collective-permute-start.3 = (f32[5,2,8,128]{3,2,1,0:T(8,128)S(1)}, f32[5,2,8,128]{3,2,1,0:T(8,128)S(1)}, u32[]{:S(2)}, u32[]{:S(2)}) collective-permute-start(f32[5,2,8,128]{3,2,1,0:T(8,128)S(1)} %get-tuple-element.28), channel_id=1, source_target_pairs={{0,19},{1,16},{2,17},{3,18},{19,0},{16,1},{17,2},{18,3},{4,23},{5,... | collective-permute-start | bytes 122888 | tf_op jit(solution)/shard_map/ppermute | solution.py:429
  12.9 1.1 %collective-permute-start.6 = (f32[20,8,128]{2,1,0:T(8,128)S(1)}, f32[20,8,128]{2,1,0:T(8,128)S(1)}, u32[]{:S(2)}, u32[]{:S(2)}) collective-permute-start(f32[20,8,128]{2,1,0:T(8,128)S(1)} %get-tuple-element.32), channel_id=1, source_target_pairs={{0,4},{4,8},{8,12},{12,0},{1,5},{5,9},{9,13},{13,1},{2,6},{6,10},{... | collective-permute-start | bytes 245768 | tf_op jit(solution)/shard_map/ppermute | solution.py:430
  14.1 1.8 %collective-permute-start.7 = (f32[20,8,128]{2,1,0:T(8,128)S(1)}, f32[20,8,128]{2,1,0:T(8,128)S(1)}, u32[]{:S(2)}, u32[]{:S(2)}) collective-permute-start(f32[20,8,128]{2,1,0:T(8,128)S(1)} %get-tuple-element.33), channel_id=1, source_target_pairs={{0,12},{4,0},{8,4},{12,8},{1,13},{5,1},{9,5},{13,9},{2,14},{6,2},{... | collective-permute-start | bytes 245768 | tf_op jit(solution)/shard_map/ppermute | solution.py:431
  15.8 0.1 collective-permute-done.5.rest_high
  16.0 0.5 %halo.1 = (f32[20,5,2,8,128]{4,3,2,1,0:T(8,128)S(1)}, f32[20,5,2,8,128]{4,3,2,1,0:T(8,128)S(1)}) custom-call(f32[8,5,2,8,128]{4,3,2,1,0:T(8,128)S(1)} %get-tuple-element.23.t0.tile0, f32[8,5,2,8,128]{4,3,2,1,0:T(8,128)S(1)} %get-tuple-element.24.t1, f32[5,2,8,128]{3,2,1,0:T(8,128)S(1)} %collective-permute-done.3.y, ...), custom_call_target="tpu_custom_call" | custom-call | flops 10000000 | bytes 983040 | tf_op jit(solution)/shard_map/halo/pallas_call | solution.py:378
  16.5 2.8 %forward.1 = (f32[20,5,2,8,128]{4,3,2,1,0:T(8,128)S(1)}, f32[20,5,2,8,128]{4,3,2,1,0:T(8,128)S(1)}, f32[20,5,2,8,128]{4,3,2,1,0:T(8,128)S(1)}, f32[8,5,2,8,128]{4,3,2,1,0:T(8,128)S(1)}) custom-call(f32[20,5,2,8,128]{4,3,2,1,0:T(8,128)S(1)} %get-tuple-element.34.u0), custom_call_target="tpu_custom_call" | custom-call | flops 1000000000 | bytes 819200 | tf_op jit(solution)/shard_map/forward/pallas_call | solution.py:378
  19.3 0.0 collective-permute-done.6.low
  19.3 0.2 collective-permute-done.7.high
  19.5 2.8 %adjoint.1 = (f32[8,5,2,8,128]{4,3,2,1,0:T(8,128)S(1)}, f32[8,5,2,8,128]{4,3,2,1,0:T(8,128)S(1)}, f32[8,5,2,8,128]{4,3,2,1,0:T(8,128)S(1)}, f32[20,5,2,8,128]{4,3,2,1,0:T(8,128)S(1)}) custom-call(f32[20,5,2,8,128]{4,3,2,1,0:T(8,128)S(1)} %get-tuple-element.31.low_lam, ...), custom_call_target="tpu_custom_call", output_to_operand_aliasing={{3}: (0, {})} | custom-call | flops 100000000 | bytes 4177920 | tf_op jit(solution)/shard_map/adjoint/pallas_call | solution.py:378
  22.3 0.1 collective-permute-start.8
  22.4 1.6 %collective-permute-done.8.got = f32[8,5,2,8,128]{4,3,2,1,0:T(8,128)S(1)} collective-permute-done((f32[8,5,2,8,128]{4,3,2,1,0:T(8,128)S(1)}, f32[8,5,2,8,128]{4,3,2,1,0:T(8,128)S(1)}, u32[]{:S(2)}, u32[]{:S(2)}) %collective-permute-start.8) | collective-permute-done | bytes 327712 | tf_op jit(solution)/shard_map/ppermute | solution.py:443
  24.0 1.0 %merge.1 = (f32[640,128]{1,0:T(8,128)}, f32[640,128]{1,0:T(8,128)}) custom-call(f32[8,5,2,8,128]{4,3,2,1,0:T(8,128)S(1)} %get-tuple-element.39.keep_a, f32[8,5,2,8,128]{4,3,2,1,0:T(8,128)S(1)} %get-tuple-element.40.keep_s, f32[8,5,2,8,128]{4,3,2,1,0:T(8,128)S(1)} %collective-permute-done.8.got), custom_call_target="tpu_custom_call" | custom-call | bytes 983040 | tf_op jit(solution)/shard_map/merge/pallas_call | solution.py:378
  (4 shorter events, 0.0 us)
Async XLA Ops:
  0.6 2.0 %collective-permute-start = (f32[640,128]{1,0:T(8,128)}, f32[640,128]{1,0:T(8,128)S(1)}, u32[]{:S(2)}, u32[]{:S(2)}) collective-permute-start(f32[640,128]{1,0:T(8,128)} %bitcast.3), channel_id=1, source_target_pairs={{0,16},{16,0},{1,17},{17,1},{2,18},{18,2},{3,19},{19,3},{4,20},{20... | collective-permute-start | bytes 983048 | tf_op jit(solution)/shard_map/ppermute | solution.py:410
  1.1 1.0 %copy-start = (f32[1,5,16,8,128]{4,3,2,1,0:T(8,128)S(1)}, f32[1,5,16,8,128]{4,3,2,1,0:T(8,128)}, u32[]{:S(2)}) copy-start(f32[1,5,16,8,128]{4,3,2,1,0:T(8,128)} %param.1) | copy-start | bytes 983044
  2.9 7.2 %collective-permute-start.1 = (f32[5,8,128]{2,1,0:T(8,128)S(1)}, f32[5,8,128]{2,1,0:T(8,128)S(1)}, u32[]{:S(2)}, u32[]{:S(2)}) collective-permute-start(f32[5,8,128]{2,1,0:T(8,128)S(1)} %get-tuple-element.26), channel_id=1, source_target_pairs={{0,4},{4,8},{8,12},{12,0},{1,5},{5,9},{9,13},{13,1},{2,6},{6,10},{... | collective-permute-start | bytes 61448 | tf_op jit(solution)/shard_map/ppermute | solution.py:416
  5.8 4.3 %collective-permute-start.2 = (f32[5,8,128]{2,1,0:T(8,128)S(1)}, f32[5,8,128]{2,1,0:T(8,128)S(1)}, u32[]{:S(2)}, u32[]{:S(2)}) collective-permute-start(f32[5,8,128]{2,1,0:T(8,128)S(1)} %get-tuple-element.27), channel_id=1, source_target_pairs={{0,12},{4,0},{8,4},{12,8},{1,13},{5,1},{9,5},{13,9},{2,14},{6,2},{... | collective-permute-start | bytes 61448 | tf_op jit(solution)/shard_map/ppermute | solution.py:417
  7.1 8.7 %collective-permute-start.4 = (f32[30,8,128]{2,1,0:T(8,128)S(1)}, f32[30,8,128]{2,1,0:T(8,128)S(1)}, u32[]{:S(2)}, u32[]{:S(2)}) collective-permute-start(f32[30,8,128]{2,1,0:T(8,128)S(1)} %get-tuple-element.29), channel_id=1, source_target_pairs={{0,4},{4,8},{8,12},{12,0},{1,5},{5,9},{9,13},{13,1},{2,6},{6,10},{... | collective-permute-start | bytes 368648 | tf_op jit(solution)/shard_map/ppermute | solution.py:421
  8.2 7.8 %collective-permute-start.5 = (f32[30,8,128]{2,1,0:T(8,128)S(1)}, f32[30,8,128]{2,1,0:T(8,128)S(1)}, u32[]{:S(2)}, u32[]{:S(2)}) collective-permute-start(f32[30,8,128]{2,1,0:T(8,128)S(1)} %get-tuple-element.30), channel_id=1, source_target_pairs={{0,12},{4,0},{8,4},{12,8},{1,13},{5,1},{9,5},{13,9},{2,14},{6,2},{... | collective-permute-start | bytes 368648 | tf_op jit(solution)/shard_map/ppermute | solution.py:422
  10.2 5.6 %collective-permute-start.3 = (f32[5,2,8,128]{3,2,1,0:T(8,128)S(1)}, f32[5,2,8,128]{3,2,1,0:T(8,128)S(1)}, u32[]{:S(2)}, u32[]{:S(2)}) collective-permute-start(f32[5,2,8,128]{3,2,1,0:T(8,128)S(1)} %get-tuple-element.28), channel_id=1, source_target_pairs={{0,19},{1,16},{2,17},{3,18},{19,0},{16,1},{17,2},{18,3},{4,23},{5,... | collective-permute-start | bytes 122888 | tf_op jit(solution)/shard_map/ppermute | solution.py:429
  12.9 6.4 %collective-permute-start.6 = (f32[20,8,128]{2,1,0:T(8,128)S(1)}, f32[20,8,128]{2,1,0:T(8,128)S(1)}, u32[]{:S(2)}, u32[]{:S(2)}) collective-permute-start(f32[20,8,128]{2,1,0:T(8,128)S(1)} %get-tuple-element.32), channel_id=1, source_target_pairs={{0,4},{4,8},{8,12},{12,0},{1,5},{5,9},{9,13},{13,1},{2,6},{6,10},{... | collective-permute-start | bytes 245768 | tf_op jit(solution)/shard_map/ppermute | solution.py:430
  14.1 5.4 %collective-permute-start.7 = (f32[20,8,128]{2,1,0:T(8,128)S(1)}, f32[20,8,128]{2,1,0:T(8,128)S(1)}, u32[]{:S(2)}, u32[]{:S(2)}) collective-permute-start(f32[20,8,128]{2,1,0:T(8,128)S(1)} %get-tuple-element.33), channel_id=1, source_target_pairs={{0,12},{4,0},{8,4},{12,8},{1,13},{5,1},{9,5},{13,9},{2,14},{6,2},{... | collective-permute-start | bytes 245768 | tf_op jit(solution)/shard_map/ppermute | solution.py:431
  22.3 1.7 %collective-permute-start.8 = (f32[8,5,2,8,128]{4,3,2,1,0:T(8,128)S(1)}, f32[8,5,2,8,128]{4,3,2,1,0:T(8,128)S(1)}, u32[]{:S(2)}, u32[]{:S(2)}) collective-permute-start(f32[8,5,2,8,128]{4,3,2,1,0:T(8,128)S(1)} %get-tuple-element.41), channel_id=1, source_target_pairs={{0,16},{16,0},{1,17},{17,1},{2,18},{18,2},{3,19},{19,3},{4,20},{20... | collective-permute-start | bytes 983048 | tf_op jit(solution)/shard_map/ppermute | solution.py:443

commit v4 on v3

--- a/solution.py
+++ b/solution.py
@@ -15,7 +15,8 @@
 TOTAL = ROWS + 2 * WS
 FK = [(f, k) for f in range(NF) for k in range(2)]
 VMEM_LIMIT = 32 * 2**20
-UNROLL = 4
+TURNS = (18, 16, 14, 8)
+BACK = (14, 12, 10, 8)
 UP1 = WS * NF
 CORNER = WS * (WS - 1) // 2 + WC * (WC - 1) // 2
 
@@ -101,6 +102,8 @@
     for f in range(NF):
         first_up[f] = edges[0][f]
         first_down[f] = edges[1][f]
+    pack_rows(t1, first_up, ROWS - WC, WC // 2, (0,), NF, lane, core)
+    pack_rows(t1, first_down, 0, WC // 2, (0,), NF, lane, core)
 
 
 def rest_kernel(t0, t1, side, rest_up, rest_down):
@@ -131,24 +134,31 @@
                 (place >= HALF) & (place < HALF + CORNER), high[f], side[f, k]
             )
             y[f, k] = jnp.where(place < CORNER, low[f], with_high)
-    pack_rows(t1, up1, ROWS - WC, WC // 2, (0, 1), 0, lane, core)
-    pack_rows(t1, down1, 0, WC // 2, (0, 1), 0, lane, core)
+    pack_rows(t1, up1, ROWS - WC, WC // 2, (1,), 0, lane, core)
+    pack_rows(t1, down1, 0, WC // 2, (1,), 0, lane, core)
+
+
+def units(which):
+    return [0.5 / u for u in UNIT] if which else UNIT
 
 
 def assemble_tile(dst, offset, which, tile, y):
     lane, core = lanes()
     width = WC if which else WS
+    unit = units(which)
     for r in range(ROWS):
         outer = ((lane + width * (1 - core)) & (LANES - 1)) < width
         for f, k in FK:
             shift = LANES - width + width * core - tile_lane(which, r) - 32 * k
-            dst[offset + r, f, k] = jnp.where(outer, turn(y[f, k], shift), tile[r, f, k])
+            v = jnp.where(outer, turn(y[f, k], shift), tile[r, f, k])
+            dst[offset + r, f, k] = v * unit[f]
 
 
 def assemble_halo(dst, offset, which, d, y, edges, packed):
     lane, core = lanes()
     mine = owned(lane, core)
     width = WC if which else WS
+    unit = units(which)
     n = width // 2
     for away in range(width):
         w, at = corner(which)[away]
@@ -165,7 +175,7 @@
                 o = turn(y[f, k], LANES - w + w * core - HALF * d - at - 32 * k)
                 i = turn(edges[f], HALF * d - at - 32 * k - w * core)
                 v = jnp.where(inner, i, jnp.where(outer, o, v))
-            dst[offset + j, f, k] = v
+            dst[offset + j, f, k] = v * unit[f]
 
 
 def halo_kernel(t0, t1, y, first_low, first_high, rest_low, rest_high, u0, lam):
@@ -184,20 +194,23 @@
 
 
 STEP = 0.025
+UNIT = (1.0, STEP, STEP, STEP, STEP * STEP)
+VISC = 0.2 * STEP
+KEEP = 1.0 - 6.0 * VISC
 
 
 def fluxes(v):
     rho, m1, m2, m3, en = v
-    inv = STEP * invert(rho)
+    inv = invert(rho)
     v1, v2, v3 = m1 * inv, m2 * inv, m3 * inv
     a, b, c = m1 * v1, m2 * v2, m3 * v3
-    p = (0.4 * STEP) * en - 0.2 * (a + b + c)
-    h = en + (1.0 / STEP) * p
+    p = 0.4 * en - 0.2 * (a + b + c)
+    h = en + p
     m12, m13, m23 = m1 * v2, m1 * v3, m2 * v3
     return (
-        (STEP * m1, a + p, m12, m13, h * v1),
-        (STEP * m2, m12, b + p, m23, h * v2),
-        (STEP * m3, m13, m23, c + p, h * v3),
+        (m1, a + p, m12, m13, h * v1),
+        (m2, m12, b + p, m23, h * v2),
+        (m3, m13, m23, c + p, h * v3),
     )
 
 
@@ -205,7 +218,7 @@
     before, after, here, left, right = [], [], [], [], []
     fl = [fluxes(v[k]) for k in range(2)]
     for f in range(NF):
-        s = [(0.2 * STEP) * v[k][f] for k in range(2)]
+        s = [VISC * v[k][f] for k in range(2)]
         before += [s[k] - fl[k][0][f] for k in range(2)]
         after += [s[k] + fl[k][0][f] for k in range(2)]
         if along_y:
@@ -220,13 +233,9 @@
     return before, after, here, left, right
 
 
-KEEP = 1.0 - 1.2 * STEP
-
-
-def rate_pass(src, lo, hi, emit):
-    _, edge, _, _, _ = pieces(load(src, lo), False)
-    _, after, here, left, right = pieces(load(src, lo + 1))
-    here = [a + b for a, b in zip(here, edge)]
+def rate_pass(src, lo, hi, emit, unroll):
+    _, after, _, _, _ = pieces(load(src, lo), False)
+    zero = [jnp.zeros((8, LANES), jnp.float32) for _ in FK]
 
     def done(here, left, right, before):
         return [
@@ -242,7 +251,7 @@
         return here2, after2, left2, right2
 
     here, _, left, right = lax.fori_loop(
-        lo + 2, hi - 1, body, (here, after, left, right), unroll=UNROLL
+        lo + 1, hi - 1, body, (zero, after, zero, zero), unroll=unroll
     )
     before, _, _, _, _ = pieces(load(src, hi - 1), False)
     emit(hi - 2, done(here, left, right, before))
@@ -265,10 +274,10 @@
 
         return emit
 
-    rate_pass(u0, 0, TOTAL, section(u0, s0))
-    rate_pass(s0, 1, TOTAL - 1, advance(u0, s0, u1, 0))
-    rate_pass(u1, 2, TOTAL - 2, section(u1, s1))
-    rate_pass(s1, WS - 1, WS + ROWS + 1, advance(u1, s1, u2, WS))
+    rate_pass(u0, 0, TOTAL, section(u0, s0), TURNS[0])
+    rate_pass(s0, 1, TOTAL - 1, advance(u0, s0, u1, 0), TURNS[1])
+    rate_pass(u1, 2, TOTAL - 2, section(u1, s1), TURNS[2])
+    rate_pass(s1, WS - 1, WS + ROWS + 1, advance(u1, s1, u2, WS - 1), TURNS[3])
 
 
 def beside_lanes(row):
@@ -310,55 +319,54 @@
             a[3] + pc,
         ]
         for f in range(NF):
-            emit(f, k, out[f] + (0.2 * around[f] - 1.2 * wc[k][f]), wc[k][f])
-
-
-def pull_pass(state, w, lo, hi, emit, shift=0):
+            emit(f, k, out[f] + (VISC * around[f] - (6.0 * VISC) * wc[k][f]), wc[k][f])
+
+
+def pull_pass(state, w, lo, hi, emit, unroll):
     def body(r, carry):
         wp = load(w, r + 1)
         ahead = beside_lanes(wp)
         pulled(
-            load(state, r - shift), load(w, r - 1), load(w, r), wp, *carry,
+            load(state, r), load(w, r - 1), load(w, r), wp, *carry,
             lambda f, k, x, c: emit(r, f, k, x, c),
         )
         return ahead
 
-    lax.fori_loop(lo, hi, body, beside_lanes(load(w, lo)), unroll=UNROLL)
+    lax.fori_loop(lo, hi, body, beside_lanes(load(w, lo)), unroll=unroll)
 
 
 def adjoint_kernel(
-    low_lam, tile0, y, first_low, first_high, low, high, s0, u1, s1, u2,
+    low_lam, u0, y, first_low, first_high, low, high, s0, u1, s1, u2,
     keep_a, keep_s, send, lam, cot, wgt, lam1,
 ):
-    assemble_halo(lam, WS - WC, 1, 0, y, first_low, lambda j: (low, 2 * NF * j))
-    assemble_halo(lam, WS + ROWS, 1, 1, y, first_high, lambda j: (high, 2 * NF * j))
+    assemble_halo(lam, WS - WC, 1, 0, y, first_low, lambda j: (low, 0) if j else (first_low, NF))
+    assemble_halo(lam, WS + ROWS, 1, 1, y, first_high, lambda j: (high, 0) if j else (first_high, NF))
     lane, core = lanes()
     first = core == 0
     mine = owned(lane, core)
 
     def section(r, f, k, x, w):
-        c = 0.0125 * x
-        cot[r, f, k] = c
-        wgt[r, f, k] = 0.0125 * w + 0.025 * c
+        cot[r, f, k] = x
+        wgt[r, f, k] = w + x
 
     def middle(r, f, k, x, w):
-        lam1[r, f, k] = lam[r, f, k] + (cot[r, f, k] + x)
+        lam1[r, f, k] = lam[r, f, k] + 0.5 * (cot[r, f, k] + x)
 
     def last(r, f, k, x, w):
         i = r - WS
         before = lam1[r, f, k]
-        start = before + (cot[r, f, k] + x)
-        mid, end = u1[r, f, k], u2[i, f, k]
+        start = before + 0.5 * (cot[r, f, k] + x)
+        mid, end = u1[r, f, k], u2[i + 1, f, k]
         keep_a[i, f, k] = jnp.where(first, start, before)
         keep_s[i, f, k] = jnp.where(first, mid, end)
         away_a = jnp.where(first, before, start)
         away_s = jnp.where(first, end, mid)
         send[i, f, k] = jnp.where(mine, away_a, turn(away_s, HALF))
 
-    pull_pass(s1, lam, 3, TOTAL - 3, section)
-    pull_pass(u1, wgt, 4, TOTAL - 4, middle)
-    pull_pass(s0, lam1, 5, TOTAL - 5, section)
-    pull_pass(tile0, wgt, WS, WS + ROWS, last, shift=WS)
+    pull_pass(s1, lam, 3, TOTAL - 3, section, BACK[0])
+    pull_pass(u1, wgt, 4, TOTAL - 4, middle, BACK[1])
+    pull_pass(s0, lam1, 5, TOTAL - 5, section, BACK[2])
+    pull_pass(u0, wgt, WS, WS + ROWS, last, BACK[3])
 
 
 def merge_kernel(keep_a, keep_s, got, out_a, out_s):
@@ -368,8 +376,9 @@
         for r in range(ROWS):
             rows = pl.ds(f * 16 * ROWS + k * ROWS + r, 8, stride=2 * ROWS)
             other = got[r, f, k]
-            out_a[rows, :] = jnp.where(mine, keep_a[r, f, k], other)
-            out_s[rows, :] = jnp.where(mine, keep_s[r, f, k], turn(other, HALF))
+            out_a[rows, :] = jnp.where(mine, keep_a[r, f, k], other) * (2.0 * UNIT[f])
+            there = jnp.where(mine, keep_s[r, f, k], turn(other, HALF))
+            out_s[rows, :] = there * (1.0 / UNIT[f])
 
 
 def call(kernel, name, outs, scratch, *args, flops=0, aliases=None):
@@ -406,7 +415,7 @@
     def pack(rows):
         return (NF * rows, 8, LANES)
 
-    edge = (NF, 8, LANES)
+    edge = (3 * NF, 8, LANES)
     got = lax.ppermute(own, "grp", swap)
     (mine,) = call(own_kernel, "own", [tile], [], own, flops=10**6)
     t0, t1, first_up, first_down = call(
@@ -421,7 +430,7 @@
     rest_low = lax.ppermute(rest_up, "tx", up)
     rest_high = lax.ppermute(rest_down, "tx", down)
     y, up1, down1 = call(
-        side_kernel, "side", [block, pack(WC), pack(WC)], [],
+        side_kernel, "side", [block, pack(WC - 2), pack(WC - 2)], [],
         side, first_low, first_high, t1, flops=10**10,
     )
     pairs = [(i, ty + (i - 1) % ty) for i in range(ty)]
@@ -434,11 +443,12 @@
         t0, t1, y, first_low, first_high, rest_low, rest_high, flops=10**7,
     )
     s0, u1, s1, u2 = call(
-        forward_kernel, "forward", [full, full, full, tile], [], u0, flops=10**9,
+        forward_kernel, "forward", [full, full, full, rows_of(ROWS + 1)], [], u0,
+        flops=10**9,
     )
     keep_a, keep_s, send, _ = call(
         adjoint_kernel, "adjoint", [tile, tile, tile, full], [full] * 3,
-        lam, t0, y, first_low, first_high, low1, high1, s0, u1, s1, u2, flops=10**8, aliases={0: 3},
+        lam, u0, y, first_low, first_high, low1, high1, s0, u1, s1, u2, flops=10**8, aliases={0: 3},
     )
     other = lax.ppermute(send, "grp", swap)
     adjoints, states = call(

time: 25.2 us -> 23.8 us (0.944)
  Pallas kernels: 7.92 us -> 6.49 us
  waiting for transfers between devices: 2.29 us -> 2.61 us
    pallas_call x8, Pallas kernels: 7.92 us -> 6.49 us  [call(): pl.pallas_call(kernel, out_shape=shapes, name=name, scratch_shapes=[pltpu...]
    ppermute x1, waiting for transfers between devices: 0.01 us -> 0.53 us  [shards(): first_high = lax.ppermute(first_down, 'tx', down)]
    ppermute x1, starting transfers between devices: 1.14 us -> 1.61 us  [shards(): low1 = lax.ppermute(up1, 'tx', up)]
    ppermute x1, starting transfers between devices: 1.78 us -> 1.31 us  [shards(): high1 = lax.ppermute(down1, 'tx', down)]
  transfers between devices with their start and end apart: 9 -> 9, of which waited for: 4 -> 3; matrix products, arithmetic and copies ran while one was open for 0% -> 0% of each run, Pallas kernels for 15% -> 13%
where the time goes in v4:
time: 23.8 us; the launch traced here: 23.7 us
  starting transfers between devices  12.9 us (54%)
  Pallas kernels  6.49 us (27%)
  waiting for transfers between devices  2.61 us (11%)
  local copies, waits for them, and re-layouts  0.97 us (4%)
  between operations  0.69 us (3%)
    pallas_call x8, Pallas kernels, call(): pl.pallas_call(kernel, out_shape=shapes, name=name, scratch_shapes=[pltpu...  6.49 us
    ppermute x1, starting transfers between devices, shards(): first_low = lax.ppermute(first_up, 'tx', up)  2.91 us
    ppermute x1, starting transfers between devices, shards(): y = lax.ppermute(y, ('grp', 'ty'), pairs)  2.49 us
    ppermute x1, starting transfers between devices, shards(): rest_high = lax.ppermute(rest_down, 'tx', down)  1.92 us
    ppermute x1, waiting for transfers between devices, shards(): other = lax.ppermute(send, 'grp', swap)  1.62 us
    ppermute x1, starting transfers between devices, shards(): low1 = lax.ppermute(up1, 'tx', up)  1.61 us
    ppermute x1, starting transfers between devices, shards(): high1 = lax.ppermute(down1, 'tx', down)  1.31 us
    ppermute x1, starting transfers between devices, shards(): rest_low = lax.ppermute(rest_up, 'tx', up)  1.06 us
  transfers between devices with their start and end apart: 9, of which 3 were waited for; matrix products, arithmetic and copies ran while one was open for 0% of the time, Pallas kernels for 13%

profile of v4, /device:TPU:0, one launch (start us, length us, event | category | flops | bytes accessed | tf_op | source)
XLA Modules:
  0.0 23.7 jit_solution(10407833459060550691)
XLA Ops:
  0.6 0.5 %collective-permute-start = (f32[640,128]{1,0:T(8,128)}, f32[640,128]{1,0:T(8,128)S(1)}, u32[]{:S(2)}, u32[]{:S(2)}) collective-permute-start(f32[640,128]{1,0:T(8,128)} %bitcast.3), channel_id=1, source_target_pairs={{0,16},{16,0},{1,17},{17,1},{2,18},{18,2},{3,19},{19,3},{4,20},{20... | collective-permute-start | bytes 983048 | tf_op jit(solution)/shard_map/ppermute | solution.py:419
  1.1 1.0 %copy-done = f32[1,5,16,8,128]{4,3,2,1,0:T(8,128)S(1)} copy-done((f32[1,5,16,8,128]{4,3,2,1,0:T(8,128)S(1)}, f32[1,5,16,8,128]{4,3,2,1,0:T(8,128)}, u32[]{:S(2)}) %copy-start) | copy-done | bytes 327704
  2.1 0.1 own.1
  2.2 0.4 %collective-permute-done.got = f32[640,128]{1,0:T(8,128)S(1)} collective-permute-done((f32[640,128]{1,0:T(8,128)}, f32[640,128]{1,0:T(8,128)S(1)}, u32[]{:S(2)}, u32[]{:S(2)}) %collective-permute-start) | collective-permute-done | bytes 327712 | tf_op jit(solution)/shard_map/ppermute | solution.py:419
  2.6 0.3 %first.1 = (f32[8,5,2,8,128]{4,3,2,1,0:T(8,128)S(1)}, f32[8,5,2,8,128]{4,3,2,1,0:T(8,128)S(1)}, f32[15,8,128]{2,1,0:T(8,128)S(1)}, f32[15,8,128]{2,1,0:T(8,128)S(1)}) custom-call(f32[8,5,2,8,128]{4,3,2,1,0:T(8,128)S(1)} %own.1, f32[640,128]{1,0:T(8,128)S(1)} %collective-permute-done.got), custom_call_target="tpu_custom_call" | custom-call | flops 1000000 | bytes 655360 | tf_op jit(solution)/shard_map/first/pallas_call | solution.py:387
  2.9 2.9 %collective-permute-start.1 = (f32[15,8,128]{2,1,0:T(8,128)S(1)}, f32[15,8,128]{2,1,0:T(8,128)S(1)}, u32[]{:S(2)}, u32[]{:S(2)}) collective-permute-start(f32[15,8,128]{2,1,0:T(8,128)S(1)} %get-tuple-element.26), channel_id=1, source_target_pairs={{0,4},{4,8},{8,12},{12,0},{1,5},{5,9},{9,13},{13,1},{2,6},{6,10},{... | collective-permute-start | bytes 184328 | tf_op jit(solution)/shard_map/ppermute | solution.py:425
  5.8 1.0 %collective-permute-start.2 = (f32[15,8,128]{2,1,0:T(8,128)S(1)}, f32[15,8,128]{2,1,0:T(8,128)S(1)}, u32[]{:S(2)}, u32[]{:S(2)}) collective-permute-start(f32[15,8,128]{2,1,0:T(8,128)S(1)} %get-tuple-element.27), channel_id=1, source_target_pairs={{0,12},{4,0},{8,4},{12,8},{1,13},{5,1},{9,5},{13,9},{2,14},{6,2},{... | collective-permute-start | bytes 184328 | tf_op jit(solution)/shard_map/ppermute | solution.py:426
  6.8 0.3 %rest.1 = (f32[5,2,8,128]{3,2,1,0:T(8,128)S(1)}, f32[30,8,128]{2,1,0:T(8,128)S(1)}, f32[30,8,128]{2,1,0:T(8,128)S(1)}) custom-call(f32[8,5,2,8,128]{4,3,2,1,0:T(8,128)S(1)} %get-tuple-element.23.t0, f32[8,5,2,8,128]{4,3,2,1,0:T(8,128)S(1)} %get-tuple-element.24.t1), custom_call_target="tpu_custom_call" | custom-call | flops 1000000 | bytes 655360 | tf_op jit(solution)/shard_map/rest/pallas_call | solution.py:387
  7.1 1.1 %collective-permute-start.4 = (f32[30,8,128]{2,1,0:T(8,128)S(1)}, f32[30,8,128]{2,1,0:T(8,128)S(1)}, u32[]{:S(2)}, u32[]{:S(2)}) collective-permute-start(f32[30,8,128]{2,1,0:T(8,128)S(1)} %get-tuple-element.29), channel_id=1, source_target_pairs={{0,4},{4,8},{8,12},{12,0},{1,5},{5,9},{9,13},{13,1},{2,6},{6,10},{... | collective-permute-start | bytes 368648 | tf_op jit(solution)/shard_map/ppermute | solution.py:430
  8.2 1.9 %collective-permute-start.5 = (f32[30,8,128]{2,1,0:T(8,128)S(1)}, f32[30,8,128]{2,1,0:T(8,128)S(1)}, u32[]{:S(2)}, u32[]{:S(2)}) collective-permute-start(f32[30,8,128]{2,1,0:T(8,128)S(1)} %get-tuple-element.30), channel_id=1, source_target_pairs={{0,12},{4,0},{8,4},{12,8},{1,13},{5,1},{9,5},{13,9},{2,14},{6,2},{... | collective-permute-start | bytes 368648 | tf_op jit(solution)/shard_map/ppermute | solution.py:431
  10.1 0.0 collective-permute-done.1.low.first_low
  10.1 0.5 %collective-permute-done.2.high.first_high = f32[15,8,128]{2,1,0:T(8,128)S(1)} collective-permute-done((f32[15,8,128]{2,1,0:T(8,128)S(1)}, f32[15,8,128]{2,1,0:T(8,128)S(1)}, u32[]{:S(2)}, u32[]{:S(2)}) %collective-permute-start.2) | collective-permute-done | bytes 61472 | tf_op jit(solution)/shard_map/ppermute | solution.py:426
  10.6 0.1 side.1
  10.7 2.5 %collective-permute-start.3 = (f32[5,2,8,128]{3,2,1,0:T(8,128)S(1)}, f32[5,2,8,128]{3,2,1,0:T(8,128)S(1)}, u32[]{:S(2)}, u32[]{:S(2)}) collective-permute-start(f32[5,2,8,128]{3,2,1,0:T(8,128)S(1)} %get-tuple-element.28), channel_id=1, source_target_pairs={{0,19},{1,16},{2,17},{3,18},{19,0},{16,1},{17,2},{18,3},{4,23},{5,... | collective-permute-start | bytes 122888 | tf_op jit(solution)/shard_map/ppermute | solution.py:438
  13.2 1.6 %collective-permute-start.6 = (f32[10,8,128]{2,1,0:T(8,128)S(1)}, f32[10,8,128]{2,1,0:T(8,128)S(1)}, u32[]{:S(2)}, u32[]{:S(2)}) collective-permute-start(f32[10,8,128]{2,1,0:T(8,128)S(1)} %get-tuple-element.33), channel_id=1, source_target_pairs={{0,4},{4,8},{8,12},{12,0},{1,5},{5,9},{9,13},{13,1},{2,6},{6,10},{... | collective-permute-start | bytes 122888 | tf_op jit(solution)/shard_map/ppermute | solution.py:439
  14.8 1.3 %collective-permute-start.7 = (f32[10,8,128]{2,1,0:T(8,128)S(1)}, f32[10,8,128]{2,1,0:T(8,128)S(1)}, u32[]{:S(2)}, u32[]{:S(2)}) collective-permute-start(f32[10,8,128]{2,1,0:T(8,128)S(1)} %get-tuple-element.34), channel_id=1, source_target_pairs={{0,12},{4,0},{8,4},{12,8},{1,13},{5,1},{9,5},{13,9},{2,14},{6,2},{... | collective-permute-start | bytes 122888 | tf_op jit(solution)/shard_map/ppermute | solution.py:440
  16.2 0.0 collective-permute-done.3.y
  16.2 0.5 %halo.1 = (f32[20,5,2,8,128]{4,3,2,1,0:T(8,128)S(1)}, f32[20,5,2,8,128]{4,3,2,1,0:T(8,128)S(1)}) custom-call(f32[8,5,2,8,128]{4,3,2,1,0:T(8,128)S(1)} %get-tuple-element.23.t0, f32[8,5,2,8,128]{4,3,2,1,0:T(8,128)S(1)} %get-tuple-element.24.t1, f32[5,2,8,128]{3,2,1,0:T(8,128)S(1)} %collective-permute-done.3.y, ...), custom_call_target="tpu_custom_call" | custom-call | flops 10000000 | bytes 1064960 | tf_op jit(solution)/shard_map/halo/pallas_call | solution.py:387
  16.7 2.1 %forward.1 = (f32[20,5,2,8,128]{4,3,2,1,0:T(8,128)S(1)}, f32[20,5,2,8,128]{4,3,2,1,0:T(8,128)S(1)}, f32[20,5,2,8,128]{4,3,2,1,0:T(8,128)S(1)}, f32[9,5,2,8,128]{4,3,2,1,0:T(8,128)S(1)}) custom-call(f32[20,5,2,8,128]{4,3,2,1,0:T(8,128)S(1)} %get-tuple-element.32.u0), custom_call_target="tpu_custom_call" | custom-call | flops 1000000000 | bytes 819200 | tf_op jit(solution)/shard_map/forward/pallas_call | solution.py:387
  18.8 0.0 collective-permute-done.7.high
  18.8 2.2 %adjoint.1 = (f32[8,5,2,8,128]{4,3,2,1,0:T(8,128)S(1)}, f32[8,5,2,8,128]{4,3,2,1,0:T(8,128)S(1)}, f32[8,5,2,8,128]{4,3,2,1,0:T(8,128)S(1)}, f32[20,5,2,8,128]{4,3,2,1,0:T(8,128)S(1)}) custom-call(f32[20,5,2,8,128]{4,3,2,1,0:T(8,128)S(1)} %get-tuple-element.31.low_lam, ...), custom_call_target="tpu_custom_call", output_to_operand_aliasing={{3}: (0, {})} | custom-call | flops 100000000 | bytes 4710400 | tf_op jit(solution)/shard_map/adjoint/pallas_call | solution.py:387
  21.0 0.1 collective-permute-start.8
  21.1 1.6 %collective-permute-done.8.got = f32[8,5,2,8,128]{4,3,2,1,0:T(8,128)S(1)} collective-permute-done((f32[8,5,2,8,128]{4,3,2,1,0:T(8,128)S(1)}, f32[8,5,2,8,128]{4,3,2,1,0:T(8,128)S(1)}, u32[]{:S(2)}, u32[]{:S(2)}) %collective-permute-start.8) | collective-permute-done | bytes 327712 | tf_op jit(solution)/shard_map/ppermute | solution.py:453
  22.7 1.0 %merge.1 = (f32[640,128]{1,0:T(8,128)}, f32[640,128]{1,0:T(8,128)}) custom-call(f32[8,5,2,8,128]{4,3,2,1,0:T(8,128)S(1)} %get-tuple-element.39.keep_a, f32[8,5,2,8,128]{4,3,2,1,0:T(8,128)S(1)} %get-tuple-element.40.keep_s, f32[8,5,2,8,128]{4,3,2,1,0:T(8,128)S(1)} %collective-permute-done.8.got), custom_call_target="tpu_custom_call" | custom-call | bytes 983040 | tf_op jit(solution)/shard_map/merge/pallas_call | solution.py:387
  (4 shorter events, 0.0 us)
Async XLA Ops:
  0.6 2.0 %collective-permute-start = (f32[640,128]{1,0:T(8,128)}, f32[640,128]{1,0:T(8,128)S(1)}, u32[]{:S(2)}, u32[]{:S(2)}) collective-permute-start(f32[640,128]{1,0:T(8,128)} %bitcast.3), channel_id=1, source_target_pairs={{0,16},{16,0},{1,17},{17,1},{2,18},{18,2},{3,19},{19,3},{4,20},{20... | collective-permute-start | bytes 983048 | tf_op jit(solution)/shard_map/ppermute | solution.py:419
  1.1 1.0 %copy-start = (f32[1,5,16,8,128]{4,3,2,1,0:T(8,128)S(1)}, f32[1,5,16,8,128]{4,3,2,1,0:T(8,128)}, u32[]{:S(2)}) copy-start(f32[1,5,16,8,128]{4,3,2,1,0:T(8,128)} %param.1) | copy-start | bytes 983044
  2.9 7.2 %collective-permute-start.1 = (f32[15,8,128]{2,1,0:T(8,128)S(1)}, f32[15,8,128]{2,1,0:T(8,128)S(1)}, u32[]{:S(2)}, u32[]{:S(2)}) collective-permute-start(f32[15,8,128]{2,1,0:T(8,128)S(1)} %get-tuple-element.26), channel_id=1, source_target_pairs={{0,4},{4,8},{8,12},{12,0},{1,5},{5,9},{9,13},{13,1},{2,6},{6,10},{... | collective-permute-start | bytes 184328 | tf_op jit(solution)/shard_map/ppermute | solution.py:425
  5.8 4.8 %collective-permute-start.2 = (f32[15,8,128]{2,1,0:T(8,128)S(1)}, f32[15,8,128]{2,1,0:T(8,128)S(1)}, u32[]{:S(2)}, u32[]{:S(2)}) collective-permute-start(f32[15,8,128]{2,1,0:T(8,128)S(1)} %get-tuple-element.27), channel_id=1, source_target_pairs={{0,12},{4,0},{8,4},{12,8},{1,13},{5,1},{9,5},{13,9},{2,14},{6,2},{... | collective-permute-start | bytes 184328 | tf_op jit(solution)/shard_map/ppermute | solution.py:426
  7.1 9.1 %collective-permute-start.4 = (f32[30,8,128]{2,1,0:T(8,128)S(1)}, f32[30,8,128]{2,1,0:T(8,128)S(1)}, u32[]{:S(2)}, u32[]{:S(2)}) collective-permute-start(f32[30,8,128]{2,1,0:T(8,128)S(1)} %get-tuple-element.29), channel_id=1, source_target_pairs={{0,4},{4,8},{8,12},{12,0},{1,5},{5,9},{9,13},{13,1},{2,6},{6,10},{... | collective-permute-start | bytes 368648 | tf_op jit(solution)/shard_map/ppermute | solution.py:430
  8.2 8.0 %collective-permute-start.5 = (f32[30,8,128]{2,1,0:T(8,128)S(1)}, f32[30,8,128]{2,1,0:T(8,128)S(1)}, u32[]{:S(2)}, u32[]{:S(2)}) collective-permute-start(f32[30,8,128]{2,1,0:T(8,128)S(1)} %get-tuple-element.30), channel_id=1, source_target_pairs={{0,12},{4,0},{8,4},{12,8},{1,13},{5,1},{9,5},{13,9},{2,14},{6,2},{... | collective-permute-start | bytes 368648 | tf_op jit(solution)/shard_map/ppermute | solution.py:431
  10.7 5.5 %collective-permute-start.3 = (f32[5,2,8,128]{3,2,1,0:T(8,128)S(1)}, f32[5,2,8,128]{3,2,1,0:T(8,128)S(1)}, u32[]{:S(2)}, u32[]{:S(2)}) collective-permute-start(f32[5,2,8,128]{3,2,1,0:T(8,128)S(1)} %get-tuple-element.28), channel_id=1, source_target_pairs={{0,19},{1,16},{2,17},{3,18},{19,0},{16,1},{17,2},{18,3},{4,23},{5,... | collective-permute-start | bytes 122888 | tf_op jit(solution)/shard_map/ppermute | solution.py:438
  13.2 5.6 %collective-permute-start.6 = (f32[10,8,128]{2,1,0:T(8,128)S(1)}, f32[10,8,128]{2,1,0:T(8,128)S(1)}, u32[]{:S(2)}, u32[]{:S(2)}) collective-permute-start(f32[10,8,128]{2,1,0:T(8,128)S(1)} %get-tuple-element.33), channel_id=1, source_target_pairs={{0,4},{4,8},{8,12},{12,0},{1,5},{5,9},{9,13},{13,1},{2,6},{6,10},{... | collective-permute-start | bytes 122888 | tf_op jit(solution)/shard_map/ppermute | solution.py:439
  14.8 4.0 %collective-permute-start.7 = (f32[10,8,128]{2,1,0:T(8,128)S(1)}, f32[10,8,128]{2,1,0:T(8,128)S(1)}, u32[]{:S(2)}, u32[]{:S(2)}) collective-permute-start(f32[10,8,128]{2,1,0:T(8,128)S(1)} %get-tuple-element.34), channel_id=1, source_target_pairs={{0,12},{4,0},{8,4},{12,8},{1,13},{5,1},{9,5},{13,9},{2,14},{6,2},{... | collective-permute-start | bytes 122888 | tf_op jit(solution)/shard_map/ppermute | solution.py:440
  21.0 1.7 %collective-permute-start.8 = (f32[8,5,2,8,128]{4,3,2,1,0:T(8,128)S(1)}, f32[8,5,2,8,128]{4,3,2,1,0:T(8,128)S(1)}, u32[]{:S(2)}, u32[]{:S(2)}) collective-permute-start(f32[8,5,2,8,128]{4,3,2,1,0:T(8,128)S(1)} %get-tuple-element.41), channel_id=1, source_target_pairs={{0,16},{16,0},{1,17},{17,1},{2,18},{18,2},{3,19},{19,3},{4,20},{20... | collective-permute-start | bytes 983048 | tf_op jit(solution)/shard_map/ppermute | solution.py:453

commit v5 on v4

--- a/solution.py
+++ b/solution.py
@@ -15,8 +15,6 @@
 TOTAL = ROWS + 2 * WS
 FK = [(f, k) for f in range(NF) for k in range(2)]
 VMEM_LIMIT = 32 * 2**20
-TURNS = (18, 16, 14, 8)
-BACK = (14, 12, 10, 8)
 UP1 = WS * NF
 CORNER = WS * (WS - 1) // 2 + WC * (WC - 1) // 2
 
@@ -102,14 +100,17 @@
     for f in range(NF):
         first_up[f] = edges[0][f]
         first_down[f] = edges[1][f]
-    pack_rows(t1, first_up, ROWS - WC, WC // 2, (0,), NF, lane, core)
-    pack_rows(t1, first_down, 0, WC // 2, (0,), NF, lane, core)
-
-
-def rest_kernel(t0, t1, side, rest_up, rest_down):
+    pack_rows(t1, first_up, ROWS - WC, WC // 2, (0, 1), NF, lane, core)
+
+
+def rest_kernel(t0, rest_up, rest_down):
     lane, core = lanes()
     pack_rows(t0, rest_up, ROWS - WS, WS // 2, (0, 1, 2), 0, lane, core)
     pack_rows(t0, rest_down, 0, WS // 2, (0, 1, 2), 0, lane, core)
+
+
+def tile_kernel(t0, t1, side):
+    lane, core = lanes()
     sides = [jnp.zeros((8, LANES), jnp.float32) for _ in FK]
     for r in range(ROWS):
         for which, width, tile in ((0, WS, t0), (1, WC, t1)):
@@ -125,7 +126,7 @@
         side[f, k] = sides[i]
 
 
-def side_kernel(side, low, high, t1, y, up1, down1):
+def side_kernel(side, low, high, t1, y, down1):
     lane, core = lanes()
     for k in range(2):
         place = (lane - 32 * k) & (LANES - 1)
@@ -134,55 +135,50 @@
                 (place >= HALF) & (place < HALF + CORNER), high[f], side[f, k]
             )
             y[f, k] = jnp.where(place < CORNER, low[f], with_high)
-    pack_rows(t1, up1, ROWS - WC, WC // 2, (1,), 0, lane, core)
-    pack_rows(t1, down1, 0, WC // 2, (1,), 0, lane, core)
+    pack_rows(t1, down1, 0, WC // 2, (0, 1), 0, lane, core)
 
 
 def units(which):
     return [0.5 / u for u in UNIT] if which else UNIT
 
 
-def assemble_tile(dst, offset, which, tile, y):
-    lane, core = lanes()
-    width = WC if which else WS
-    unit = units(which)
-    for r in range(ROWS):
-        outer = ((lane + width * (1 - core)) & (LANES - 1)) < width
-        for f, k in FK:
-            shift = LANES - width + width * core - tile_lane(which, r) - 32 * k
-            v = jnp.where(outer, turn(y[f, k], shift), tile[r, f, k])
-            dst[offset + r, f, k] = v * unit[f]
-
-
-def assemble_halo(dst, offset, which, d, y, edges, packed):
-    lane, core = lanes()
-    mine = owned(lane, core)
+def row_maker(which, tile, y, edges, packs):
+    lane, core = lanes()
     width = WC if which else WS
     unit = units(which)
     n = width // 2
-    for away in range(width):
-        w, at = corner(which)[away]
-        j = away if d else width - 1 - away
-        src, base = packed(j % n)
-        if w:
+
+    def make(i):
+        r = i - width
+        if 0 <= r < ROWS:
+            outer = ((lane + width * (1 - core)) & (LANES - 1)) < width
+
+            def block(f, k):
+                shift = LANES - width + width * core - tile_lane(which, r) - 32 * k
+                return jnp.where(outer, turn(y[f, k], shift), tile[r, f, k])
+
+        else:
+            d = 0 if r < 0 else 1
+            away = r - ROWS if d else -1 - r
+            j = away if d else i
+            w, at = corner(which)[away]
+            src, base = packs[d](j % n)
             outer = ((lane + w * (1 - core)) & (LANES - 1)) < w
             inner = ((lane - HALF + w * core) & (LANES - 1)) < w
-        for f, k in FK:
-            v = src[base + 2 * f + k]
-            if j >= n:
-                v = turn(v, HALF)
-            if w:
-                o = turn(y[f, k], LANES - w + w * core - HALF * d - at - 32 * k)
-                i = turn(edges[f], HALF * d - at - 32 * k - w * core)
-                v = jnp.where(inner, i, jnp.where(outer, o, v))
-            dst[offset + j, f, k] = v * unit[f]
-
-
-def halo_kernel(t0, t1, y, first_low, first_high, rest_low, rest_high, u0, lam):
-    assemble_halo(u0, 0, 0, 0, y, first_low, lambda j: (rest_low, 2 * NF * j))
-    assemble_tile(u0, WS, 0, t0, y)
-    assemble_halo(u0, WS + ROWS, 0, 1, y, first_high, lambda j: (rest_high, 2 * NF * j))
-    assemble_tile(lam, WS, 1, t1, y)
+
+            def block(f, k):
+                v = src[base + 2 * f + k]
+                if j >= n:
+                    v = turn(v, HALF)
+                if w:
+                    o = turn(y[f, k], LANES - w + w * core - HALF * d - at - 32 * k)
+                    i = turn(edges[d][f], HALF * d - at - 32 * k - w * core)
+                    v = jnp.where(inner, i, jnp.where(outer, o, v))
+                return v
+
+        return [[block(f, k) * unit[f] for f in range(NF)] for k in range(2)]
+
+    return make
 
 
 def load(ref, r):
@@ -233,31 +229,31 @@
     return before, after, here, left, right
 
 
-def rate_pass(src, lo, hi, emit, unroll):
-    _, after, _, _, _ = pieces(load(src, lo), False)
-    zero = [jnp.zeros((8, LANES), jnp.float32) for _ in FK]
-
-    def done(here, left, right, before):
-        return [
-            (turn(a, -1) + turn(b, 1)) + (c + d)
-            for a, b, c, d in zip(left, right, here, before)
-        ]
-
-    def body(r, carry):
-        here, after, left, right = carry
-        before, after2, here2, left2, right2 = pieces(load(src, r))
-        emit(r - 1, done(here, left, right, before))
-        here2 = [a + b for a, b in zip(here2, after)]
-        return here2, after2, left2, right2
-
-    here, _, left, right = lax.fori_loop(
-        lo + 1, hi - 1, body, (zero, after, zero, zero), unroll=unroll
-    )
-    before, _, _, _, _ = pieces(load(src, hi - 1), False)
-    emit(hi - 2, done(here, left, right, before))
-
-
-def forward_kernel(u0, s0, u1, s1, u2):
+def rate_pass(get, lo, hi, emit):
+    _, after, _, _, _ = pieces(get(lo), False)
+    here = left = right = None
+    for r in range(lo + 1, hi):
+        before, after2, here2, left2, right2 = pieces(get(r), r < hi - 1)
+        if here is not None:
+            sums = zip(left, right, here, before)
+            emit(r - 1, [(turn(a, -1) + turn(b, 1)) + (c + d) for a, b, c, d in sums])
+        here = [a + b for a, b in zip(here2, after)]
+        after, left, right = after2, left2, right2
+
+
+def forward_kernel(
+    t0, y, first_low, first_high, rest_low, rest_high, u0, s0, u1, s1, u2
+):
+    make = row_maker(
+        0, t0, y, (first_low, first_high),
+        (lambda j: (rest_low, 2 * NF * j), lambda j: (rest_high, 2 * NF * j)),
+    )
+
+    for r in range(TOTAL):
+        v = make(r)
+        for f, k in FK:
+            u0[r, f, k] = v[k][f]
+
     def section(base, dst):
         def emit(r, rate):
             for (f, k), x in zip(FK, rate):
@@ -268,16 +264,18 @@
     def advance(base, sec, dst, shift):
         def emit(r, rate):
             for (f, k), x in zip(FK, rate):
-                dst[r - shift, f, k] = 0.5 * (
-                    base[r, f, k] + (KEEP * sec[r, f, k] + x)
-                )
+                there = KEEP * sec[r, f, k] + x
+                dst[r - shift, f, k] = 0.5 * (base[r, f, k] + there)
 
         return emit
 
-    rate_pass(u0, 0, TOTAL, section(u0, s0), TURNS[0])
-    rate_pass(s0, 1, TOTAL - 1, advance(u0, s0, u1, 0), TURNS[1])
-    rate_pass(u1, 2, TOTAL - 2, section(u1, s1), TURNS[2])
-    rate_pass(s1, WS - 1, WS + ROWS + 1, advance(u1, s1, u2, WS - 1), TURNS[3])
+    def rows(ref):
+        return lambda r: load(ref, r)
+
+    rate_pass(rows(u0), 0, TOTAL, section(u0, s0))
+    rate_pass(rows(s0), 1, TOTAL - 1, advance(u0, s0, u1, 0))
+    rate_pass(rows(u1), 2, TOTAL - 2, section(u1, s1))
+    rate_pass(rows(s1), WS - 1, WS + ROWS + 1, advance(u1, s1, u2, WS))
 
 
 def beside_lanes(row):
@@ -322,51 +320,101 @@
             emit(f, k, out[f] + (VISC * around[f] - (6.0 * VISC) * wc[k][f]), wc[k][f])
 
 
-def pull_pass(state, w, lo, hi, emit, unroll):
-    def body(r, carry):
-        wp = load(w, r + 1)
+def pull_pass(state, w, lo, hi, emit, make=None):
+    def row(r):
+        if make:
+            v = make(r)
+            for f, k in FK:
+                w[r, f, k] = v[k][f]
+        return load(w, r)
+
+    row(lo - 1)
+    beside = beside_lanes(row(lo))
+    for r in range(lo, hi):
+        wp = row(r + 1)
         ahead = beside_lanes(wp)
         pulled(
-            load(state, r), load(w, r - 1), load(w, r), wp, *carry,
+            load(state, r), load(w, r - 1), load(w, r), wp, *beside,
             lambda f, k, x, c: emit(r, f, k, x, c),
         )
-        return ahead
-
-    lax.fori_loop(lo, hi, body, beside_lanes(load(w, lo)), unroll=unroll)
-
-
-def adjoint_kernel(
-    low_lam, u0, y, first_low, first_high, low, high, s0, u1, s1, u2,
-    keep_a, keep_s, send, lam, cot, wgt, lam1,
-):
-    assemble_halo(lam, WS - WC, 1, 0, y, first_low, lambda j: (low, 0) if j else (first_low, NF))
-    assemble_halo(lam, WS + ROWS, 1, 1, y, first_high, lambda j: (high, 0) if j else (first_high, NF))
-    lane, core = lanes()
-    first = core == 0
-    mine = owned(lane, core)
-
+        beside = ahead
+
+
+def send_block(out, i, f, k, lam, state, mine):
+    out[i, f, k] = jnp.where(mine, lam, turn(state, HALF))
+
+
+def last_step(s0, u0, lam1, cot, wgt, emit):
     def section(r, f, k, x, w):
         cot[r, f, k] = x
         wgt[r, f, k] = w + x
 
+    def last(r, f, k, x, w):
+        emit(r - WS, f, k, lam1[r, f, k] + 0.5 * (cot[r, f, k] + x))
+
+    pull_pass(s0, lam1, 5, TOTAL - 5, section)
+    pull_pass(u0, wgt, WS, WS + ROWS, last)
+
+
+def adjoint_kernel(
+    t1, y, first_low, first_high, high, u0, s0, u1, s1, u2,
+    lam1, send, lam, cot, wgt,
+):
+    make = row_maker(
+        1, t1, y, (first_low, first_high),
+        (
+            lambda j: (first_low, NF + 2 * NF * j),
+            lambda j: (high, 2 * NF * j),
+        ),
+    )
+    lane, core = lanes()
+    mine = owned(lane, core)
+
+    def section(r, f, k, x, w):
+        cot[r, f, k] = x
+        wgt[r, f, k] = w + x
+
     def middle(r, f, k, x, w):
         lam1[r, f, k] = lam[r, f, k] + 0.5 * (cot[r, f, k] + x)
 
-    def last(r, f, k, x, w):
-        i = r - WS
-        before = lam1[r, f, k]
-        start = before + 0.5 * (cot[r, f, k] + x)
-        mid, end = u1[r, f, k], u2[i + 1, f, k]
-        keep_a[i, f, k] = jnp.where(first, start, before)
-        keep_s[i, f, k] = jnp.where(first, mid, end)
-        away_a = jnp.where(first, before, start)
-        away_s = jnp.where(first, end, mid)
-        send[i, f, k] = jnp.where(mine, away_a, turn(away_s, HALF))
-
-    pull_pass(s1, lam, 3, TOTAL - 3, section, BACK[0])
-    pull_pass(u1, wgt, 4, TOTAL - 4, middle, BACK[1])
-    pull_pass(s0, lam1, 5, TOTAL - 5, section, BACK[2])
-    pull_pass(u0, wgt, WS, WS + ROWS, last, BACK[3])
+    for r in range(2, TOTAL - 2):
+        v = make(r - (WS - WC))
+        for f, k in FK:
+            lam[r, f, k] = v[k][f]
+    pull_pass(s1, lam, 3, TOTAL - 3, section)
+    pull_pass(u1, wgt, 4, TOTAL - 4, middle)
+
+    @pl.when(core == 0)
+    def _():
+        for i in range(ROWS):
+            for f, k in FK:
+                send_block(send, i, f, k, lam1[WS + i, f, k], u2[i, f, k], mine)
+
+    @pl.when(core == 1)
+    def _():
+        last_step(
+            s0, u0, lam1, cot, wgt,
+            lambda i, f, k, x: send_block(send, i, f, k, x, u1[WS + i, f, k], mine),
+        )
+
+
+def finish_kernel(lam1, u0, s0, u1, u2, keep_a, keep_s, cot, wgt):
+    core = lax.axis_index("grp")
+
+    @pl.when(core == 0)
+    def _():
+        def emit(i, f, k, x):
+            keep_a[i, f, k] = x
+            keep_s[i, f, k] = u1[WS + i, f, k]
+
+        last_step(s0, u0, lam1, cot, wgt, emit)
+
+    @pl.when(core == 1)
+    def _():
+        for i in range(ROWS):
+            for f, k in FK:
+                keep_a[i, f, k] = lam1[WS + i, f, k]
+                keep_s[i, f, k] = u2[i, f, k]
 
 
 def merge_kernel(keep_a, keep_s, got, out_a, out_s):
@@ -415,42 +463,42 @@
     def pack(rows):
         return (NF * rows, 8, LANES)
 
-    edge = (3 * NF, 8, LANES)
+    edge = (NF, 8, LANES)
     got = lax.ppermute(own, "grp", swap)
     (mine,) = call(own_kernel, "own", [tile], [], own, flops=10**6)
     t0, t1, first_up, first_down = call(
-        first_kernel, "first", [tile, tile, edge, edge], [], mine, got,
+        first_kernel, "first", [tile, tile, pack(WC + 1), edge], [], mine, got,
         flops=10**6,
     )
     first_low = lax.ppermute(first_up, "tx", up)
     first_high = lax.ppermute(first_down, "tx", down)
-    side, rest_up, rest_down = call(
-        rest_kernel, "rest", [block, pack(WS), pack(WS)], [], t0, t1, flops=10**6
-    )
+    rest_up, rest_down = call(
+        rest_kernel, "rest", [pack(WS), pack(WS)], [], t0, flops=10**6
+    )
+    (side,) = call(tile_kernel, "tile", [block], [], t0, t1, flops=10**7)
     rest_low = lax.ppermute(rest_up, "tx", up)
     rest_high = lax.ppermute(rest_down, "tx", down)
-    y, up1, down1 = call(
-        side_kernel, "side", [block, pack(WC - 2), pack(WC - 2)], [],
+    y, down1 = call(
+        side_kernel, "side", [block, pack(WC)], [],
         side, first_low, first_high, t1, flops=10**10,
     )
     pairs = [(i, ty + (i - 1) % ty) for i in range(ty)]
     pairs += [(b, a) for a, b in pairs]
     y = lax.ppermute(y, ("grp", "ty"), pairs)
-    low1 = lax.ppermute(up1, "tx", up)
     high1 = lax.ppermute(down1, "tx", down)
-    u0, lam = call(
-        halo_kernel, "halo", [full, full], [],
-        t0, t1, y, first_low, first_high, rest_low, rest_high, flops=10**7,
-    )
-    s0, u1, s1, u2 = call(
-        forward_kernel, "forward", [full, full, full, rows_of(ROWS + 1)], [], u0,
-        flops=10**9,
-    )
-    keep_a, keep_s, send, _ = call(
-        adjoint_kernel, "adjoint", [tile, tile, tile, full], [full] * 3,
-        lam, u0, y, first_low, first_high, low1, high1, s0, u1, s1, u2, flops=10**8, aliases={0: 3},
+    u0, s0, u1, s1, u2 = call(
+        forward_kernel, "forward", [full, full, full, full, tile], [],
+        t0, y, first_low, first_high, rest_low, rest_high, flops=10**9,
+    )
+    lam1, send = call(
+        adjoint_kernel, "adjoint", [full, tile], [full] * 3,
+        t1, y, first_low, first_high, high1, u0, s0, u1, s1, u2, flops=10**8,
     )
     other = lax.ppermute(send, "grp", swap)
+    keep_a, keep_s = call(
+        finish_kernel, "finish", [tile, tile], [full] * 2, lam1, u0, s0, u1, u2,
+        flops=10**8,
+    )
     adjoints, states = call(
         merge_kernel, "merge", [own.shape, own.shape], [], keep_a, keep_s, other
     )

time: 23.8 us -> 22.8 us (0.958)
  starting transfers between devices: 12.9 us -> 11.2 us
  waiting for transfers between devices: 2.61 us -> 3.42 us
    ppermute x1, waiting for transfers between devices: 0.01 us -> 1.65 us  [shards(): rest_high = lax.ppermute(rest_down, 'tx', down)]
    ppermute x1 -> x0, starting transfers between devices: 1.61 us -> none  [shards(): low1 = lax.ppermute(up1, 'tx', up)]
    ppermute x1, waiting for transfers between devices: 1.62 us -> 0.81 us  [shards(): other = lax.ppermute(send, 'grp', swap)]
    pallas_call x8 -> x9, Pallas kernels: 6.49 us -> 6.31 us  [call(): pl.pallas_call(kernel, out_shape=shapes, name=name, scratch_shapes=[pltpu...]
  transfers between devices with their start and end apart: 9 -> 8, of which waited for: 3 -> 5; matrix products, arithmetic and copies ran while one was open for 0% -> 0% of each run, Pallas kernels for 13% -> 16%
where the time goes in v5:
time: 22.8 us; the launch traced here: 22.6 us
  starting transfers between devices  11.2 us (49%)
  Pallas kernels  6.31 us (28%)
  waiting for transfers between devices  3.42 us (15%)
  local copies, waits for them, and re-layouts  0.97 us (4%)
  between operations  0.71 us (3%)
    pallas_call x9, Pallas kernels, call(): pl.pallas_call(kernel, out_shape=shapes, name=name, scratch_shapes=[pltpu...  6.31 us
    ppermute x1, starting transfers between devices, shards(): first_low = lax.ppermute(first_up, 'tx', up)  2.91 us
    ppermute x1, starting transfers between devices, shards(): y = lax.ppermute(y, ('grp', 'ty'), pairs)  2.56 us
    ppermute x1, starting transfers between devices, shards(): rest_high = lax.ppermute(rest_down, 'tx', down)  1.92 us
    ppermute x1, waiting for transfers between devices, shards(): rest_high = lax.ppermute(rest_down, 'tx', down)  1.65 us
    ppermute x1, starting transfers between devices, shards(): high1 = lax.ppermute(down1, 'tx', down)  1.14 us
    ppermute x1, starting transfers between devices, shards(): rest_low = lax.ppermute(rest_up, 'tx', up)  1.06 us
    ppermute x1, starting transfers between devices, shards(): first_high = lax.ppermute(first_down, 'tx', down)  1.02 us
  transfers between devices with their start and end apart: 8, of which 5 were waited for; matrix products, arithmetic and copies ran while one was open for 0% of the time, Pallas kernels for 16%

profile of v5, /device:TPU:0, one launch (start us, length us, event | category | flops | bytes accessed | tf_op | source)
XLA Modules:
  0.0 22.6 jit_solution(12588843153173322039)
XLA Ops:
  0.6 0.5 %collective-permute-start = (f32[640,128]{1,0:T(8,128)}, f32[640,128]{1,0:T(8,128)S(1)}, u32[]{:S(2)}, u32[]{:S(2)}) collective-permute-start(f32[640,128]{1,0:T(8,128)} %bitcast.3), channel_id=1, source_target_pairs={{0,16},{16,0},{1,17},{17,1},{2,18},{18,2},{3,19},{19,3},{4,20},{20... | collective-permute-start | bytes 983048 | tf_op jit(solution)/shard_map/ppermute | solution.py:467
  1.1 1.0 %copy-done = f32[1,5,16,8,128]{4,3,2,1,0:T(8,128)S(1)} copy-done((f32[1,5,16,8,128]{4,3,2,1,0:T(8,128)S(1)}, f32[1,5,16,8,128]{4,3,2,1,0:T(8,128)}, u32[]{:S(2)}) %copy-start) | copy-done | bytes 327704
  2.1 0.1 own.1
  2.2 0.4 %collective-permute-done.got = f32[640,128]{1,0:T(8,128)S(1)} collective-permute-done((f32[640,128]{1,0:T(8,128)}, f32[640,128]{1,0:T(8,128)S(1)}, u32[]{:S(2)}, u32[]{:S(2)}) %collective-permute-start) | collective-permute-done | bytes 327712 | tf_op jit(solution)/shard_map/ppermute | solution.py:467
  2.6 0.3 %first.1 = (f32[8,5,2,8,128]{4,3,2,1,0:T(8,128)S(1)}, f32[8,5,2,8,128]{4,3,2,1,0:T(8,128)S(1)}, f32[25,8,128]{2,1,0:T(8,128)S(1)}, f32[5,8,128]{2,1,0:T(8,128)S(1)}) custom-call(f32[8,5,2,8,128]{4,3,2,1,0:T(8,128)S(1)} %own.1, f32[640,128]{1,0:T(8,128)S(1)} %collective-permute-done.got), custom_call_target="tpu_custom_call" | custom-call | flops 1000000 | bytes 655360 | tf_op jit(solution)/shard_map/first/pallas_call | solution.py:435
  2.9 2.9 %collective-permute-start.1 = (f32[25,8,128]{2,1,0:T(8,128)S(1)}, f32[25,8,128]{2,1,0:T(8,128)S(1)}, u32[]{:S(2)}, u32[]{:S(2)}) collective-permute-start(f32[25,8,128]{2,1,0:T(8,128)S(1)} %get-tuple-element.23), channel_id=1, source_target_pairs={{0,4},{4,8},{8,12},{12,0},{1,5},{5,9},{9,13},{13,1},{2,6},{6,10},{... | collective-permute-start | bytes 307208 | tf_op jit(solution)/shard_map/ppermute | solution.py:473
  5.8 1.0 %collective-permute-start.2 = (f32[5,8,128]{2,1,0:T(8,128)S(1)}, f32[5,8,128]{2,1,0:T(8,128)S(1)}, u32[]{:S(2)}, u32[]{:S(2)}) collective-permute-start(f32[5,8,128]{2,1,0:T(8,128)S(1)} %get-tuple-element.24), channel_id=1, source_target_pairs={{0,12},{4,0},{8,4},{12,8},{1,13},{5,1},{9,5},{13,9},{2,14},{6,2},{... | collective-permute-start | bytes 61448 | tf_op jit(solution)/shard_map/ppermute | solution.py:474
  6.8 0.1 rest.1
  7.0 1.1 %collective-permute-start.5 = (f32[30,8,128]{2,1,0:T(8,128)S(1)}, f32[30,8,128]{2,1,0:T(8,128)S(1)}, u32[]{:S(2)}, u32[]{:S(2)}) collective-permute-start(f32[30,8,128]{2,1,0:T(8,128)S(1)} %get-tuple-element.27), channel_id=1, source_target_pairs={{0,4},{4,8},{8,12},{12,0},{1,5},{5,9},{9,13},{13,1},{2,6},{6,10},{... | collective-permute-start | bytes 368648 | tf_op jit(solution)/shard_map/ppermute | solution.py:479
  8.0 1.9 %collective-permute-start.6 = (f32[30,8,128]{2,1,0:T(8,128)S(1)}, f32[30,8,128]{2,1,0:T(8,128)S(1)}, u32[]{:S(2)}, u32[]{:S(2)}) collective-permute-start(f32[30,8,128]{2,1,0:T(8,128)S(1)} %get-tuple-element.28), channel_id=1, source_target_pairs={{0,12},{4,0},{8,4},{12,8},{1,13},{5,1},{9,5},{13,9},{2,14},{6,2},{... | collective-permute-start | bytes 368648 | tf_op jit(solution)/shard_map/ppermute | solution.py:480
  9.9 0.2 %tile.1.side = f32[5,2,8,128]{3,2,1,0:T(8,128)S(1)} custom-call(f32[8,5,2,8,128]{4,3,2,1,0:T(8,128)S(1)} %get-tuple-element.22.t0, f32[8,5,2,8,128]{4,3,2,1,0:T(8,128)S(1)} %get-tuple-element.21.t1), custom_call_target="tpu_custom_call" | custom-call | flops 10000000 | bytes 655360 | tf_op jit(solution)/shard_map/tile/pallas_call | solution.py:435
  10.2 0.5 %collective-permute-done.2.high.first_high = f32[5,8,128]{2,1,0:T(8,128)S(1)} collective-permute-done((f32[5,8,128]{2,1,0:T(8,128)S(1)}, f32[5,8,128]{2,1,0:T(8,128)S(1)}, u32[]{:S(2)}, u32[]{:S(2)}) %collective-permute-start.2) | collective-permute-done | bytes 20512 | tf_op jit(solution)/shard_map/ppermute | solution.py:474
  10.7 0.0 collective-permute-done.1.low.first_low
  10.7 0.1 side.1
  10.8 2.6 %collective-permute-start.3 = (f32[5,2,8,128]{3,2,1,0:T(8,128)S(1)}, f32[5,2,8,128]{3,2,1,0:T(8,128)S(1)}, u32[]{:S(2)}, u32[]{:S(2)}) collective-permute-start(f32[5,2,8,128]{3,2,1,0:T(8,128)S(1)} %get-tuple-element.25), channel_id=1, source_target_pairs={{0,19},{1,16},{2,17},{3,18},{19,0},{16,1},{17,2},{18,3},{4,23},{5,... | collective-permute-start | bytes 122888 | tf_op jit(solution)/shard_map/ppermute | solution.py:487
  13.3 1.1 %collective-permute-start.4 = (f32[20,8,128]{2,1,0:T(8,128)S(1)}, f32[20,8,128]{2,1,0:T(8,128)S(1)}, u32[]{:S(2)}, u32[]{:S(2)}) collective-permute-start(f32[20,8,128]{2,1,0:T(8,128)S(1)} %get-tuple-element.26), channel_id=1, source_target_pairs={{0,12},{4,0},{8,4},{12,8},{1,13},{5,1},{9,5},{13,9},{2,14},{6,2},{... | collective-permute-start | bytes 245768 | tf_op jit(solution)/shard_map/ppermute | solution.py:488
  14.5 1.6 %collective-permute-done.6.rest_high = f32[30,8,128]{2,1,0:T(8,128)S(1)} collective-permute-done((f32[30,8,128]{2,1,0:T(8,128)S(1)}, f32[30,8,128]{2,1,0:T(8,128)S(1)}, u32[]{:S(2)}, u32[]{:S(2)}) %collective-permute-start.6) | collective-permute-done | bytes 122912 | tf_op jit(solution)/shard_map/ppermute | solution.py:480
  16.1 0.1 collective-permute-done.3.y
  16.2 2.2 %forward.1 = (f32[20,5,2,8,128]{4,3,2,1,0:T(8,128)S(1)}, f32[20,5,2,8,128]{4,3,2,1,0:T(8,128)S(1)}, f32[20,5,2,8,128]{4,3,2,1,0:T(8,128)S(1)}, f32[20,5,2,8,128]{4,3,2,1,0:T(8,128)S(1)}, f32[8,5,2,8,128]{4,3,2,1,0:T(8,128)S(1)}) custom-call(f32[8,5,2,8,128]{4,3,2,1,0:T(8,128)S(1)} %get-tuple-element.22.t0, f32[5,2,8,128]{3,2,1,0:T(8,128)S(1)} %collective-permute-done.3.y, ...), custom_call_target="tpu_custom_call" | custom-call | flops 1000000000 | bytes 737280 | tf_op jit(solution)/shard_map/forward/pallas_call | solution.py:435
  18.5 1.5 %adjoint.1 = (f32[20,5,2,8,128]{4,3,2,1,0:T(8,128)S(1)}, f32[8,5,2,8,128]{4,3,2,1,0:T(8,128)S(1)}) custom-call(f32[8,5,2,8,128]{4,3,2,1,0:T(8,128)S(1)} %get-tuple-element.21.t1, f32[5,2,8,128]{3,2,1,0:T(8,128)S(1)} %collective-permute-done.3.y, f32[25,8,128]{2,1,0:T(8,128)S(1)} %collective-permute-done.1.low.first_low, ...), custom_call_target="tpu_custom_call" | custom-call | flops 100000000 | bytes 4177920 | tf_op jit(solution)/shard_map/adjoint/pallas_call | solution.py:435
  20.0 0.1 collective-permute-start.7
  20.0 0.8 %finish.1 = (f32[8,5,2,8,128]{4,3,2,1,0:T(8,128)S(1)}, f32[8,5,2,8,128]{4,3,2,1,0:T(8,128)S(1)}) custom-call(f32[20,5,2,8,128]{4,3,2,1,0:T(8,128)S(1)} %get-tuple-element.34.lam1, f32[20,5,2,8,128]{4,3,2,1,0:T(8,128)S(1)} %get-tuple-element.29.u0, f32[20,5,2,8,128]{4,3,2,1,0:T(8,128)S(1)} %get-tuple-element.30.s0, ...), custom_call_target="tpu_custom_call" | custom-call | flops 100000000 | bytes 3604480 | tf_op jit(solution)/shard_map/finish/pallas_call | solution.py:435
  20.8 0.8 %collective-permute-done.7.got = f32[8,5,2,8,128]{4,3,2,1,0:T(8,128)S(1)} collective-permute-done((f32[8,5,2,8,128]{4,3,2,1,0:T(8,128)S(1)}, f32[8,5,2,8,128]{4,3,2,1,0:T(8,128)S(1)}, u32[]{:S(2)}, u32[]{:S(2)}) %collective-permute-start.7) | collective-permute-done | bytes 327712 | tf_op jit(solution)/shard_map/ppermute | solution.py:497
  21.6 1.0 %merge.1 = (f32[640,128]{1,0:T(8,128)}, f32[640,128]{1,0:T(8,128)}) custom-call(f32[8,5,2,8,128]{4,3,2,1,0:T(8,128)S(1)} %get-tuple-element.35.keep_a, f32[8,5,2,8,128]{4,3,2,1,0:T(8,128)S(1)} %get-tuple-element.36.keep_s, f32[8,5,2,8,128]{4,3,2,1,0:T(8,128)S(1)} %collective-permute-done.7.got), custom_call_target="tpu_custom_call" | custom-call | bytes 983040 | tf_op jit(solution)/shard_map/merge/pallas_call | solution.py:435
  (3 shorter events, 0.0 us)
Async XLA Ops:
  0.6 2.0 %collective-permute-start = (f32[640,128]{1,0:T(8,128)}, f32[640,128]{1,0:T(8,128)S(1)}, u32[]{:S(2)}, u32[]{:S(2)}) collective-permute-start(f32[640,128]{1,0:T(8,128)} %bitcast.3), channel_id=1, source_target_pairs={{0,16},{16,0},{1,17},{17,1},{2,18},{18,2},{3,19},{19,3},{4,20},{20... | collective-permute-start | bytes 983048 | tf_op jit(solution)/shard_map/ppermute | solution.py:467
  1.1 1.0 %copy-start = (f32[1,5,16,8,128]{4,3,2,1,0:T(8,128)S(1)}, f32[1,5,16,8,128]{4,3,2,1,0:T(8,128)}, u32[]{:S(2)}) copy-start(f32[1,5,16,8,128]{4,3,2,1,0:T(8,128)} %param.1) | copy-start | bytes 983044
  2.9 7.8 %collective-permute-start.1 = (f32[25,8,128]{2,1,0:T(8,128)S(1)}, f32[25,8,128]{2,1,0:T(8,128)S(1)}, u32[]{:S(2)}, u32[]{:S(2)}) collective-permute-start(f32[25,8,128]{2,1,0:T(8,128)S(1)} %get-tuple-element.23), channel_id=1, source_target_pairs={{0,4},{4,8},{8,12},{12,0},{1,5},{5,9},{9,13},{13,1},{2,6},{6,10},{... | collective-permute-start | bytes 307208 | tf_op jit(solution)/shard_map/ppermute | solution.py:473
  5.8 4.8 %collective-permute-start.2 = (f32[5,8,128]{2,1,0:T(8,128)S(1)}, f32[5,8,128]{2,1,0:T(8,128)S(1)}, u32[]{:S(2)}, u32[]{:S(2)}) collective-permute-start(f32[5,8,128]{2,1,0:T(8,128)S(1)} %get-tuple-element.24), channel_id=1, source_target_pairs={{0,12},{4,0},{8,4},{12,8},{1,13},{5,1},{9,5},{13,9},{2,14},{6,2},{... | collective-permute-start | bytes 61448 | tf_op jit(solution)/shard_map/ppermute | solution.py:474
  7.0 7.5 %collective-permute-start.5 = (f32[30,8,128]{2,1,0:T(8,128)S(1)}, f32[30,8,128]{2,1,0:T(8,128)S(1)}, u32[]{:S(2)}, u32[]{:S(2)}) collective-permute-start(f32[30,8,128]{2,1,0:T(8,128)S(1)} %get-tuple-element.27), channel_id=1, source_target_pairs={{0,4},{4,8},{8,12},{12,0},{1,5},{5,9},{9,13},{13,1},{2,6},{6,10},{... | collective-permute-start | bytes 368648 | tf_op jit(solution)/shard_map/ppermute | solution.py:479
  8.0 8.1 %collective-permute-start.6 = (f32[30,8,128]{2,1,0:T(8,128)S(1)}, f32[30,8,128]{2,1,0:T(8,128)S(1)}, u32[]{:S(2)}, u32[]{:S(2)}) collective-permute-start(f32[30,8,128]{2,1,0:T(8,128)S(1)} %get-tuple-element.28), channel_id=1, source_target_pairs={{0,12},{4,0},{8,4},{12,8},{1,13},{5,1},{9,5},{13,9},{2,14},{6,2},{... | collective-permute-start | bytes 368648 | tf_op jit(solution)/shard_map/ppermute | solution.py:480
  10.8 5.5 %collective-permute-start.3 = (f32[5,2,8,128]{3,2,1,0:T(8,128)S(1)}, f32[5,2,8,128]{3,2,1,0:T(8,128)S(1)}, u32[]{:S(2)}, u32[]{:S(2)}) collective-permute-start(f32[5,2,8,128]{3,2,1,0:T(8,128)S(1)} %get-tuple-element.25), channel_id=1, source_target_pairs={{0,19},{1,16},{2,17},{3,18},{19,0},{16,1},{17,2},{18,3},{4,23},{5,... | collective-permute-start | bytes 122888 | tf_op jit(solution)/shard_map/ppermute | solution.py:487
  13.3 5.2 %collective-permute-start.4 = (f32[20,8,128]{2,1,0:T(8,128)S(1)}, f32[20,8,128]{2,1,0:T(8,128)S(1)}, u32[]{:S(2)}, u32[]{:S(2)}) collective-permute-start(f32[20,8,128]{2,1,0:T(8,128)S(1)} %get-tuple-element.26), channel_id=1, source_target_pairs={{0,12},{4,0},{8,4},{12,8},{1,13},{5,1},{9,5},{13,9},{2,14},{6,2},{... | collective-permute-start | bytes 245768 | tf_op jit(solution)/shard_map/ppermute | solution.py:488
  20.0 1.7 %collective-permute-start.7 = (f32[8,5,2,8,128]{4,3,2,1,0:T(8,128)S(1)}, f32[8,5,2,8,128]{4,3,2,1,0:T(8,128)S(1)}, u32[]{:S(2)}, u32[]{:S(2)}) collective-permute-start(f32[8,5,2,8,128]{4,3,2,1,0:T(8,128)S(1)} %get-tuple-element.37), channel_id=1, source_target_pairs={{0,16},{16,0},{1,17},{17,1},{2,18},{18,2},{3,19},{19,3},{4,20},{20... | collective-permute-start | bytes 983048 | tf_op jit(solution)/shard_map/ppermute | solution.py:497

commit v6 on v5

--- a/solution.py
+++ b/solution.py
@@ -109,6 +109,11 @@
     pack_rows(t0, rest_down, 0, WS // 2, (0, 1, 2), 0, lane, core)
 
 
+def late_kernel(t1, y, down1):
+    lane, core = lanes()
+    pack_rows(t1, down1, 0, WC // 2, (0, 1), 0, lane, core)
+
+
 def tile_kernel(t0, t1, side):
     lane, core = lanes()
     sides = [jnp.zeros((8, LANES), jnp.float32) for _ in FK]
@@ -126,7 +131,7 @@
         side[f, k] = sides[i]
 
 
-def side_kernel(side, low, high, t1, y, down1):
+def side_kernel(side, low, high, y):
     lane, core = lanes()
     for k in range(2):
         place = (lane - 32 * k) & (LANES - 1)
@@ -135,7 +140,6 @@
                 (place >= HALF) & (place < HALF + CORNER), high[f], side[f, k]
             )
             y[f, k] = jnp.where(place < CORNER, low[f], with_high)
-    pack_rows(t1, down1, 0, WC // 2, (0, 1), 0, lane, core)
 
 
 def units(which):
@@ -241,6 +245,40 @@
         after, left, right = after2, left2, right2
 
 
+def steps(u0, s0, u1, s1, u2):
+    def section(base, dst):
+        def emit(r, rate):
+            for (f, k), x in zip(FK, rate):
+                dst[r, f, k] = KEEP * base[r, f, k] + x
+
+        return emit
+
+    def advance(base, sec, dst, shift):
+        def emit(r, rate):
+            for (f, k), x in zip(FK, rate):
+                there = KEEP * sec[r, f, k] + x
+                dst[r - shift, f, k] = 0.5 * (base[r, f, k] + there)
+
+        return emit
+
+    def run(ref, emit):
+        return lambda lo, hi: rate_pass(lambda r: load(ref, r), lo, hi, emit)
+
+    return (
+        run(u0, section(u0, s0)),
+        run(s0, advance(u0, s0, u1, 0)),
+        run(u1, section(u1, s1)),
+        run(s1, advance(u1, s1, u2, WS)),
+    )
+
+
+def outer_forward(u0, s0, u1, s1):
+    passes = steps(u0, s0, u1, s1, None)
+    for n in range(3):
+        passes[n](n, n + 4)
+        passes[n](TOTAL - 4 - n, TOTAL - n)
+
+
 def forward_kernel(
     t0, y, first_low, first_high, rest_low, rest_high, u0, s0, u1, s1, u2
 ):
@@ -248,34 +286,16 @@
         0, t0, y, (first_low, first_high),
         (lambda j: (rest_low, 2 * NF * j), lambda j: (rest_high, 2 * NF * j)),
     )
-
     for r in range(TOTAL):
         v = make(r)
         for f, k in FK:
             u0[r, f, k] = v[k][f]
-
-    def section(base, dst):
-        def emit(r, rate):
-            for (f, k), x in zip(FK, rate):
-                dst[r, f, k] = KEEP * base[r, f, k] + x
-
-        return emit
-
-    def advance(base, sec, dst, shift):
-        def emit(r, rate):
-            for (f, k), x in zip(FK, rate):
-                there = KEEP * sec[r, f, k] + x
-                dst[r - shift, f, k] = 0.5 * (base[r, f, k] + there)
-
-        return emit
-
-    def rows(ref):
-        return lambda r: load(ref, r)
-
-    rate_pass(rows(u0), 0, TOTAL, section(u0, s0))
-    rate_pass(rows(s0), 1, TOTAL - 1, advance(u0, s0, u1, 0))
-    rate_pass(rows(u1), 2, TOTAL - 2, section(u1, s1))
-    rate_pass(rows(s1), WS - 1, WS + ROWS + 1, advance(u1, s1, u2, WS))
+    for n, step in enumerate(steps(u0, s0, u1, s1, u2)):
+        step(2 + n, TOTAL - 2 - n)
+
+    @pl.when(lax.axis_index("grp") == 1)
+    def _():
+        outer_forward(u0, s0, u1, s1)
 
 
 def beside_lanes(row):
@@ -356,6 +376,24 @@
     pull_pass(u0, wgt, WS, WS + ROWS, last)
 
 
+def first_step(s1, u1, lam, cot, wgt, lam1, cuts):
+    def section(r, f, k, x, w):
+        cot[r, f, k] = x
+        wgt[r, f, k] = w + x
+
+    def middle(r, f, k, x, w):
+        lam1[r, f, k] = lam[r, f, k] + 0.5 * (cot[r, f, k] + x)
+
+    for lo, hi in cuts[0]:
+        pull_pass(s1, lam, lo, hi, section)
+    for lo, hi in cuts[1]:
+        pull_pass(u1, wgt, lo, hi, middle)
+
+
+INNER = (((5, TOTAL - 5),), ((6, TOTAL - 6),))
+OUTER = (((3, 5), (TOTAL - 5, TOTAL - 3)), ((4, 6), (TOTAL - 6, TOTAL - 4)))
+
+
 def adjoint_kernel(
     t1, y, first_low, first_high, high, u0, s0, u1, s1, u2,
     lam1, send, lam, cot, wgt,
@@ -369,20 +407,11 @@
     )
     lane, core = lanes()
     mine = owned(lane, core)
-
-    def section(r, f, k, x, w):
-        cot[r, f, k] = x
-        wgt[r, f, k] = w + x
-
-    def middle(r, f, k, x, w):
-        lam1[r, f, k] = lam[r, f, k] + 0.5 * (cot[r, f, k] + x)
-
     for r in range(2, TOTAL - 2):
         v = make(r - (WS - WC))
         for f, k in FK:
             lam[r, f, k] = v[k][f]
-    pull_pass(s1, lam, 3, TOTAL - 3, section)
-    pull_pass(u1, wgt, 4, TOTAL - 4, middle)
+    first_step(s1, u1, lam, cot, wgt, lam1, INNER)
 
     @pl.when(core == 0)
     def _():
@@ -392,13 +421,16 @@
 
     @pl.when(core == 1)
     def _():
+        first_step(s1, u1, lam, cot, wgt, lam1, OUTER)
         last_step(
             s0, u0, lam1, cot, wgt,
             lambda i, f, k, x: send_block(send, i, f, k, x, u1[WS + i, f, k], mine),
         )
 
 
-def finish_kernel(lam1, u0, s0, u1, u2, keep_a, keep_s, cot, wgt):
+def finish_kernel(
+    a, b, c, d, e, g, u0, lam, u2, keep_a, keep_s, s0, u1, s1, lam1, cot, wgt
+):
     core = lax.axis_index("grp")
 
     @pl.when(core == 0)
@@ -407,6 +439,8 @@
             keep_a[i, f, k] = x
             keep_s[i, f, k] = u1[WS + i, f, k]
 
+        outer_forward(u0, s0, u1, s1)
+        first_step(s1, u1, lam, cot, wgt, lam1, OUTER)
         last_step(s0, u0, lam1, cot, wgt, emit)
 
     @pl.when(core == 1)
@@ -478,26 +512,27 @@
     (side,) = call(tile_kernel, "tile", [block], [], t0, t1, flops=10**7)
     rest_low = lax.ppermute(rest_up, "tx", up)
     rest_high = lax.ppermute(rest_down, "tx", down)
-    y, down1 = call(
-        side_kernel, "side", [block, pack(WC)], [],
-        side, first_low, first_high, t1, flops=10**10,
-    )
+    (sent,) = call(
+        side_kernel, "side", [block], [], side, first_low, first_high, flops=10**10,
+    )
+    (down1,) = call(late_kernel, "late", [pack(WC)], [], t1, sent, flops=10**6)
     pairs = [(i, ty + (i - 1) % ty) for i in range(ty)]
     pairs += [(b, a) for a, b in pairs]
-    y = lax.ppermute(y, ("grp", "ty"), pairs)
+    y = lax.ppermute(sent, ("grp", "ty"), pairs)
     high1 = lax.ppermute(down1, "tx", down)
     u0, s0, u1, s1, u2 = call(
         forward_kernel, "forward", [full, full, full, full, tile], [],
         t0, y, first_low, first_high, rest_low, rest_high, flops=10**9,
     )
-    lam1, send = call(
-        adjoint_kernel, "adjoint", [full, tile], [full] * 3,
+    lam1, send, lam, cot, wgt = call(
+        adjoint_kernel, "adjoint", [full, tile, full, full, full], [],
         t1, y, first_low, first_high, high1, u0, s0, u1, s1, u2, flops=10**8,
     )
     other = lax.ppermute(send, "grp", swap)
-    keep_a, keep_s = call(
-        finish_kernel, "finish", [tile, tile], [full] * 2, lam1, u0, s0, u1, u2,
-        flops=10**8,
+    keep_a, keep_s, *_ = call(
+        finish_kernel, "finish", [tile, tile] + [full] * 6, [],
+        s0, u1, s1, lam1, cot, wgt, u0, lam, u2,
+        flops=10**8, aliases={i: i + 2 for i in range(6)},
     )
     adjoints, states = call(
         merge_kernel, "merge", [own.shape, own.shape], [], keep_a, keep_s, other

time: 22.8 us -> 22 us (0.965)
  waiting for transfers between devices: 3.42 us -> 2.52 us
    ppermute x1, waiting for transfers between devices: 0.81 us -> 0.05 us  [shards(): other = lax.ppermute(send, 'grp', swap)]
    pallas_call x9 -> x10, Pallas kernels: 6.31 us -> 6.37 us  [call(): pl.pallas_call(kernel, out_shape=shapes, name=name, scratch_shapes=[pltpu...]
  transfers between devices with their start and end apart: 8 -> 8, of which waited for: 5 -> 4; matrix products, arithmetic and copies ran while one was open for 0% -> 0% of each run, Pallas kernels for 16% -> 18%
where the time goes in v6:
time: 22 us; the launch traced here: 21.8 us
  starting transfers between devices  11.3 us (51%)
  Pallas kernels  6.37 us (29%)
  waiting for transfers between devices  2.52 us (11%)
  local copies, waits for them, and re-layouts  0.97 us (4%)
  between operations  0.71 us (3%)
    pallas_call x10, Pallas kernels, call(): pl.pallas_call(kernel, out_shape=shapes, name=name, scratch_shapes=[pltpu...  6.37 us
    ppermute x1, starting transfers between devices, shards(): first_low = lax.ppermute(first_up, 'tx', up)  2.91 us
    ppermute x1, starting transfers between devices, shards(): y = lax.ppermute(sent, ('grp', 'ty'), pairs)  2.56 us
    ppermute x1, starting transfers between devices, shards(): rest_high = lax.ppermute(rest_down, 'tx', down)  1.92 us
    ppermute x1, waiting for transfers between devices, shards(): rest_high = lax.ppermute(rest_down, 'tx', down)  1.52 us
    ppermute x1, starting transfers between devices, shards(): high1 = lax.ppermute(down1, 'tx', down)  1.19 us
    ppermute x1, starting transfers between devices, shards(): rest_low = lax.ppermute(rest_up, 'tx', up)  1.06 us
    ppermute x1, starting transfers between devices, shards(): first_high = lax.ppermute(first_down, 'tx', down)  1.02 us
  transfers between devices with their start and end apart: 8, of which 4 were waited for; matrix products, arithmetic and copies ran while one was open for 0% of the time, Pallas kernels for 18%

profile of v6, /device:TPU:0, one launch (start us, length us, event | category | flops | bytes accessed | tf_op | source)
XLA Modules:
  0.0 21.8 jit_solution(1880878083781307160)
XLA Ops:
  0.6 0.5 %collective-permute-start = (f32[640,128]{1,0:T(8,128)}, f32[640,128]{1,0:T(8,128)S(1)}, u32[]{:S(2)}, u32[]{:S(2)}) collective-permute-start(f32[640,128]{1,0:T(8,128)} %bitcast.3), channel_id=1, source_target_pairs={{0,16},{16,0},{1,17},{17,1},{2,18},{18,2},{3,19},{19,3},{4,20},{20... | collective-permute-start | bytes 983048 | tf_op jit(solution)/shard_map/ppermute | solution.py:501
  1.1 1.0 %copy-done = f32[1,5,16,8,128]{4,3,2,1,0:T(8,128)S(1)} copy-done((f32[1,5,16,8,128]{4,3,2,1,0:T(8,128)S(1)}, f32[1,5,16,8,128]{4,3,2,1,0:T(8,128)}, u32[]{:S(2)}) %copy-start) | copy-done | bytes 327704
  2.1 0.1 own.1
  2.2 0.4 %collective-permute-done.got = f32[640,128]{1,0:T(8,128)S(1)} collective-permute-done((f32[640,128]{1,0:T(8,128)}, f32[640,128]{1,0:T(8,128)S(1)}, u32[]{:S(2)}, u32[]{:S(2)}) %collective-permute-start) | collective-permute-done | bytes 327712 | tf_op jit(solution)/shard_map/ppermute | solution.py:501
  2.6 0.3 %first.1 = (f32[8,5,2,8,128]{4,3,2,1,0:T(8,128)S(1)}, f32[8,5,2,8,128]{4,3,2,1,0:T(8,128)S(1)}, f32[25,8,128]{2,1,0:T(8,128)S(1)}, f32[5,8,128]{2,1,0:T(8,128)S(1)}) custom-call(f32[8,5,2,8,128]{4,3,2,1,0:T(8,128)S(1)} %own.1, f32[640,128]{1,0:T(8,128)S(1)} %collective-permute-done.got), custom_call_target="tpu_custom_call" | custom-call | flops 1000000 | bytes 655360 | tf_op jit(solution)/shard_map/first/pallas_call | solution.py:469
  2.9 2.9 %collective-permute-start.1 = (f32[25,8,128]{2,1,0:T(8,128)S(1)}, f32[25,8,128]{2,1,0:T(8,128)S(1)}, u32[]{:S(2)}, u32[]{:S(2)}) collective-permute-start(f32[25,8,128]{2,1,0:T(8,128)S(1)} %get-tuple-element.24), channel_id=1, source_target_pairs={{0,4},{4,8},{8,12},{12,0},{1,5},{5,9},{9,13},{13,1},{2,6},{6,10},{... | collective-permute-start | bytes 307208 | tf_op jit(solution)/shard_map/ppermute | solution.py:507
  5.8 1.0 %collective-permute-start.2 = (f32[5,8,128]{2,1,0:T(8,128)S(1)}, f32[5,8,128]{2,1,0:T(8,128)S(1)}, u32[]{:S(2)}, u32[]{:S(2)}) collective-permute-start(f32[5,8,128]{2,1,0:T(8,128)S(1)} %get-tuple-element.25), channel_id=1, source_target_pairs={{0,12},{4,0},{8,4},{12,8},{1,13},{5,1},{9,5},{13,9},{2,14},{6,2},{... | collective-permute-start | bytes 61448 | tf_op jit(solution)/shard_map/ppermute | solution.py:508
  6.8 0.1 rest.1
  7.0 1.1 %collective-permute-start.4 = (f32[30,8,128]{2,1,0:T(8,128)S(1)}, f32[30,8,128]{2,1,0:T(8,128)S(1)}, u32[]{:S(2)}, u32[]{:S(2)}) collective-permute-start(f32[30,8,128]{2,1,0:T(8,128)S(1)} %get-tuple-element.26), channel_id=1, source_target_pairs={{0,4},{4,8},{8,12},{12,0},{1,5},{5,9},{9,13},{13,1},{2,6},{6,10},{... | collective-permute-start | bytes 368648 | tf_op jit(solution)/shard_map/ppermute | solution.py:513
  8.0 1.9 %collective-permute-start.5 = (f32[30,8,128]{2,1,0:T(8,128)S(1)}, f32[30,8,128]{2,1,0:T(8,128)S(1)}, u32[]{:S(2)}, u32[]{:S(2)}) collective-permute-start(f32[30,8,128]{2,1,0:T(8,128)S(1)} %get-tuple-element.27), channel_id=1, source_target_pairs={{0,12},{4,0},{8,4},{12,8},{1,13},{5,1},{9,5},{13,9},{2,14},{6,2},{... | collective-permute-start | bytes 368648 | tf_op jit(solution)/shard_map/ppermute | solution.py:514
  9.9 0.2 %tile.1.side = f32[5,2,8,128]{3,2,1,0:T(8,128)S(1)} custom-call(f32[8,5,2,8,128]{4,3,2,1,0:T(8,128)S(1)} %get-tuple-element.22.t0, f32[8,5,2,8,128]{4,3,2,1,0:T(8,128)S(1)} %get-tuple-element.23.t1), custom_call_target="tpu_custom_call" | custom-call | flops 10000000 | bytes 655360 | tf_op jit(solution)/shard_map/tile/pallas_call | solution.py:469
  10.2 0.5 %collective-permute-done.2.high.first_high = f32[5,8,128]{2,1,0:T(8,128)S(1)} collective-permute-done((f32[5,8,128]{2,1,0:T(8,128)S(1)}, f32[5,8,128]{2,1,0:T(8,128)S(1)}, u32[]{:S(2)}, u32[]{:S(2)}) %collective-permute-start.2) | collective-permute-done | bytes 20512 | tf_op jit(solution)/shard_map/ppermute | solution.py:508
  10.7 2.6 %collective-permute-start.3 = (f32[5,2,8,128]{3,2,1,0:T(8,128)S(1)}, f32[5,2,8,128]{3,2,1,0:T(8,128)S(1)}, u32[]{:S(2)}, u32[]{:S(2)}) collective-permute-start(f32[5,2,8,128]{3,2,1,0:T(8,128)S(1)} %side.1.y), channel_id=1, source_target_pairs={{0,19},{1,16},{2,17},{3,18},{19,0},{16,1},{17,2},{18,3},{4,23},{5,... | collective-permute-start | bytes 122888 | tf_op jit(solution)/shard_map/ppermute | solution.py:521
  13.2 0.1 late.1
  13.3 1.2 %collective-permute-start.6 = (f32[20,8,128]{2,1,0:T(8,128)S(1)}, f32[20,8,128]{2,1,0:T(8,128)S(1)}, u32[]{:S(2)}, u32[]{:S(2)}) collective-permute-start(f32[20,8,128]{2,1,0:T(8,128)S(1)} %late.1), channel_id=1, source_target_pairs={{0,12},{4,0},{8,4},{12,8},{1,13},{5,1},{9,5},{13,9},{2,14},{6,2},{... | collective-permute-start | bytes 245768 | tf_op jit(solution)/shard_map/ppermute | solution.py:522
  14.5 1.5 %collective-permute-done.5.rest_high = f32[30,8,128]{2,1,0:T(8,128)S(1)} collective-permute-done((f32[30,8,128]{2,1,0:T(8,128)S(1)}, f32[30,8,128]{2,1,0:T(8,128)S(1)}, u32[]{:S(2)}, u32[]{:S(2)}) %collective-permute-start.5) | collective-permute-done | bytes 122912 | tf_op jit(solution)/shard_map/ppermute | solution.py:514
  16.0 0.1 collective-permute-done.3.y
  16.1 1.9 %forward.1 = (f32[20,5,2,8,128]{4,3,2,1,0:T(8,128)S(1)}, f32[20,5,2,8,128]{4,3,2,1,0:T(8,128)S(1)}, f32[20,5,2,8,128]{4,3,2,1,0:T(8,128)S(1)}, f32[20,5,2,8,128]{4,3,2,1,0:T(8,128)S(1)}, f32[8,5,2,8,128]{4,3,2,1,0:T(8,128)S(1)}) custom-call(f32[8,5,2,8,128]{4,3,2,1,0:T(8,128)S(1)} %get-tuple-element.22.t0, f32[5,2,8,128]{3,2,1,0:T(8,128)S(1)} %collective-permute-done.3.y, ...), custom_call_target="tpu_custom_call" | custom-call | flops 1000000000 | bytes 737280 | tf_op jit(solution)/shard_map/forward/pallas_call | solution.py:469
  18.0 0.0 collective-permute-done.6.high
  18.0 1.1 %adjoint.1 = (f32[20,5,2,8,128]{4,3,2,1,0:T(8,128)S(1)}, f32[8,5,2,8,128]{4,3,2,1,0:T(8,128)S(1)}, f32[20,5,2,8,128]{4,3,2,1,0:T(8,128)S(1)}, f32[20,5,2,8,128]{4,3,2,1,0:T(8,128)S(1)}, f32[20,5,2,8,128]{4,3,2,1,0:T(8,128)S(1)}) custom-call(f32[8,5,2,8,128]{4,3,2,1,0:T(8,128)S(1)} %get-tuple-element.23.t1, f32[5,2,8,128]{3,2,1,0:T(8,128)S(1)} %collective-permute-done.3.y, ...), custom_call_target="tpu_custom_call" | custom-call | flops 100000000 | bytes 4177920 | tf_op jit(solution)/shard_map/adjoint/pallas_call | solution.py:469
  19.2 0.1 collective-permute-start.7
  19.2 1.6 %finish.1 = (f32[8,5,2,8,128]{4,3,2,1,0:T(8,128)S(1)}, f32[8,5,2,8,128]{4,3,2,1,0:T(8,128)S(1)}, f32[20,5,2,8,128]{4,3,2,1,0:T(8,128)S(1)}, f32[20,5,2,8,128]{4,...) custom-call(f32[20,5,2,8,128]{4,3,2,1,0:T(8,128)S(1)} %get-tuple-ele, ...), custom_call_target="tpu_custom_call", output_to_operand_aliasing={{2}: (0, {}), {3}: (1, {}), {4}: (2, {}), {5}: (3, {}), {6}... | custom-call | flops 100000000 | bytes 6881280 | tf_op jit(solution)/shard_map/finish/pallas_call | solution.py:469
  20.8 0.0 collective-permute-done.7.got
  20.9 1.0 %merge.1 = (f32[640,128]{1,0:T(8,128)}, f32[640,128]{1,0:T(8,128)}) custom-call(f32[8,5,2,8,128]{4,3,2,1,0:T(8,128)S(1)} %get-tuple-element.37.keep_a, f32[8,5,2,8,128]{4,3,2,1,0:T(8,128)S(1)} %get-tuple-element.38.keep_s, f32[8,5,2,8,128]{4,3,2,1,0:T(8,128)S(1)} %collective-permute-done.7.got), custom_call_target="tpu_custom_call" | custom-call | bytes 983040 | tf_op jit(solution)/shard_map/merge/pallas_call | solution.py:469
  (4 shorter events, 0.0 us)
Async XLA Ops:
  0.6 2.0 %collective-permute-start = (f32[640,128]{1,0:T(8,128)}, f32[640,128]{1,0:T(8,128)S(1)}, u32[]{:S(2)}, u32[]{:S(2)}) collective-permute-start(f32[640,128]{1,0:T(8,128)} %bitcast.3), channel_id=1, source_target_pairs={{0,16},{16,0},{1,17},{17,1},{2,18},{18,2},{3,19},{19,3},{4,20},{20... | collective-permute-start | bytes 983048 | tf_op jit(solution)/shard_map/ppermute | solution.py:501
  1.1 1.0 %copy-start = (f32[1,5,16,8,128]{4,3,2,1,0:T(8,128)S(1)}, f32[1,5,16,8,128]{4,3,2,1,0:T(8,128)}, u32[]{:S(2)}) copy-start(f32[1,5,16,8,128]{4,3,2,1,0:T(8,128)} %param.1) | copy-start | bytes 983044
  2.9 7.8 %collective-permute-start.1 = (f32[25,8,128]{2,1,0:T(8,128)S(1)}, f32[25,8,128]{2,1,0:T(8,128)S(1)}, u32[]{:S(2)}, u32[]{:S(2)}) collective-permute-start(f32[25,8,128]{2,1,0:T(8,128)S(1)} %get-tuple-element.24), channel_id=1, source_target_pairs={{0,4},{4,8},{8,12},{12,0},{1,5},{5,9},{9,13},{13,1},{2,6},{6,10},{... | collective-permute-start | bytes 307208 | tf_op jit(solution)/shard_map/ppermute | solution.py:507
  5.8 4.8 %collective-permute-start.2 = (f32[5,8,128]{2,1,0:T(8,128)S(1)}, f32[5,8,128]{2,1,0:T(8,128)S(1)}, u32[]{:S(2)}, u32[]{:S(2)}) collective-permute-start(f32[5,8,128]{2,1,0:T(8,128)S(1)} %get-tuple-element.25), channel_id=1, source_target_pairs={{0,12},{4,0},{8,4},{12,8},{1,13},{5,1},{9,5},{13,9},{2,14},{6,2},{... | collective-permute-start | bytes 61448 | tf_op jit(solution)/shard_map/ppermute | solution.py:508
  7.0 7.6 %collective-permute-start.4 = (f32[30,8,128]{2,1,0:T(8,128)S(1)}, f32[30,8,128]{2,1,0:T(8,128)S(1)}, u32[]{:S(2)}, u32[]{:S(2)}) collective-permute-start(f32[30,8,128]{2,1,0:T(8,128)S(1)} %get-tuple-element.26), channel_id=1, source_target_pairs={{0,4},{4,8},{8,12},{12,0},{1,5},{5,9},{9,13},{13,1},{2,6},{6,10},{... | collective-permute-start | bytes 368648 | tf_op jit(solution)/shard_map/ppermute | solution.py:513
  8.0 8.0 %collective-permute-start.5 = (f32[30,8,128]{2,1,0:T(8,128)S(1)}, f32[30,8,128]{2,1,0:T(8,128)S(1)}, u32[]{:S(2)}, u32[]{:S(2)}) collective-permute-start(f32[30,8,128]{2,1,0:T(8,128)S(1)} %get-tuple-element.27), channel_id=1, source_target_pairs={{0,12},{4,0},{8,4},{12,8},{1,13},{5,1},{9,5},{13,9},{2,14},{6,2},{... | collective-permute-start | bytes 368648 | tf_op jit(solution)/shard_map/ppermute | solution.py:514
  10.7 5.5 %collective-permute-start.3 = (f32[5,2,8,128]{3,2,1,0:T(8,128)S(1)}, f32[5,2,8,128]{3,2,1,0:T(8,128)S(1)}, u32[]{:S(2)}, u32[]{:S(2)}) collective-permute-start(f32[5,2,8,128]{3,2,1,0:T(8,128)S(1)} %side.1.y), channel_id=1, source_target_pairs={{0,19},{1,16},{2,17},{3,18},{19,0},{16,1},{17,2},{18,3},{4,23},{5,... | collective-permute-start | bytes 122888 | tf_op jit(solution)/shard_map/ppermute | solution.py:521
  13.3 4.7 %collective-permute-start.6 = (f32[20,8,128]{2,1,0:T(8,128)S(1)}, f32[20,8,128]{2,1,0:T(8,128)S(1)}, u32[]{:S(2)}, u32[]{:S(2)}) collective-permute-start(f32[20,8,128]{2,1,0:T(8,128)S(1)} %late.1), channel_id=1, source_target_pairs={{0,12},{4,0},{8,4},{12,8},{1,13},{5,1},{9,5},{13,9},{2,14},{6,2},{... | collective-permute-start | bytes 245768 | tf_op jit(solution)/shard_map/ppermute | solution.py:522
  19.2 1.7 %collective-permute-start.7 = (f32[8,5,2,8,128]{4,3,2,1,0:T(8,128)S(1)}, f32[8,5,2,8,128]{4,3,2,1,0:T(8,128)S(1)}, u32[]{:S(2)}, u32[]{:S(2)}) collective-permute-start(f32[8,5,2,8,128]{4,3,2,1,0:T(8,128)S(1)} %get-tuple-element.39), channel_id=1, source_target_pairs={{0,16},{16,0},{1,17},{17,1},{2,18},{18,2},{3,19},{19,3},{4,20},{20... | collective-permute-start | bytes 983048 | tf_op jit(solution)/shard_map/ppermute | solution.py:531

commit v7 on v6

--- a/solution.py
+++ b/solution.py
@@ -361,7 +361,7 @@
 
 
 def send_block(out, i, f, k, lam, state, mine):
-    out[i, f, k] = jnp.where(mine, lam, turn(state, HALF))
+    out[i, f, k] = jnp.where(mine, lam, state[i, f, k])
 
 
 def last_step(s0, u0, lam1, cot, wgt, emit):
@@ -396,7 +396,7 @@
 
 def adjoint_kernel(
     t1, y, first_low, first_high, high, u0, s0, u1, s1, u2,
-    lam1, send, lam, cot, wgt,
+    lam1, send, lam, cot, wgt, moved,
 ):
     make = row_maker(
         1, t1, y, (first_low, first_high),
@@ -411,20 +411,24 @@
         v = make(r - (WS - WC))
         for f, k in FK:
             lam[r, f, k] = v[k][f]
+    for i in range(ROWS):
+        for f, k in FK:
+            away = jnp.where(core == 0, u2[i, f, k], u1[WS + i, f, k])
+            moved[i, f, k] = turn(away, HALF)
     first_step(s1, u1, lam, cot, wgt, lam1, INNER)
 
     @pl.when(core == 0)
     def _():
         for i in range(ROWS):
             for f, k in FK:
-                send_block(send, i, f, k, lam1[WS + i, f, k], u2[i, f, k], mine)
+                send_block(send, i, f, k, lam1[WS + i, f, k], moved, mine)
 
     @pl.when(core == 1)
     def _():
         first_step(s1, u1, lam, cot, wgt, lam1, OUTER)
         last_step(
             s0, u0, lam1, cot, wgt,
-            lambda i, f, k, x: send_block(send, i, f, k, x, u1[WS + i, f, k], mine),
+            lambda i, f, k, x: send_block(send, i, f, k, x, moved, mine),
         )
 
 
@@ -525,7 +529,7 @@
         t0, y, first_low, first_high, rest_low, rest_high, flops=10**9,
     )
     lam1, send, lam, cot, wgt = call(
-        adjoint_kernel, "adjoint", [full, tile, full, full, full], [],
+        adjoint_kernel, "adjoint", [full, tile, full, full, full], [tile],
         t1, y, first_low, first_high, high1, u0, s0, u1, s1, u2, flops=10**8,
     )
     other = lax.ppermute(send, "grp", swap)

time: 22 us -> 21.9 us (level)
  no operation moved by 1% of the time
where the time goes in v7:
time: 21.9 us; the launch traced here: 21.8 us
  starting transfers between devices  11.3 us (52%)
  Pallas kernels  6.33 us (29%)
  waiting for transfers between devices  2.52 us (12%)
  local copies, waits for them, and re-layouts  0.97 us (4%)
  between operations  0.71 us (3%)
    pallas_call x10, Pallas kernels, call(): pl.pallas_call(kernel, out_shape=shapes, name=name, scratch_shapes=[pltpu...  6.33 us
    ppermute x1, starting transfers between devices, shards(): first_low = lax.ppermute(first_up, 'tx', up)  2.91 us
    ppermute x1, starting transfers between devices, shards(): y = lax.ppermute(sent, ('grp', 'ty'), pairs)  2.56 us
    ppermute x1, starting transfers between devices, shards(): rest_high = lax.ppermute(rest_down, 'tx', down)  1.92 us
    ppermute x1, waiting for transfers between devices, shards(): rest_high = lax.ppermute(rest_down, 'tx', down)  1.52 us
    ppermute x1, starting transfers between devices, shards(): high1 = lax.ppermute(down1, 'tx', down)  1.19 us
    ppermute x1, starting transfers between devices, shards(): rest_low = lax.ppermute(rest_up, 'tx', up)  1.06 us
    ppermute x1, starting transfers between devices, shards(): first_high = lax.ppermute(first_down, 'tx', down)  1.02 us
  transfers between devices with their start and end apart: 8, of which 4 were waited for; matrix products, arithmetic and copies ran while one was open for 0% of the time, Pallas kernels for 18%

profile of v7, /device:TPU:0, one launch (start us, length us, event | category | flops | bytes accessed | tf_op | source)
XLA Modules:
  0.0 21.8 jit_solution(16460229159990764464)
XLA Ops:
  0.6 0.5 %collective-permute-start = (f32[640,128]{1,0:T(8,128)}, f32[640,128]{1,0:T(8,128)S(1)}, u32[]{:S(2)}, u32[]{:S(2)}) collective-permute-start(f32[640,128]{1,0:T(8,128)} %bitcast.3), channel_id=1, source_target_pairs={{0,16},{16,0},{1,17},{17,1},{2,18},{18,2},{3,19},{19,3},{4,20},{20... | collective-permute-start | bytes 983048 | tf_op jit(solution)/shard_map/ppermute | solution.py:505
  1.1 1.0 %copy-done = f32[1,5,16,8,128]{4,3,2,1,0:T(8,128)S(1)} copy-done((f32[1,5,16,8,128]{4,3,2,1,0:T(8,128)S(1)}, f32[1,5,16,8,128]{4,3,2,1,0:T(8,128)}, u32[]{:S(2)}) %copy-start) | copy-done | bytes 327704
  2.1 0.1 own.1
  2.2 0.4 %collective-permute-done.got = f32[640,128]{1,0:T(8,128)S(1)} collective-permute-done((f32[640,128]{1,0:T(8,128)}, f32[640,128]{1,0:T(8,128)S(1)}, u32[]{:S(2)}, u32[]{:S(2)}) %collective-permute-start) | collective-permute-done | bytes 327712 | tf_op jit(solution)/shard_map/ppermute | solution.py:505
  2.6 0.3 %first.1 = (f32[8,5,2,8,128]{4,3,2,1,0:T(8,128)S(1)}, f32[8,5,2,8,128]{4,3,2,1,0:T(8,128)S(1)}, f32[25,8,128]{2,1,0:T(8,128)S(1)}, f32[5,8,128]{2,1,0:T(8,128)S(1)}) custom-call(f32[8,5,2,8,128]{4,3,2,1,0:T(8,128)S(1)} %own.1, f32[640,128]{1,0:T(8,128)S(1)} %collective-permute-done.got), custom_call_target="tpu_custom_call" | custom-call | flops 1000000 | bytes 655360 | tf_op jit(solution)/shard_map/first/pallas_call | solution.py:473
  2.9 2.9 %collective-permute-start.1 = (f32[25,8,128]{2,1,0:T(8,128)S(1)}, f32[25,8,128]{2,1,0:T(8,128)S(1)}, u32[]{:S(2)}, u32[]{:S(2)}) collective-permute-start(f32[25,8,128]{2,1,0:T(8,128)S(1)} %get-tuple-element.24), channel_id=1, source_target_pairs={{0,4},{4,8},{8,12},{12,0},{1,5},{5,9},{9,13},{13,1},{2,6},{6,10},{... | collective-permute-start | bytes 307208 | tf_op jit(solution)/shard_map/ppermute | solution.py:511
  5.8 1.0 %collective-permute-start.2 = (f32[5,8,128]{2,1,0:T(8,128)S(1)}, f32[5,8,128]{2,1,0:T(8,128)S(1)}, u32[]{:S(2)}, u32[]{:S(2)}) collective-permute-start(f32[5,8,128]{2,1,0:T(8,128)S(1)} %get-tuple-element.25), channel_id=1, source_target_pairs={{0,12},{4,0},{8,4},{12,8},{1,13},{5,1},{9,5},{13,9},{2,14},{6,2},{... | collective-permute-start | bytes 61448 | tf_op jit(solution)/shard_map/ppermute | solution.py:512
  6.8 0.1 rest.1
  7.0 1.1 %collective-permute-start.4 = (f32[30,8,128]{2,1,0:T(8,128)S(1)}, f32[30,8,128]{2,1,0:T(8,128)S(1)}, u32[]{:S(2)}, u32[]{:S(2)}) collective-permute-start(f32[30,8,128]{2,1,0:T(8,128)S(1)} %get-tuple-element.26), channel_id=1, source_target_pairs={{0,4},{4,8},{8,12},{12,0},{1,5},{5,9},{9,13},{13,1},{2,6},{6,10},{... | collective-permute-start | bytes 368648 | tf_op jit(solution)/shard_map/ppermute | solution.py:517
  8.0 1.9 %collective-permute-start.5 = (f32[30,8,128]{2,1,0:T(8,128)S(1)}, f32[30,8,128]{2,1,0:T(8,128)S(1)}, u32[]{:S(2)}, u32[]{:S(2)}) collective-permute-start(f32[30,8,128]{2,1,0:T(8,128)S(1)} %get-tuple-element.27), channel_id=1, source_target_pairs={{0,12},{4,0},{8,4},{12,8},{1,13},{5,1},{9,5},{13,9},{2,14},{6,2},{... | collective-permute-start | bytes 368648 | tf_op jit(solution)/shard_map/ppermute | solution.py:518
  9.9 0.2 %tile.1.side = f32[5,2,8,128]{3,2,1,0:T(8,128)S(1)} custom-call(f32[8,5,2,8,128]{4,3,2,1,0:T(8,128)S(1)} %get-tuple-element.22.t0, f32[8,5,2,8,128]{4,3,2,1,0:T(8,128)S(1)} %get-tuple-element.23.t1), custom_call_target="tpu_custom_call" | custom-call | flops 10000000 | bytes 655360 | tf_op jit(solution)/shard_map/tile/pallas_call | solution.py:473
  10.2 0.5 %collective-permute-done.2.high.first_high = f32[5,8,128]{2,1,0:T(8,128)S(1)} collective-permute-done((f32[5,8,128]{2,1,0:T(8,128)S(1)}, f32[5,8,128]{2,1,0:T(8,128)S(1)}, u32[]{:S(2)}, u32[]{:S(2)}) %collective-permute-start.2) | collective-permute-done | bytes 20512 | tf_op jit(solution)/shard_map/ppermute | solution.py:512
  10.7 0.0 collective-permute-done.1.low.first_low
  10.7 2.6 %collective-permute-start.3 = (f32[5,2,8,128]{3,2,1,0:T(8,128)S(1)}, f32[5,2,8,128]{3,2,1,0:T(8,128)S(1)}, u32[]{:S(2)}, u32[]{:S(2)}) collective-permute-start(f32[5,2,8,128]{3,2,1,0:T(8,128)S(1)} %side.1.y), channel_id=1, source_target_pairs={{0,19},{1,16},{2,17},{3,18},{19,0},{16,1},{17,2},{18,3},{4,23},{5,... | collective-permute-start | bytes 122888 | tf_op jit(solution)/shard_map/ppermute | solution.py:525
  13.2 0.1 late.1
  13.3 1.2 %collective-permute-start.6 = (f32[20,8,128]{2,1,0:T(8,128)S(1)}, f32[20,8,128]{2,1,0:T(8,128)S(1)}, u32[]{:S(2)}, u32[]{:S(2)}) collective-permute-start(f32[20,8,128]{2,1,0:T(8,128)S(1)} %late.1), channel_id=1, source_target_pairs={{0,12},{4,0},{8,4},{12,8},{1,13},{5,1},{9,5},{13,9},{2,14},{6,2},{... | collective-permute-start | bytes 245768 | tf_op jit(solution)/shard_map/ppermute | solution.py:526
  14.5 1.5 %collective-permute-done.5.rest_high = f32[30,8,128]{2,1,0:T(8,128)S(1)} collective-permute-done((f32[30,8,128]{2,1,0:T(8,128)S(1)}, f32[30,8,128]{2,1,0:T(8,128)S(1)}, u32[]{:S(2)}, u32[]{:S(2)}) %collective-permute-start.5) | collective-permute-done | bytes 122912 | tf_op jit(solution)/shard_map/ppermute | solution.py:518
  16.0 0.1 collective-permute-done.3.y
  16.1 1.9 %forward.1 = (f32[20,5,2,8,128]{4,3,2,1,0:T(8,128)S(1)}, f32[20,5,2,8,128]{4,3,2,1,0:T(8,128)S(1)}, f32[20,5,2,8,128]{4,3,2,1,0:T(8,128)S(1)}, f32[20,5,2,8,128]{4,3,2,1,0:T(8,128)S(1)}, f32[8,5,2,8,128]{4,3,2,1,0:T(8,128)S(1)}) custom-call(f32[8,5,2,8,128]{4,3,2,1,0:T(8,128)S(1)} %get-tuple-element.22.t0, f32[5,2,8,128]{3,2,1,0:T(8,128)S(1)} %collective-permute-done.3.y, ...), custom_call_target="tpu_custom_call" | custom-call | flops 1000000000 | bytes 737280 | tf_op jit(solution)/shard_map/forward/pallas_call | solution.py:473
  18.0 1.1 %adjoint.1 = (f32[20,5,2,8,128]{4,3,2,1,0:T(8,128)S(1)}, f32[8,5,2,8,128]{4,3,2,1,0:T(8,128)S(1)}, f32[20,5,2,8,128]{4,3,2,1,0:T(8,128)S(1)}, f32[20,5,2,8,128]{4,3,2,1,0:T(8,128)S(1)}, f32[20,5,2,8,128]{4,3,2,1,0:T(8,128)S(1)}) custom-call(f32[8,5,2,8,128]{4,3,2,1,0:T(8,128)S(1)} %get-tuple-element.23.t1, f32[5,2,8,128]{3,2,1,0:T(8,128)S(1)} %collective-permute-done.3.y, ...), custom_call_target="tpu_custom_call" | custom-call | flops 100000000 | bytes 4177920 | tf_op jit(solution)/shard_map/adjoint/pallas_call | solution.py:473
  19.1 0.1 collective-permute-start.7
  19.2 1.6 %finish.1 = (f32[8,5,2,8,128]{4,3,2,1,0:T(8,128)S(1)}, f32[8,5,2,8,128]{4,3,2,1,0:T(8,128)S(1)}, f32[20,5,2,8,128]{4,3,2,1,0:T(8,128)S(1)}, f32[20,5,2,8,128]{4,...) custom-call(f32[20,5,2,8,128]{4,3,2,1,0:T(8,128)S(1)} %get-tuple-ele, ...), custom_call_target="tpu_custom_call", output_to_operand_aliasing={{2}: (0, {}), {3}: (1, {}), {4}: (2, {}), {5}: (3, {}), {6}... | custom-call | flops 100000000 | bytes 6881280 | tf_op jit(solution)/shard_map/finish/pallas_call | solution.py:473
  20.8 0.0 collective-permute-done.7.got
  20.8 1.0 %merge.1 = (f32[640,128]{1,0:T(8,128)}, f32[640,128]{1,0:T(8,128)}) custom-call(f32[8,5,2,8,128]{4,3,2,1,0:T(8,128)S(1)} %get-tuple-element.37.keep_a, f32[8,5,2,8,128]{4,3,2,1,0:T(8,128)S(1)} %get-tuple-element.38.keep_s, f32[8,5,2,8,128]{4,3,2,1,0:T(8,128)S(1)} %collective-permute-done.7.got), custom_call_target="tpu_custom_call" | custom-call | bytes 983040 | tf_op jit(solution)/shard_map/merge/pallas_call | solution.py:473
  (4 shorter events, 0.0 us)
Async XLA Ops:
  0.6 2.0 %collective-permute-start = (f32[640,128]{1,0:T(8,128)}, f32[640,128]{1,0:T(8,128)S(1)}, u32[]{:S(2)}, u32[]{:S(2)}) collective-permute-start(f32[640,128]{1,0:T(8,128)} %bitcast.3), channel_id=1, source_target_pairs={{0,16},{16,0},{1,17},{17,1},{2,18},{18,2},{3,19},{19,3},{4,20},{20... | collective-permute-start | bytes 983048 | tf_op jit(solution)/shard_map/ppermute | solution.py:505
  1.1 1.0 %copy-start = (f32[1,5,16,8,128]{4,3,2,1,0:T(8,128)S(1)}, f32[1,5,16,8,128]{4,3,2,1,0:T(8,128)}, u32[]{:S(2)}) copy-start(f32[1,5,16,8,128]{4,3,2,1,0:T(8,128)} %param.1) | copy-start | bytes 983044
  2.9 7.8 %collective-permute-start.1 = (f32[25,8,128]{2,1,0:T(8,128)S(1)}, f32[25,8,128]{2,1,0:T(8,128)S(1)}, u32[]{:S(2)}, u32[]{:S(2)}) collective-permute-start(f32[25,8,128]{2,1,0:T(8,128)S(1)} %get-tuple-element.24), channel_id=1, source_target_pairs={{0,4},{4,8},{8,12},{12,0},{1,5},{5,9},{9,13},{13,1},{2,6},{6,10},{... | collective-permute-start | bytes 307208 | tf_op jit(solution)/shard_map/ppermute | solution.py:511
  5.8 4.8 %collective-permute-start.2 = (f32[5,8,128]{2,1,0:T(8,128)S(1)}, f32[5,8,128]{2,1,0:T(8,128)S(1)}, u32[]{:S(2)}, u32[]{:S(2)}) collective-permute-start(f32[5,8,128]{2,1,0:T(8,128)S(1)} %get-tuple-element.25), channel_id=1, source_target_pairs={{0,12},{4,0},{8,4},{12,8},{1,13},{5,1},{9,5},{13,9},{2,14},{6,2},{... | collective-permute-start | bytes 61448 | tf_op jit(solution)/shard_map/ppermute | solution.py:512
  7.0 7.6 %collective-permute-start.4 = (f32[30,8,128]{2,1,0:T(8,128)S(1)}, f32[30,8,128]{2,1,0:T(8,128)S(1)}, u32[]{:S(2)}, u32[]{:S(2)}) collective-permute-start(f32[30,8,128]{2,1,0:T(8,128)S(1)} %get-tuple-element.26), channel_id=1, source_target_pairs={{0,4},{4,8},{8,12},{12,0},{1,5},{5,9},{9,13},{13,1},{2,6},{6,10},{... | collective-permute-start | bytes 368648 | tf_op jit(solution)/shard_map/ppermute | solution.py:517
  8.0 8.0 %collective-permute-start.5 = (f32[30,8,128]{2,1,0:T(8,128)S(1)}, f32[30,8,128]{2,1,0:T(8,128)S(1)}, u32[]{:S(2)}, u32[]{:S(2)}) collective-permute-start(f32[30,8,128]{2,1,0:T(8,128)S(1)} %get-tuple-element.27), channel_id=1, source_target_pairs={{0,12},{4,0},{8,4},{12,8},{1,13},{5,1},{9,5},{13,9},{2,14},{6,2},{... | collective-permute-start | bytes 368648 | tf_op jit(solution)/shard_map/ppermute | solution.py:518
  10.7 5.5 %collective-permute-start.3 = (f32[5,2,8,128]{3,2,1,0:T(8,128)S(1)}, f32[5,2,8,128]{3,2,1,0:T(8,128)S(1)}, u32[]{:S(2)}, u32[]{:S(2)}) collective-permute-start(f32[5,2,8,128]{3,2,1,0:T(8,128)S(1)} %side.1.y), channel_id=1, source_target_pairs={{0,19},{1,16},{2,17},{3,18},{19,0},{16,1},{17,2},{18,3},{4,23},{5,... | collective-permute-start | bytes 122888 | tf_op jit(solution)/shard_map/ppermute | solution.py:525
  13.3 4.7 %collective-permute-start.6 = (f32[20,8,128]{2,1,0:T(8,128)S(1)}, f32[20,8,128]{2,1,0:T(8,128)S(1)}, u32[]{:S(2)}, u32[]{:S(2)}) collective-permute-start(f32[20,8,128]{2,1,0:T(8,128)S(1)} %late.1), channel_id=1, source_target_pairs={{0,12},{4,0},{8,4},{12,8},{1,13},{5,1},{9,5},{13,9},{2,14},{6,2},{... | collective-permute-start | bytes 245768 | tf_op jit(solution)/shard_map/ppermute | solution.py:526
  19.1 1.7 %collective-permute-start.7 = (f32[8,5,2,8,128]{4,3,2,1,0:T(8,128)S(1)}, f32[8,5,2,8,128]{4,3,2,1,0:T(8,128)S(1)}, u32[]{:S(2)}, u32[]{:S(2)}) collective-permute-start(f32[8,5,2,8,128]{4,3,2,1,0:T(8,128)S(1)} %get-tuple-element.39), channel_id=1, source_target_pairs={{0,16},{16,0},{1,17},{17,1},{2,18},{18,2},{3,19},{19,3},{4,20},{20... | collective-permute-start | bytes 983048 | tf_op jit(solution)/shard_map/ppermute | solution.py:535

commit v8 on v6

--- a/solution.py
+++ b/solution.py
@@ -451,27 +451,35 @@
                 keep_s[i, f, k] = u2[i, f, k]
 
 
-def merge_kernel(keep_a, keep_s, got, out_a, out_s):
+def merge_kernel(keep_a, keep_s, got, out_a, out_s, buf, sem):
     lane, core = lanes()
     mine = owned(lane, core)
-    for f, k in FK:
-        for r in range(ROWS):
-            rows = pl.ds(f * 16 * ROWS + k * ROWS + r, 8, stride=2 * ROWS)
-            other = got[r, f, k]
-            out_a[rows, :] = jnp.where(mine, keep_a[r, f, k], other) * (2.0 * UNIT[f])
-            there = jnp.where(mine, keep_s[r, f, k], turn(other, HALF))
-            out_s[rows, :] = there * (1.0 / UNIT[f])
-
-
-def call(kernel, name, outs, scratch, *args, flops=0, aliases=None):
+    copies = []
+    for i, (keep, out) in enumerate(((keep_a, out_a), (keep_s, out_s))):
+        for f, k in FK:
+            unit = 1.0 / UNIT[f] if i else 2.0 * UNIT[f]
+            for r in range(ROWS):
+                there = turn(got[r, f, k], HALF) if i else got[r, f, k]
+                rows = pl.ds(f * 16 * ROWS + k * ROWS + r, 8, stride=2 * ROWS)
+                buf[i, rows, :] = jnp.where(mine, keep[r, f, k], there) * unit
+        copies.append(pltpu.make_async_copy(buf.at[i], out, sem.at[i]))
+        copies[i].start()
+    for copy in copies:
+        copy.wait()
+
+
+def call(kernel, name, outs, scratch, *args, flops=0, aliases=None, **specs):
     shapes = [jax.ShapeDtypeStruct(s, jnp.float32) for s in outs]
     size = 4 * sum(a.size for a in args)
     return pl.pallas_call(
         kernel,
         out_shape=shapes,
         name=name,
-        scratch_shapes=[pltpu.VMEM(s, jnp.float32) for s in scratch],
+        scratch_shapes=[
+            pltpu.VMEM(s, jnp.float32) if isinstance(s, tuple) else s for s in scratch
+        ],
         input_output_aliases=aliases or {},
+        **specs,
         compiler_params=pltpu.CompilerParams(vmem_limit_bytes=VMEM_LIMIT),
         cost_estimate=pl.CostEstimate(flops=flops, bytes_accessed=size, transcendentals=0),
     )(*args)
@@ -535,7 +543,9 @@
         flops=10**8, aliases={i: i + 2 for i in range(6)},
     )
     adjoints, states = call(
-        merge_kernel, "merge", [own.shape, own.shape], [], keep_a, keep_s, other
+        merge_kernel, "merge", [own.shape, own.shape],
+        [(2,) + own.shape, pltpu.SemaphoreType.DMA((2,))],
+        keep_a, keep_s, other, out_specs=[pl.BlockSpec(memory_space=pl.ANY)] * 2,
     )
     return adjoints.reshape(shape), states.reshape(shape)
 

time: 22 us -> 22 us (level)
  no operation moved by 1% of the time
where the time goes in v8:
time: 22 us; the launch traced here: 21.8 us
  starting transfers between devices  11.3 us (51%)
  Pallas kernels  6.37 us (29%)
  waiting for transfers between devices  2.52 us (11%)
  local copies, waits for them, and re-layouts  0.97 us (4%)
  between operations  0.71 us (3%)
    pallas_call x10, Pallas kernels, call(): pl.pallas_call(kernel, out_shape=shapes, name=name, scratch_shapes=[pltpu...  6.37 us
    ppermute x1, starting transfers between devices, shards(): first_low = lax.ppermute(first_up, 'tx', up)  2.91 us
    ppermute x1, starting transfers between devices, shards(): y = lax.ppermute(sent, ('grp', 'ty'), pairs)  2.56 us
    ppermute x1, starting transfers between devices, shards(): rest_high = lax.ppermute(rest_down, 'tx', down)  1.92 us
    ppermute x1, waiting for transfers between devices, shards(): rest_high = lax.ppermute(rest_down, 'tx', down)  1.52 us
    ppermute x1, starting transfers between devices, shards(): high1 = lax.ppermute(down1, 'tx', down)  1.19 us
    ppermute x1, starting transfers between devices, shards(): rest_low = lax.ppermute(rest_up, 'tx', up)  1.06 us
    ppermute x1, starting transfers between devices, shards(): first_high = lax.ppermute(first_down, 'tx', down)  1.02 us
  transfers between devices with their start and end apart: 8, of which 4 were waited for; matrix products, arithmetic and copies ran while one was open for 0% of the time, Pallas kernels for 18%

profile of v8, /device:TPU:0, one launch (start us, length us, event | category | flops | bytes accessed | tf_op | source)
XLA Modules:
  0.0 21.8 jit_solution(9904582508182457032)
XLA Ops:
  0.6 0.5 %collective-permute-start = (f32[640,128]{1,0:T(8,128)}, f32[640,128]{1,0:T(8,128)S(1)}, u32[]{:S(2)}, u32[]{:S(2)}) collective-permute-start(f32[640,128]{1,0:T(8,128)} %bitcast.3), channel_id=1, source_target_pairs={{0,16},{16,0},{1,17},{17,1},{2,18},{18,2},{3,19},{19,3},{4,20},{20... | collective-permute-start | bytes 983048 | tf_op jit(solution)/shard_map/ppermute | solution.py:509
  1.1 1.0 %copy-done = f32[1,5,16,8,128]{4,3,2,1,0:T(8,128)S(1)} copy-done((f32[1,5,16,8,128]{4,3,2,1,0:T(8,128)S(1)}, f32[1,5,16,8,128]{4,3,2,1,0:T(8,128)}, u32[]{:S(2)}) %copy-start) | copy-done | bytes 327704
  2.1 0.1 own.1
  2.2 0.4 %collective-permute-done.got = f32[640,128]{1,0:T(8,128)S(1)} collective-permute-done((f32[640,128]{1,0:T(8,128)}, f32[640,128]{1,0:T(8,128)S(1)}, u32[]{:S(2)}, u32[]{:S(2)}) %collective-permute-start) | collective-permute-done | bytes 327712 | tf_op jit(solution)/shard_map/ppermute | solution.py:509
  2.6 0.3 %first.1 = (f32[8,5,2,8,128]{4,3,2,1,0:T(8,128)S(1)}, f32[8,5,2,8,128]{4,3,2,1,0:T(8,128)S(1)}, f32[25,8,128]{2,1,0:T(8,128)S(1)}, f32[5,8,128]{2,1,0:T(8,128)S(1)}) custom-call(f32[8,5,2,8,128]{4,3,2,1,0:T(8,128)S(1)} %own.1, f32[640,128]{1,0:T(8,128)S(1)} %collective-permute-done.got), custom_call_target="tpu_custom_call" | custom-call | flops 1000000 | bytes 655360 | tf_op jit(solution)/shard_map/first/pallas_call | solution.py:474
  2.9 2.9 %collective-permute-start.1 = (f32[25,8,128]{2,1,0:T(8,128)S(1)}, f32[25,8,128]{2,1,0:T(8,128)S(1)}, u32[]{:S(2)}, u32[]{:S(2)}) collective-permute-start(f32[25,8,128]{2,1,0:T(8,128)S(1)} %get-tuple-element.24), channel_id=1, source_target_pairs={{0,4},{4,8},{8,12},{12,0},{1,5},{5,9},{9,13},{13,1},{2,6},{6,10},{... | collective-permute-start | bytes 307208 | tf_op jit(solution)/shard_map/ppermute | solution.py:515
  5.8 1.0 %collective-permute-start.2 = (f32[5,8,128]{2,1,0:T(8,128)S(1)}, f32[5,8,128]{2,1,0:T(8,128)S(1)}, u32[]{:S(2)}, u32[]{:S(2)}) collective-permute-start(f32[5,8,128]{2,1,0:T(8,128)S(1)} %get-tuple-element.25), channel_id=1, source_target_pairs={{0,12},{4,0},{8,4},{12,8},{1,13},{5,1},{9,5},{13,9},{2,14},{6,2},{... | collective-permute-start | bytes 61448 | tf_op jit(solution)/shard_map/ppermute | solution.py:516
  6.8 0.1 rest.1
  7.0 1.1 %collective-permute-start.4 = (f32[30,8,128]{2,1,0:T(8,128)S(1)}, f32[30,8,128]{2,1,0:T(8,128)S(1)}, u32[]{:S(2)}, u32[]{:S(2)}) collective-permute-start(f32[30,8,128]{2,1,0:T(8,128)S(1)} %get-tuple-element.26), channel_id=1, source_target_pairs={{0,4},{4,8},{8,12},{12,0},{1,5},{5,9},{9,13},{13,1},{2,6},{6,10},{... | collective-permute-start | bytes 368648 | tf_op jit(solution)/shard_map/ppermute | solution.py:521
  8.0 1.9 %collective-permute-start.5 = (f32[30,8,128]{2,1,0:T(8,128)S(1)}, f32[30,8,128]{2,1,0:T(8,128)S(1)}, u32[]{:S(2)}, u32[]{:S(2)}) collective-permute-start(f32[30,8,128]{2,1,0:T(8,128)S(1)} %get-tuple-element.27), channel_id=1, source_target_pairs={{0,12},{4,0},{8,4},{12,8},{1,13},{5,1},{9,5},{13,9},{2,14},{6,2},{... | collective-permute-start | bytes 368648 | tf_op jit(solution)/shard_map/ppermute | solution.py:522
  9.9 0.2 %tile.1.side = f32[5,2,8,128]{3,2,1,0:T(8,128)S(1)} custom-call(f32[8,5,2,8,128]{4,3,2,1,0:T(8,128)S(1)} %get-tuple-element.22.t0, f32[8,5,2,8,128]{4,3,2,1,0:T(8,128)S(1)} %get-tuple-element.23.t1), custom_call_target="tpu_custom_call" | custom-call | flops 10000000 | bytes 655360 | tf_op jit(solution)/shard_map/tile/pallas_call | solution.py:474
  10.2 0.5 %collective-permute-done.2.high.first_high = f32[5,8,128]{2,1,0:T(8,128)S(1)} collective-permute-done((f32[5,8,128]{2,1,0:T(8,128)S(1)}, f32[5,8,128]{2,1,0:T(8,128)S(1)}, u32[]{:S(2)}, u32[]{:S(2)}) %collective-permute-start.2) | collective-permute-done | bytes 20512 | tf_op jit(solution)/shard_map/ppermute | solution.py:516
  10.7 2.6 %collective-permute-start.3 = (f32[5,2,8,128]{3,2,1,0:T(8,128)S(1)}, f32[5,2,8,128]{3,2,1,0:T(8,128)S(1)}, u32[]{:S(2)}, u32[]{:S(2)}) collective-permute-start(f32[5,2,8,128]{3,2,1,0:T(8,128)S(1)} %side.1.y), channel_id=1, source_target_pairs={{0,19},{1,16},{2,17},{3,18},{19,0},{16,1},{17,2},{18,3},{4,23},{5,... | collective-permute-start | bytes 122888 | tf_op jit(solution)/shard_map/ppermute | solution.py:529
  13.2 0.1 late.1
  13.3 1.2 %collective-permute-start.6 = (f32[20,8,128]{2,1,0:T(8,128)S(1)}, f32[20,8,128]{2,1,0:T(8,128)S(1)}, u32[]{:S(2)}, u32[]{:S(2)}) collective-permute-start(f32[20,8,128]{2,1,0:T(8,128)S(1)} %late.1), channel_id=1, source_target_pairs={{0,12},{4,0},{8,4},{12,8},{1,13},{5,1},{9,5},{13,9},{2,14},{6,2},{... | collective-permute-start | bytes 245768 | tf_op jit(solution)/shard_map/ppermute | solution.py:530
  14.5 0.0 collective-permute-done.4.rest_low
  14.5 1.5 %collective-permute-done.5.rest_high = f32[30,8,128]{2,1,0:T(8,128)S(1)} collective-permute-done((f32[30,8,128]{2,1,0:T(8,128)S(1)}, f32[30,8,128]{2,1,0:T(8,128)S(1)}, u32[]{:S(2)}, u32[]{:S(2)}) %collective-permute-start.5) | collective-permute-done | bytes 122912 | tf_op jit(solution)/shard_map/ppermute | solution.py:522
  16.0 0.1 collective-permute-done.3.y
  16.1 1.9 %forward.1 = (f32[20,5,2,8,128]{4,3,2,1,0:T(8,128)S(1)}, f32[20,5,2,8,128]{4,3,2,1,0:T(8,128)S(1)}, f32[20,5,2,8,128]{4,3,2,1,0:T(8,128)S(1)}, f32[20,5,2,8,128]{4,3,2,1,0:T(8,128)S(1)}, f32[8,5,2,8,128]{4,3,2,1,0:T(8,128)S(1)}) custom-call(f32[8,5,2,8,128]{4,3,2,1,0:T(8,128)S(1)} %get-tuple-element.22.t0, f32[5,2,8,128]{3,2,1,0:T(8,128)S(1)} %collective-permute-done.3.y, ...), custom_call_target="tpu_custom_call" | custom-call | flops 1000000000 | bytes 737280 | tf_op jit(solution)/shard_map/forward/pallas_call | solution.py:474
  18.0 1.1 %adjoint.1 = (f32[20,5,2,8,128]{4,3,2,1,0:T(8,128)S(1)}, f32[8,5,2,8,128]{4,3,2,1,0:T(8,128)S(1)}, f32[20,5,2,8,128]{4,3,2,1,0:T(8,128)S(1)}, f32[20,5,2,8,128]{4,3,2,1,0:T(8,128)S(1)}, f32[20,5,2,8,128]{4,3,2,1,0:T(8,128)S(1)}) custom-call(f32[8,5,2,8,128]{4,3,2,1,0:T(8,128)S(1)} %get-tuple-element.23.t1, f32[5,2,8,128]{3,2,1,0:T(8,128)S(1)} %collective-permute-done.3.y, ...), custom_call_target="tpu_custom_call" | custom-call | flops 100000000 | bytes 4177920 | tf_op jit(solution)/shard_map/adjoint/pallas_call | solution.py:474
  19.2 0.1 collective-permute-start.7
  19.2 1.6 %finish.1 = (f32[8,5,2,8,128]{4,3,2,1,0:T(8,128)S(1)}, f32[8,5,2,8,128]{4,3,2,1,0:T(8,128)S(1)}, f32[20,5,2,8,128]{4,3,2,1,0:T(8,128)S(1)}, f32[20,5,2,8,128]{4,...) custom-call(f32[20,5,2,8,128]{4,3,2,1,0:T(8,128)S(1)} %get-tuple-ele, ...), custom_call_target="tpu_custom_call", output_to_operand_aliasing={{2}: (0, {}), {3}: (1, {}), {4}: (2, {}), {5}: (3, {}), {6}... | custom-call | flops 100000000 | bytes 6881280 | tf_op jit(solution)/shard_map/finish/pallas_call | solution.py:474
  20.8 0.0 collective-permute-done.7.got
  20.9 1.0 %merge.1 = (f32[640,128]{1,0:T(8,128)}, f32[640,128]{1,0:T(8,128)}) custom-call(f32[8,5,2,8,128]{4,3,2,1,0:T(8,128)S(1)} %get-tuple-element.37.keep_a, f32[8,5,2,8,128]{4,3,2,1,0:T(8,128)S(1)} %get-tuple-element.38.keep_s, f32[8,5,2,8,128]{4,3,2,1,0:T(8,128)S(1)} %collective-permute-done.7.got), custom_call_target="tpu_custom_call" | custom-call | bytes 983040 | tf_op jit(solution)/shard_map/merge/pallas_call | solution.py:474
  (4 shorter events, 0.0 us)
Async XLA Ops:
  0.6 2.0 %collective-permute-start = (f32[640,128]{1,0:T(8,128)}, f32[640,128]{1,0:T(8,128)S(1)}, u32[]{:S(2)}, u32[]{:S(2)}) collective-permute-start(f32[640,128]{1,0:T(8,128)} %bitcast.3), channel_id=1, source_target_pairs={{0,16},{16,0},{1,17},{17,1},{2,18},{18,2},{3,19},{19,3},{4,20},{20... | collective-permute-start | bytes 983048 | tf_op jit(solution)/shard_map/ppermute | solution.py:509
  1.1 1.0 %copy-start = (f32[1,5,16,8,128]{4,3,2,1,0:T(8,128)S(1)}, f32[1,5,16,8,128]{4,3,2,1,0:T(8,128)}, u32[]{:S(2)}) copy-start(f32[1,5,16,8,128]{4,3,2,1,0:T(8,128)} %param.1) | copy-start | bytes 983044
  2.9 7.8 %collective-permute-start.1 = (f32[25,8,128]{2,1,0:T(8,128)S(1)}, f32[25,8,128]{2,1,0:T(8,128)S(1)}, u32[]{:S(2)}, u32[]{:S(2)}) collective-permute-start(f32[25,8,128]{2,1,0:T(8,128)S(1)} %get-tuple-element.24), channel_id=1, source_target_pairs={{0,4},{4,8},{8,12},{12,0},{1,5},{5,9},{9,13},{13,1},{2,6},{6,10},{... | collective-permute-start | bytes 307208 | tf_op jit(solution)/shard_map/ppermute | solution.py:515
  5.8 4.8 %collective-permute-start.2 = (f32[5,8,128]{2,1,0:T(8,128)S(1)}, f32[5,8,128]{2,1,0:T(8,128)S(1)}, u32[]{:S(2)}, u32[]{:S(2)}) collective-permute-start(f32[5,8,128]{2,1,0:T(8,128)S(1)} %get-tuple-element.25), channel_id=1, source_target_pairs={{0,12},{4,0},{8,4},{12,8},{1,13},{5,1},{9,5},{13,9},{2,14},{6,2},{... | collective-permute-start | bytes 61448 | tf_op jit(solution)/shard_map/ppermute | solution.py:516
  7.0 7.6 %collective-permute-start.4 = (f32[30,8,128]{2,1,0:T(8,128)S(1)}, f32[30,8,128]{2,1,0:T(8,128)S(1)}, u32[]{:S(2)}, u32[]{:S(2)}) collective-permute-start(f32[30,8,128]{2,1,0:T(8,128)S(1)} %get-tuple-element.26), channel_id=1, source_target_pairs={{0,4},{4,8},{8,12},{12,0},{1,5},{5,9},{9,13},{13,1},{2,6},{6,10},{... | collective-permute-start | bytes 368648 | tf_op jit(solution)/shard_map/ppermute | solution.py:521
  8.0 8.0 %collective-permute-start.5 = (f32[30,8,128]{2,1,0:T(8,128)S(1)}, f32[30,8,128]{2,1,0:T(8,128)S(1)}, u32[]{:S(2)}, u32[]{:S(2)}) collective-permute-start(f32[30,8,128]{2,1,0:T(8,128)S(1)} %get-tuple-element.27), channel_id=1, source_target_pairs={{0,12},{4,0},{8,4},{12,8},{1,13},{5,1},{9,5},{13,9},{2,14},{6,2},{... | collective-permute-start | bytes 368648 | tf_op jit(solution)/shard_map/ppermute | solution.py:522
  10.7 5.5 %collective-permute-start.3 = (f32[5,2,8,128]{3,2,1,0:T(8,128)S(1)}, f32[5,2,8,128]{3,2,1,0:T(8,128)S(1)}, u32[]{:S(2)}, u32[]{:S(2)}) collective-permute-start(f32[5,2,8,128]{3,2,1,0:T(8,128)S(1)} %side.1.y), channel_id=1, source_target_pairs={{0,19},{1,16},{2,17},{3,18},{19,0},{16,1},{17,2},{18,3},{4,23},{5,... | collective-permute-start | bytes 122888 | tf_op jit(solution)/shard_map/ppermute | solution.py:529
  13.3 4.7 %collective-permute-start.6 = (f32[20,8,128]{2,1,0:T(8,128)S(1)}, f32[20,8,128]{2,1,0:T(8,128)S(1)}, u32[]{:S(2)}, u32[]{:S(2)}) collective-permute-start(f32[20,8,128]{2,1,0:T(8,128)S(1)} %late.1), channel_id=1, source_target_pairs={{0,12},{4,0},{8,4},{12,8},{1,13},{5,1},{9,5},{13,9},{2,14},{6,2},{... | collective-permute-start | bytes 245768 | tf_op jit(solution)/shard_map/ppermute | solution.py:530
  19.2 1.7 %collective-permute-start.7 = (f32[8,5,2,8,128]{4,3,2,1,0:T(8,128)S(1)}, f32[8,5,2,8,128]{4,3,2,1,0:T(8,128)S(1)}, u32[]{:S(2)}, u32[]{:S(2)}) collective-permute-start(f32[8,5,2,8,128]{4,3,2,1,0:T(8,128)S(1)} %get-tuple-element.39), channel_id=1, source_target_pairs={{0,16},{16,0},{1,17},{17,1},{2,18},{18,2},{3,19},{19,3},{4,20},{20... | collective-permute-start | bytes 983048 | tf_op jit(solution)/shard_map/ppermute | solution.py:539
